TPU v7x, 32 devices: a whole 2x2x4 slice. The times are simulated.
32 devices in a mesh: groups: 2 (over x), dp: 16 (over z, y, core).
Axes of the slice: x: 2, y: 2, z: 4, core: 2. Of those that a mesh axis runs over, the one named last changes fastest.
Arguments:
- activations: bfloat16 [4096, 8192], P(('groups', 'dp')), parts along dimension 0, may hold values from -6 to 6
- upstream: bfloat16 [4096, 1024], P(('groups', 'dp')), parts along dimension 0, may hold values from -6 to 6
- row_job_labels: int32 [4096], P(('groups', 'dp')), parts along dimension 0, may hold values from 0 to 15, as said below
- value_projection_weight: bfloat16 [8192, 1024], P('dp'), may hold values from -0.0625 to 0.0625
- adapter_down_weight: bfloat16 [16, 8192, 64], P('dp'), may hold values from -0.0625 to 0.0625
- adapter_up_weight: bfloat16 [16, 64, 1024], P('dp'), may hold values from -0.75 to 0.75
Outputs:
- projected: bfloat16 [4096, 1024], P(('groups', 'dp')), parts along dimension 0
- entering_derivative: bfloat16 [4096, 8192], P(('groups', 'dp')), parts along dimension 0
- down_grad: float32 [32, 8192, 64], P(('groups', 'dp')), parts along dimension 0
- up_adapter_gradient: float32 [32, 64, 1024], P(('groups', 'dp')), parts along dimension 0
There are 2 independent parts, one for each index of `groups`. A program takes and returns all parts, laid end to end along the dimension named above; an argument that names none is the same for every part. Nothing has to cross between parts.
Inputs may be any that keep to these rules, and one draw needn't show every extreme that they name: `row_job_labels`: in each device's rows the two jobs j and j + 8 together are named at most 2 * 16 times, and on some device exactly so.
All inputs are finite; a program needn't handle non-finite values.
Results may differ from a plain program's by a relative error of at most 0.0055.
Values may be sent and summed in bfloat16 or wider, within the bound.
No kernel may reach another device: no remote copies, remote signals or barrier semaphores. Data moves between devices by JAX's collectives and lax.ppermute only.
A program may use at most 128 MiB of HBM per device.

v0:
```python
import jax
import jax.numpy as jnp
from jax import lax
from jax.sharding import PartitionSpec as P

ADAPTER_SCALE = 2.0


def passed_along(array, axis, by):
    peers = lax.axis_size(axis)
    return lax.ppermute(array, axis, [(i, (i + by) % peers) for i in range(peers)])


def per_device(
    activations,
    upstream,
    row_job_labels,
    value_projection_weight,
    adapter_down_weight,
    adapter_up_weight,
):
    row_count = activations.shape[0]
    width = activations.shape[1]
    out_width = upstream.shape[1]
    devices = lax.axis_size("dp")
    half_axis = devices // 2
    capacity = max(2, 2 * row_count // devices)
    slot_total = devices * capacity
    pair_index = row_job_labels % half_axis
    row_iota = jnp.arange(row_count, dtype=jnp.int32)
    same_pair = pair_index[:, None] == pair_index[None, :]
    earlier = row_iota[:, None] > row_iota[None, :]
    within = jnp.sum((same_pair & earlier).astype(jnp.int32), axis=1)
    target = pair_index + within % 2 * half_axis
    position = target * capacity + within // 2
    own_job = row_job_labels == target
    send_rows = jnp.zeros((slot_total, width), jnp.bfloat16).at[position].set(activations)
    send_grads = jnp.zeros((slot_total, out_width), jnp.bfloat16).at[position].set(upstream)
    send_tags = (
        jnp.zeros((slot_total,), jnp.bfloat16)
        .at[position]
        .set(jnp.where(own_job, 1.0, 2.0).astype(jnp.bfloat16))
    )
    got_rows, got_grads, got_tags = (
        lax.all_to_all(send_rows, "dp", split_axis=0, concat_axis=0, tiled=True),
        lax.all_to_all(send_grads, "dp", split_axis=0, concat_axis=0, tiled=True),
        lax.all_to_all(send_tags, "dp", split_axis=0, concat_axis=0, tiled=True),
    )
    whole_weight = lax.all_gather(value_projection_weight, "dp", axis=0, tiled=True)
    frozen_output = jnp.dot(activations, whole_weight, preferred_element_type=jnp.float32)
    frozen_backward = lax.dot_general(
        upstream, whole_weight, (((1,), (1,)), ((), ())), preferred_element_type=jnp.float32
    )
    own_slot = got_tags == 1.0
    help_slot = got_tags == 2.0
    zero_value = jnp.zeros((), jnp.bfloat16)
    owned_down_adapter = adapter_down_weight[0]
    owned_up_adapter = adapter_up_weight[0]
    own_rows = jnp.where(own_slot[:, None], got_rows, zero_value)
    own_grads = jnp.where(own_slot[:, None], got_grads, zero_value)
    help_rows_out = jnp.where(help_slot[:, None], got_rows, zero_value)
    help_grads_out = jnp.where(help_slot[:, None], got_grads, zero_value)
    moved_rows, moved_grads = passed_along((help_rows_out, help_grads_out), "dp", half_axis)
    all_rows = jnp.concatenate([own_rows, moved_rows], axis=0)
    all_grads = jnp.concatenate([own_grads, moved_grads], axis=0)
    summed_result = jnp.dot(
        all_rows, owned_down_adapter, preferred_element_type=jnp.float32
    ).astype(jnp.bfloat16)
    output_term = (
        ADAPTER_SCALE * jnp.dot(summed_result, owned_up_adapter, preferred_element_type=jnp.float32)
    ).astype(jnp.bfloat16)
    scaled_output = (
        ADAPTER_SCALE
        * lax.dot_general(
            all_grads,
            owned_up_adapter,
            (((1,), (1,)), ((), ())),
            preferred_element_type=jnp.float32,
        )
    ).astype(jnp.bfloat16)
    term_back = lax.dot_general(
        scaled_output,
        owned_down_adapter,
        (((1,), (1,)), ((), ())),
        preferred_element_type=jnp.float32,
    ).astype(jnp.bfloat16)
    down_grad = lax.dot_general(
        all_rows, scaled_output, (((0,), (0,)), ((), ())), preferred_element_type=jnp.float32
    )
    up_adapter_gradient = ADAPTER_SCALE * lax.dot_general(
        summed_result, all_grads, (((0,), (0,)), ((), ())), preferred_element_type=jnp.float32
    )
    other_out, other_back = passed_along(
        (output_term[slot_total:], term_back[slot_total:]), "dp", half_axis
    )
    slot_out = jnp.where(help_slot[:, None], other_out, output_term[:slot_total])
    slot_back = jnp.where(help_slot[:, None], other_back, term_back[:slot_total])
    home_out, home_back = (
        lax.all_to_all(slot_out, "dp", split_axis=0, concat_axis=0, tiled=True),
        lax.all_to_all(slot_back, "dp", split_axis=0, concat_axis=0, tiled=True),
    )
    projected = (frozen_output + home_out[position].astype(jnp.float32)).astype(jnp.bfloat16)
    entering_derivative = (frozen_backward + home_back[position].astype(jnp.float32)).astype(
        jnp.bfloat16
    )
    return (projected, entering_derivative, down_grad[None], up_adapter_gradient[None])


def solution(mesh):
    return jax.shard_map(
        per_device,
        mesh=mesh,
        in_specs=(
            P(("groups", "dp"), None),
            P(("groups", "dp"), None),
            P(("groups", "dp")),
            P("dp", None),
            P("dp", None, None),
            P("dp", None, None),
        ),
        out_specs=(
            P(("groups", "dp"), None),
            P(("groups", "dp"), None),
            P(("groups", "dp"), None, None),
            P(("groups", "dp"), None, None),
        ),
        check_vma=False,
    )
```

profile of v0, /device:TPU:0, one launch (start us, length us, event | category | flops | bytes accessed | tf_op | source)
XLA Modules:
  0.0 780.3 jit_solution(10855712426864647327)
XLA Ops:
  7.2 0.0 copy-start
  7.2 0.0 all-gather.2.cloned.1.call-start
  7.2 0.7 all-gather.2.cloned.1.call-update
  7.9 0.7 and_select_fusion.2
  8.6 0.2 convert_reduce_fusion
  8.8 0.7 fusion.17
  9.5 1.3 scatter_custom_fusion
  10.8 0.7 all_to_all.52
  11.5 7.4 all-to-all-start
  18.9 7.3 scatter_custom_fusion.1
  26.1 0.0 all-to-all-done
  26.1 6.1 all-to-all-start.1
  32.2 0.1 compare_reduce_fusion
  32.3 0.1 eq.51
  32.4 0.1 eq.54
  32.5 126.8 %all-to-all-done.1 = bf16[16,16,8192]{2,1,0:T(8,128)(2,1)} async-done(((bf16[16,16,8192]{2,1,0:T(8,128)(2,1)}), bf16[16,16,8192]{2,1,0:T(8,128)(2,1)}, u32[]{:S(2)}, u32[]{:S(2)}) %all-to-all-start.1) | async-done | bytes 4194336 | tf_op jit(solution)/shard_map/all_to_all | solution.py:45
  159.3 5.2 bitcast_select_fusion.1
  164.5 50.5 %collective-permute-start = (bf16[256,8192]{1,0:T(8,128)(2,1)}, bf16[256,8192]{1,0:T(8,128)(2,1)}, u32[]{:S(2)}, u32[]{:S(2)}) collective-permute-start(bf16[256,8192]{1,0:T(8,128)(2,1)} %get-tuple-element.9), channel_id=1, source_target_pairs={{0,8},{1,9},{2,10},{3,11},{4,12},{5,13},{6,14},{7,15},{8,0},{9,1},... | collective-permute-start | bytes 12582920 | tf_op jit(solution)/shard_map/ppermute | solution.py:11
  215.1 2.4 scatter_custom_fusion.2
  217.4 5.3 all-to-all-start.3
  222.8 179.7 %collective-permute-done = bf16[256,8192]{1,0:T(8,128)(2,1)} collective-permute-done((bf16[256,8192]{1,0:T(8,128)(2,1)}, bf16[256,8192]{1,0:T(8,128)(2,1)}, u32[]{:S(2)}, u32[]{:S(2)}) %collective-permute-start) | collective-permute-done | bytes 4194336 | tf_op jit(solution)/shard_map/ppermute | solution.py:11
  402.5 0.0 copy-done
  402.5 0.0 copy-start.4
  402.5 5.1 fusion.7
  407.6 0.0 copy-done.4
  407.6 0.5 multiply_convert_fusion
  408.1 0.1 collective-permute-start.1
  408.2 0.0 all-to-all-done.3
  408.2 24.1 %collective-permute-done.1 = bf16[256,1024]{1,0:T(8,128)(2,1)} collective-permute-done((bf16[256,1024]{1,0:T(8,128)(2,1)S(1)}, bf16[256,1024]{1,0:T(8,128)(2,1)}, u32[]{:S(2)}, u32[]{:S(2)}) %collective-permute-start.1) | collective-permute-done | bytes 524320 | tf_op jit(solution)/shard_map/ppermute | solution.py:11
  432.3 2.1 bitcast_select_fusion.3
  434.4 0.0 collective-permute-start.2
  434.4 25.3 %collective-permute-done.2 = bf16[256,1024]{1,0:T(8,128)(2,1)S(1)} collective-permute-done((bf16[256,1024]{1,0:T(8,128)(2,1)S(1)}, bf16[256,1024]{1,0:T(8,128)(2,1)S(1)}, u32[]{:S(2)}, u32[]{:S(2)}) %collective-permute-start.2) | collective-permute-done | bytes 524320 | tf_op jit(solution)/shard_map/ppermute | solution.py:11
  459.7 0.4 fusion.6
  460.1 2.4 convolution_convert_fusion
  462.5 0.0 copy-start.2
  462.5 2.8 slice.22
  465.2 1.9 copy-done.2
  467.1 0.0 collective-permute-start.3
  467.1 6.3 all-to-all-start.2
  473.4 182.2 %collective-permute-done.3 = bf16[256,8192]{1,0:T(8,128)(2,1)} collective-permute-done((bf16[256,8192]{1,0:T(8,128)(2,1)}, bf16[256,8192]{1,0:T(8,128)(2,1)}, u32[]{:S(2)}, u32[]{:S(2)}) %collective-permute-start.3) | collective-permute-done | bytes 4194336 | tf_op jit(solution)/shard_map/ppermute | solution.py:11
  655.6 6.0 slice_select_fusion
  661.6 0.0 all-to-all-done.2
  661.6 5.4 all-to-all-start.4
  667.0 1.0 fusion.5
  668.0 6.4 convolution_bitcast_fusion
  674.4 0.9 gather_fusion
  675.3 69.4 %all-to-all-done.4 = bf16[16,16,8192]{2,1,0:T(8,128)(2,1)} async-done(((bf16[16,16,8192]{2,1,0:T(8,128)(2,1)}), bf16[16,16,8192]{2,1,0:T(8,128)(2,1)}, u32[]{:S(2)}, u32[]{:S(2)}) %all-to-all-start.4) | async-done | bytes 4194336 | tf_op jit(solution)/shard_map/all_to_all | solution.py:100
  744.7 0.0 copy-start.3
  744.7 6.5 gather_fusion.1
  751.2 0.0 all-gather.2.cloned.1.call-done
  751.3 0.0 copy-done.3
  751.3 12.7 %fusion = bf16[128,8192]{1,0:T(8,128)(2,1)} fusion(bf16[128,1024]{1,0:T(8,128)(2,1)S(1)} %copy-done.3, bf16[8192,1024]{1,0:T(8,128)(2,1)} %all-gather.2.cloned.1.call-done, bf16[128,8192]{1,0:T(8,128)(2,1)S(1)} %gather_fusion.1), kind=kOutput, calls=%fused_computation.7 | convolution fusion | flops 2150629376 | bytes 21233664 | tf_op jit(solution)/shard_map/dot_general | solution.py:51
  764.0 0.0 copy-start.1
  764.0 9.5 %fusion.4 = bf16[128,1024]{1,0:T(8,128)(2,1)} fusion(bf16[128,8192]{1,0:T(8,128)(2,1)} %param.6, bf16[8192,1024]{1,0:T(8,128)(2,1)} %all-gather.2.cloned.1.call-done, bf16[128,1024]{1,0:T(8,128)(2,1)S(1)} %gather_fusion), kind=kOutput, calls=%fused_computation.18 | convolution fusion | flops 2147876864 | bytes 19398656 | tf_op jit(solution)/shard_map/dot_general | solution.py:50
  773.5 0.0 copy-done.1
  (3 shorter events, 0.1 us)
Async XLA Ops:
  7.2 395.3 %copy-start = (bf16[1,8192,64]{1,2,0:T(8,128)(2,1)S(1)}, bf16[1,8192,64]{1,2,0:T(8,128)(2,1)}, u32[]{:S(2)}) copy-start(bf16[1,8192,64]{1,2,0:T(8,128)(2,1)} %param.10) | copy-start | bytes 3145732
  7.2 744.1 %all-gather.2.cloned.1.call-start = ((), (), s32[]{:S(2)}) async-start(), calls=%async_computation.5 | async-start | bytes 17825792 | tf_op jit(solution)/shard_map/all_gather | solution.py:49
  11.5 14.6 %all-to-all-start = ((bf16[16,16,1]{1,2,0:T(2,128)(2,1)}), bf16[16,16,1]{1,2,0:T(2,128)(2,1)S(1)}, u32[]{:S(2)}, u32[]{:S(2)}) async-start(bf16[16,16,1]{1,2,0:T(2,128)(2,1)} %all_to_all.52), calls=%async_computation | async-start | bytes 16384 | tf_op jit(solution)/shard_map/all_to_all | solution.py:47
  26.1 133.1 %all-to-all-start.1 = ((bf16[16,16,8192]{2,1,0:T(8,128)(2,1)}), bf16[16,16,8192]{2,1,0:T(8,128)(2,1)}, u32[]{:S(2)}, u32[]{:S(2)}) async-start(bf16[16,16,8192]{2,1,0:T(8,128)(2,1)} %bitcast.35), calls=%async_computation.1 | async-start | bytes 8388608 | tf_op jit(solution)/shard_map/all_to_all | solution.py:45
  164.5 238.0 %collective-permute-start = (bf16[256,8192]{1,0:T(8,128)(2,1)}, bf16[256,8192]{1,0:T(8,128)(2,1)}, u32[]{:S(2)}, u32[]{:S(2)}) collective-permute-start(bf16[256,8192]{1,0:T(8,128)(2,1)} %get-tuple-element.9), channel_id=1, source_target_pairs={{0,8},{1,9},{2,10},{3,11},{4,12},{5,13},{6,14},{7,15},{8,0},{9,1},... | collective-permute-start | bytes 12582920 | tf_op jit(solution)/shard_map/ppermute | solution.py:11
  217.4 190.8 %all-to-all-start.3 = ((bf16[16,16,1024]{2,1,0:T(8,128)(2,1)}), bf16[16,16,1024]{2,1,0:T(8,128)(2,1)S(1)}, u32[]{:S(2)}, u32[]{:S(2)}) async-start(bf16[16,16,1024]{2,1,0:T(8,128)(2,1)} %bitcast.6), calls=%async_computation.3 | async-start | bytes 1048576 | tf_op jit(solution)/shard_map/all_to_all | solution.py:46
  402.5 5.1 copy-start.4
  408.1 24.2 %collective-permute-start.1 = (bf16[256,1024]{1,0:T(8,128)(2,1)S(1)}, bf16[256,1024]{1,0:T(8,128)(2,1)}, u32[]{:S(2)}, u32[]{:S(2)}) collective-permute-start(bf16[256,1024]{1,0:T(8,128)(2,1)S(1)} %slice.20), channel_id=1, source_target_pairs={{0,8},{1,9},{2,10},{3,11},{4,12},{5,13},{6,14},{7,15},{8,0},{9,1},... | collective-permute-start | bytes 1572872 | tf_op jit(solution)/shard_map/ppermute | solution.py:11
  434.4 25.3 %collective-permute-start.2 = (bf16[256,1024]{1,0:T(8,128)(2,1)S(1)}, bf16[256,1024]{1,0:T(8,128)(2,1)S(1)}, u32[]{:S(2)}, u32[]{:S(2)}) collective-permute-start(bf16[256,1024]{1,0:T(8,128)(2,1)S(1)} %get-tuple-element.11), channel_id=1, source_target_pairs={{0,8},{1,9},{2,10},{3,11},{4,12},{5,13},{6,14},{7,15},{8,0},{9,1},... | collective-permute-start | bytes 1572872 | tf_op jit(solution)/shard_map/ppermute | solution.py:11
  462.5 4.6 copy-start.2
  467.1 188.5 %collective-permute-start.3 = (bf16[256,8192]{1,0:T(8,128)(2,1)}, bf16[256,8192]{1,0:T(8,128)(2,1)}, u32[]{:S(2)}, u32[]{:S(2)}) collective-permute-start(bf16[256,8192]{1,0:T(8,128)(2,1)} %slice.22), channel_id=1, source_target_pairs={{0,8},{1,9},{2,10},{3,11},{4,12},{5,13},{6,14},{7,15},{8,0},{9,1},... | collective-permute-start | bytes 12582920 | tf_op jit(solution)/shard_map/ppermute | solution.py:11
  467.1 194.5 %all-to-all-start.2 = ((bf16[16,16,1024]{2,1,0:T(8,128)(2,1)}), bf16[16,16,1024]{2,1,0:T(8,128)(2,1)S(1)}, u32[]{:S(2)}, u32[]{:S(2)}) async-start(bf16[16,16,1024]{2,1,0:T(8,128)(2,1)} %bitcast.4), calls=%async_computation.2 | async-start | bytes 1048576 | tf_op jit(solution)/shard_map/all_to_all | solution.py:99
  661.6 83.0 %all-to-all-start.4 = ((bf16[16,16,8192]{2,1,0:T(8,128)(2,1)}), bf16[16,16,8192]{2,1,0:T(8,128)(2,1)}, u32[]{:S(2)}, u32[]{:S(2)}) async-start(bf16[16,16,8192]{2,1,0:T(8,128)(2,1)} %bitcast.34), calls=%async_computation.4 | async-start | bytes 8388608 | tf_op jit(solution)/shard_map/all_to_all | solution.py:100
  744.7 6.6 copy-start.3
  764.0 9.5 %copy-start.1 = (bf16[1,8192,64]{1,2,0:T(8,128)(2,1)S(1)}, bf16[1,8192,64]{1,2,0:T(8,128)(2,1)}, u32[]{:S(2)}) copy-start(bf16[1,8192,64]{1,2,0:T(8,128)(2,1)} %param.10) | copy-start | bytes 3145732
Sparse Core Ops, SparseCore 0:
  10.2 309.6 all-gather.1
where the time goes:
time: 795 us; the launch traced here: 780 us
  waiting for transfers between devices  608 us (76%)
  starting transfers between devices  81.1 us (10%)
  matrix products  37.9 us (5%)
  local copies, waits for them, and re-layouts  23.9 us (3%)
  other arithmetic  14.9 us (2%)
  between operations  14.2 us (2%)
    ppermute x4, waiting for transfers between devices, passed_along(): lax.ppermute(array, axis, [(i, (i + by) % peers) for i in range(peers)])  411 us
    all_to_all x1, waiting for transfers between devices, per_device(): lax.all_to_all(send_rows, 'dp', split_axis=0, concat_axis=0, tiled=True)  127 us
    all_to_all x1, waiting for transfers between devices, per_device(): lax.all_to_all(slot_back, 'dp', split_axis=0, concat_axis=0, tiled=True)  69.4 us
    ppermute x4, starting transfers between devices, passed_along(): lax.ppermute(array, axis, [(i, (i + by) % peers) for i in range(peers)])  50.6 us
  transfers between devices with their start and end apart: 10, of which 6 were waited for; matrix products, arithmetic and copies ran while one was open for 7% of the time, Pallas kernels for 0%

commit v1 on v0

v1 whole, which is shorter than its diff:
```python
import functools

import jax
import jax.numpy as jnp
from jax import lax
from jax.sharding import Mesh
from jax.sharding import PartitionSpec as P

ADAPTER_SCALE = 2.0
PLANE = ("groups", "q")
F32 = jnp.float32
BF16 = jnp.bfloat16


def swapped(array, axis, bit):
    peers = lax.axis_size(axis)
    return lax.ppermute(array, axis, [(i, i ^ bit) for i in range(peers)])


def shifted(array, axis, by):
    peers = lax.axis_size(axis)
    return lax.ppermute(array, axis, [(i, (i + by) % peers) for i in range(peers)])


def cube_gather(array, axes):
    stack = array[None]
    for axis in axes:
        bit = lax.axis_size(axis) // 2
        while bit:
            mine = (lax.axis_index(axis) & bit) > 0
            other = swapped(stack, axis, bit)
            pair = jnp.stack(
                [jnp.where(mine, other, stack), jnp.where(mine, stack, other)], axis=1
            )
            stack = pair.reshape((-1,) + array.shape)
            bit //= 2
    return stack


def straight_gather(array, axis):
    peers = lax.axis_size(axis)
    me = lax.axis_index(axis)
    stack = jnp.zeros((peers,) + array.shape, array.dtype)
    stack = lax.dynamic_update_index_in_dim(stack, array, me, 0)
    for by in range(1, peers):
        got = shifted(array, axis, by)
        stack = lax.dynamic_update_index_in_dim(stack, got, (me - by) % peers, 0)
    return stack


def line_gather(array, axis):
    peers = lax.axis_size(axis)
    me = lax.axis_index(axis)
    upward = [(i, i + 1) for i in range(peers - 1)]
    downward = [(i + 1, i) for i in range(peers - 1)]
    rising, falling = [array], [array]
    for _ in range(peers - 1):
        rising.append(lax.ppermute(rising[-1], axis, upward))
        falling.append(lax.ppermute(falling[-1], axis, downward))
    stack = jnp.zeros((peers,) + array.shape, array.dtype)
    stack = lax.dynamic_update_index_in_dim(stack, array, me, 0)
    for by in range(1, peers):
        block = jnp.where(me >= by, rising[by], falling[peers - by])
        stack = lax.dynamic_update_index_in_dim(stack, block, (me - by) % peers, 0)
    return stack


def exchanged(array, axes):
    return lax.all_to_all(array, axes, split_axis=0, concat_axis=0, tiled=True)


def dot(left, right, left_dim, right_dim):
    return lax.dot_general(
        left, right, (((left_dim,), (right_dim,)), ((), ())), preferred_element_type=F32
    )


def per_device(
    activations,
    upstream,
    row_job_labels,
    value_projection_weight,
    adapter_down_weight,
    adapter_up_weight,
):
    rows, width = activations.shape
    out_width = upstream.shape[1]
    rank = adapter_down_weight.shape[2]
    groups, outer, inner = (lax.axis_size(a) for a in ("groups", "z", "q"))
    group, level, place = (lax.axis_index(a) for a in ("groups", "z", "q"))
    plane = groups * inner
    jobs = outer * inner
    piece = width // (jobs * groups)
    flat = outer * piece
    plane_rows = plane * rows

    def spread(values, labels, first, count):
        wanted = first + jnp.arange(count, dtype=jnp.int32)
        hit = labels[None, None, :] == wanted[:, None, None]
        wide = jnp.where(hit, values[None], jnp.zeros((), values.dtype))
        return wide.reshape(count * rank, -1)

    def gathered_in(wide, labels, order):
        hit = labels[None, None, :] == order[:, None, None]
        return jnp.sum(jnp.where(hit, wide.reshape(order.shape[0], rank, -1), 0.0), axis=0)

    up_line = straight_gather(adapter_up_weight[0], "z")
    up_all = cube_gather(up_line.reshape(outer * rank, out_width), ("q",))
    up_all = up_all.reshape(jobs * rank, out_width)
    up_order = (
        jnp.arange(outer, dtype=jnp.int32)[None, :] * inner
        + jnp.arange(inner, dtype=jnp.int32)[:, None]
    ).reshape(-1)

    act_send = activations.reshape(rows, outer, inner, groups, piece)
    act_send = act_send.transpose(3, 2, 0, 1, 4).reshape(plane_rows, flat)
    act_plane = exchanged(act_send, PLANE)
    act_deep = act_plane.reshape(plane_rows, outer, piece).transpose(1, 0, 2)
    act_deep = exchanged(act_deep.reshape(outer * plane_rows, piece), "z")

    part = value_projection_weight.shape[0] // groups
    weight_half = lax.dynamic_slice_in_dim(value_projection_weight, group * part, part, 0)
    weight = line_gather(weight_half, "z").reshape(flat, out_width)
    down_send = adapter_down_weight[0].T.reshape(rank, outer, inner, groups, piece)
    down_send = lax.dynamic_index_in_dim(down_send, group, 3, keepdims=False)
    down_send = down_send.transpose(2, 0, 1, 3).reshape(inner * rank, flat)
    down_block = exchanged(down_send, "q")
    down = line_gather(down_block, "z")

    labels_plane = cube_gather(row_job_labels, PLANE)
    labels_deep = straight_gather(labels_plane, "z")
    labels_plane = labels_plane.reshape(-1)
    upstream_plane = cube_gather(upstream, PLANE)

    wide = ADAPTER_SCALE * dot(up_all, upstream, 1, 1)
    scaled = gathered_in(wide, row_job_labels, up_order).astype(BF16)
    scaled_plane = cube_gather(scaled, PLANE)
    scaled_deep = straight_gather(scaled_plane, "z")
    scaled_plane = scaled_plane.transpose(1, 0, 2).reshape(rank, plane_rows)

    act_deep = act_deep.reshape(outer, groups, inner * rows, piece)
    scaled_deep = scaled_deep.reshape(outer, groups, inner, rank, rows)
    scaled_deep = scaled_deep.transpose(1, 3, 0, 2, 4).reshape(groups, rank, -1)
    labels_deep = labels_deep.reshape(outer, groups, inner * rows)
    small = jobs * rank * outer * inner * rows <= 1 << 22

    def down_grad_part(g, first, count):
        columns = act_deep[:, g].reshape(-1, piece)
        wide = spread(scaled_deep[g], labels_deep[:, g].reshape(-1), first, count)
        return dot(wide, columns, 1, 0).astype(BF16)

    if small:
        down_parts = [down_grad_part(g, 0, jobs) for g in range(groups)]
    else:
        down_parts = [
            lax.map(
                functools.partial(lambda g, b: down_grad_part(g, b * inner, inner), g),
                jnp.arange(outer, dtype=jnp.int32),
            ).reshape(jobs * rank, piece)
            for g in range(groups)
        ]
    down_parts = exchanged(jnp.concatenate(down_parts, axis=0), ("groups", "z", "q"))
    down_parts = down_parts.reshape(groups, outer, inner, rank, piece)
    down_grad = down_parts.transpose(3, 1, 2, 0, 4).reshape(rank, width).astype(F32).T

    frozen = dot(act_plane, weight, 1, 0).astype(BF16)
    frozen = exchanged(frozen, PLANE).reshape(plane, rows, out_width)
    frozen = jnp.sum(frozen.astype(F32), axis=0)

    back = dot(upstream_plane.reshape(plane_rows, out_width), weight, 1, 1)
    if small:
        down_all = down.reshape(jobs * rank, flat)
        back = back + dot(spread(scaled_plane, labels_plane, 0, jobs), down_all, 0, 0)
        reduced = gathered_in(
            dot(down_all, act_plane, 1, 1), labels_plane, jnp.arange(jobs, dtype=jnp.int32)
        )
    else:

        def step(carry, operands):
            back, reduced = carry
            block, first = operands
            wide = spread(scaled_plane, labels_plane, first, inner)
            order = first + jnp.arange(inner, dtype=jnp.int32)
            back = back + dot(wide, block, 0, 0)
            reduced = reduced + gathered_in(dot(block, act_plane, 1, 1), labels_plane, order)
            return (back, reduced), None

        firsts = jnp.arange(outer, dtype=jnp.int32) * inner
        start = (back, jnp.zeros((rank, plane_rows), F32))
        (back, reduced), _ = lax.scan(step, start, (down, firsts))
    back = exchanged(back.astype(BF16), PLANE)
    entering_derivative = back.reshape(groups, inner, rows, outer, piece)
    entering_derivative = entering_derivative.transpose(2, 3, 1, 0, 4).reshape(rows, width)

    reduced = reduced.reshape(rank, groups, inner * rows)
    total = lax.dynamic_index_in_dim(reduced, group, 1, keepdims=False)
    for by in range(1, groups):
        leaving = lax.dynamic_index_in_dim(reduced, (group + by) % groups, 1, keepdims=False)
        total = total + shifted(leaving, "groups", by)
    bit = inner // 2
    while bit:
        total = total + swapped(total, "q", bit)
        bit //= 2
    reduced = total.astype(BF16)
    reduced_own = lax.dynamic_slice_in_dim(reduced, place * rows, rows, 1)

    hit = row_job_labels[None, None, :] == up_order[:, None, None]
    wide = jnp.where(hit, reduced_own[None], jnp.zeros((), BF16)).reshape(jobs * rank, rows)
    projected = (frozen + ADAPTER_SCALE * dot(wide, up_all, 0, 0)).astype(BF16)

    upstream_group = lax.dynamic_index_in_dim(
        upstream_plane.reshape(groups, inner * rows, out_width), group, 0, keepdims=False
    )
    labels_group = lax.dynamic_index_in_dim(
        labels_plane.reshape(groups, inner * rows), group, 0, keepdims=False
    )
    wanted = jnp.arange(outer, dtype=jnp.int32) * inner + place
    hit = labels_group[None, None, :] == wanted[:, None, None]
    wide = jnp.where(hit, reduced[None], jnp.zeros((), BF16)).reshape(outer * rank, -1)
    up_part = (ADAPTER_SCALE * dot(wide, upstream_group, 1, 0)).reshape(outer, rank, out_width)
    up_grad = lax.dynamic_index_in_dim(up_part, level, 0, keepdims=False)
    up_send = up_part.astype(BF16)
    for by in range(1, outer):
        leaving = lax.dynamic_index_in_dim(up_send, (level + by) % outer, 0, keepdims=False)
        up_grad = up_grad + shifted(leaving, "z", by).astype(F32)
    return (projected, entering_derivative, down_grad[None], up_grad[None])


def solution(mesh):
    groups, devices = mesh.devices.shape
    inner = 1
    while inner * inner < devices:
        inner *= 2
    fine = Mesh(
        mesh.devices.reshape(groups, devices // inner, inner), ("groups", "z", "q")
    )
    every = ("groups", "z", "q")
    owner = ("z", "q")
    return jax.shard_map(
        per_device,
        mesh=fine,
        in_specs=(
            P(every, None),
            P(every, None),
            P(every),
            P(owner, None),
            P(owner, None, None),
            P(owner, None, None),
        ),
        out_specs=(
            P(every, None),
            P(every, None),
            P(every, None, None),
            P(every, None, None),
        ),
        check_vma=False,
    )
```

time: 795 us -> 325 us (0.41); the launches traced: 780 us -> 323 us
  waiting for transfers between devices: 608 us -> 117 us
  local copies, waits for them, and re-layouts: 23.9 us -> 63.3 us
  between operations: 14.2 us -> 1.63 us
  matrix products: 37.9 us -> 26 us
  starting transfers between devices: 81.1 us -> 92.4 us
  other arithmetic: 14.9 us -> 23.2 us
    ppermute x4 -> x38, waiting for transfers between devices: 411 us -> 83 us  [the longest x13 44.4 us: shifted(): lax.ppermute(array, axis, [(i, (i + by) % peers) for i in range(peers)])]
    all_to_all x5 -> x6, waiting for transfers between devices: 196 us -> 33.8 us  [exchanged(): return lax.all_to_all(array, axes, split_axis=0, concat_axis=0, tiled=True)]
    reshape x0 -> x9, local copies, waits for them, and re-layouts: none -> 25 us  [the longest x2 7.88 us: per_device(): entering_derivative = back.reshape(groups, inner, rows, outer, piece)]
    ppermute x4 -> x38, starting transfers between devices: 50.6 us -> 68.5 us  [the longest x6 32.6 us: line_gather(): rising.append(lax.ppermute(rising[-1], axis, upward))]
    all_to_all x1 -> x4, local copies, waits for them, and re-layouts: 0.69 us -> 13 us  [exchanged(): return lax.all_to_all(array, axes, split_axis=0, concat_axis=0, tiled=True)]
    dot_general x8 -> x9, matrix products: 37.9 us -> 26 us  [dot(): lax.dot_general(left, right, (((left_dim,), (right_dim,)), ((), ())), pre...]
    scatter x3 -> x0, local copies, waits for them, and re-layouts: 11 us -> none  [the longest x1 7.25 us: per_device(): jnp.zeros((slot_total, width), jnp.bfloat16).at[position].set(activations)]
    dynamic_update_slice x0 -> x6, other arithmetic: none -> 9.25 us  [line_gather(): stack = lax.dynamic_update_index_in_dim(stack, block, (me - by) % peers, 0)]
  transfers between devices with their start and end apart: 10 -> 44, of which waited for: 6 -> 15; matrix products, arithmetic and copies ran while one was open for 7% -> 32% of each run, Pallas kernels for 0% -> 0%
where the time goes in v1:
time: 325 us; the launch traced here: 323 us
  waiting for transfers between devices  117 us (36%)
  starting transfers between devices  92.4 us (28%)
  local copies, waits for them, and re-layouts  63.3 us (19%)
  matrix products  26 us (8%)
  other arithmetic  23.2 us (7%)
    ppermute x13, waiting for transfers between devices, shifted(): lax.ppermute(array, axis, [(i, (i + by) % peers) for i in range(peers)])  44.4 us
    ppermute x13, waiting for transfers between devices, swapped(): return lax.ppermute(array, axis, [(i, i ^ bit) for i in range(peers)])  36.4 us
    all_to_all x6, waiting for transfers between devices, exchanged(): return lax.all_to_all(array, axes, split_axis=0, concat_axis=0, tiled=True)  33.8 us
    ppermute x6, starting transfers between devices, line_gather(): rising.append(lax.ppermute(rising[-1], axis, upward))  32.6 us
    dot_general x9, matrix products, dot(): lax.dot_general(left, right, (((left_dim,), (right_dim,)), ((), ())), pre...  26 us
    all_to_all x6, starting transfers between devices, exchanged(): return lax.all_to_all(array, axes, split_axis=0, concat_axis=0, tiled=True)  23.9 us
    ppermute x13, starting transfers between devices, shifted(): lax.ppermute(array, axis, [(i, (i + by) % peers) for i in range(peers)])  19.5 us
    all_to_all x4, local copies, waits for them, and re-layouts, exchanged(): return lax.all_to_all(array, axes, split_axis=0, concat_axis=0, tiled=True)  13 us
  transfers between devices with their start and end apart: 44, of which 15 were waited for; matrix products, arithmetic and copies ran while one was open for 32% of the time, Pallas kernels for 0%

profile of v1, /device:TPU:0, one launch (start us, length us, event | category | flops | bytes accessed | tf_op | source)
XLA Modules:
  0.0 323.3 jit_solution(14952868334341225600)
XLA Ops:
  0.7 1.6 broadcast.184.clone
  3.4 5.7 %collective-permute-start = (bf16[256,1024]{1,0:T(8,128)(2,1)}, bf16[256,1024]{1,0:T(8,128)(2,1)}, u32[]{:S(2)}, u32[]{:S(2)}) collective-permute-start(bf16[256,1024]{1,0:T(8,128)(2,1)} %get-tuple-element.5), channel_id=1, source_target_pairs={{0,4},{4,8},{8,12},{1,5},{5,9},{9,13},{2,6},{6,10},{10,14},{3,7},{... | collective-permute-start | bytes 1572872 | tf_op jit(solution)/shard_map/ppermute | solution.py:58
  10.4 2.7 collective-permute-start.18
  13.1 2.5 collective-permute-start.19
  15.6 1.5 collective-permute-start.6
  20.6 3.5 %all-to-all-start.2 = ((bf16[4,64,1024]{2,1,0:T(8,128)(2,1)}), bf16[4,64,1024]{2,1,0:T(8,128)(2,1)S(1)}, u32[]{:S(2)}, u32[]{:S(2)}) async-start(bf16[4,64,1024]{2,1,0:T(8,128)(2,1)} %bitcast.119), calls=%async_computation.2 | async-start | bytes 1048576 | tf_op jit(solution)/shard_map/all_to_all | solution.py:69
  25.6 2.0 collective-permute-start.7
  27.5 5.4 %collective-permute-done.7 = s32[2,128]{1,0:T(2,128)S(1)} collective-permute-done((s32[2,128]{1,0:T(2,128)S(1)}, s32[2,128]{1,0:T(2,128)S(1)}, u32[]{:S(2)}, u32[]{:S(2)}) %collective-permute-start.7) | collective-permute-done | bytes 1056 | tf_op jit(solution)/shard_map/ppermute | solution.py:17
  33.1 3.3 %reshape.349 = bf16[128,4,4,2,256]{4,3,2,1,0:T(2,128)(2,1)S(1)} reshape(bf16[128,8192]{1,0:T(8,128)(2,1)} %param.6) | data formatting | bytes 4194304 | tf_op jit(solution)/shard_map/reshape | solution.py:115
  36.4 4.2 %copy.69 = bf16[128,4,4,2,256]{0,4,1,2,3:T(8,128)(2,1)} copy(bf16[128,4,4,2,256]{4,3,2,1,0:T(2,128)(2,1)S(1)} %reshape.349) | data formatting | bytes 4194304 | tf_op jit(solution)/shard_map/reshape | solution.py:115
  41.3 4.8 %collective-permute-done.29 = s32[8,128]{1,0:T(8,128)S(1)} collective-permute-done((s32[8,128]{1,0:T(8,128)S(1)}, s32[8,128]{1,0:T(8,128)S(1)}, u32[]{:S(2)}, u32[]{:S(2)}) %collective-permute-start.29) | collective-permute-done | bytes 4128 | tf_op jit(solution)/shard_map/ppermute | solution.py:22
  46.1 4.5 %collective-permute-done.30 = s32[8,128]{1,0:T(8,128)S(1)} collective-permute-done((s32[8,128]{1,0:T(8,128)S(1)}, s32[8,128]{1,0:T(8,128)S(1)}, u32[]{:S(2)}, u32[]{:S(2)}) %collective-permute-start.30) | collective-permute-done | bytes 4128 | tf_op jit(solution)/shard_map/ppermute | solution.py:22
  50.6 3.6 %collective-permute-done.31 = s32[8,128]{1,0:T(8,128)S(1)} collective-permute-done((s32[8,128]{1,0:T(8,128)S(1)}, s32[8,128]{1,0:T(8,128)S(1)}, u32[]{:S(2)}, u32[]{:S(2)}) %collective-permute-start.31) | collective-permute-done | bytes 4128 | tf_op jit(solution)/shard_map/ppermute | solution.py:22
  54.2 1.8 collective-permute-start.20
  59.7 2.8 collective-permute-done.23
  63.0 4.4 %all-to-all-start = ((bf16[8,128,1024]{1,2,0:T(8,128)(2,1)}), bf16[8,128,1024]{1,2,0:T(8,128)(2,1)}, u32[]{:S(2)}, u32[]{:S(2)}) async-start(bf16[8,128,1024]{1,2,0:T(8,128)(2,1)} %bitcast.6), calls=%async_computation | async-start | bytes 4194304 | tf_op jit(solution)/shard_map/all_to_all | solution.py:69
  67.4 2.2 collective-permute-start.9
  69.6 6.8 %collective-permute-done.21 = bf16[1,256,1024]{2,1,0:T(8,128)(2,1)S(1)} collective-permute-done((bf16[1,256,1024]{2,1,0:T(8,128)(2,1)S(1)}, bf16[1,256,1024]{2,1,0:T(8,128)(2,1)S(1)}, u32[]{:S(2)}, u32[]{:S(2)}) %collective-permute-start.21) | collective-permute-done | bytes 524320 | tf_op jit(solution)/shard_map/ppermute | solution.py:17
  79.4 17.3 %collective-permute-done.24 = bf16[2,128,1024]{2,1,0:T(8,128)(2,1)S(1)} collective-permute-done((bf16[2,128,1024]{2,1,0:T(8,128)(2,1)S(1)}, bf16[2,128,1024]{2,1,0:T(8,128)(2,1)S(1)}, u32[]{:S(2)}, u32[]{:S(2)}) %collective-permute-start.24) | collective-permute-done | bytes 524320 | tf_op jit(solution)/shard_map/ppermute | solution.py:17
  96.6 1.6 collective-permute-start.4
  99.6 5.4 %collective-permute-start.13 = (bf16[256,1024]{1,0:T(8,128)(2,1)S(1)}, bf16[256,1024]{1,0:T(8,128)(2,1)}, u32[]{:S(2)}, u32[]{:S(2)}) collective-permute-start(bf16[256,1024]{1,0:T(8,128)(2,1)S(1)} %collective-permute-done.9), channel_id=1, source_target_pairs={{0,4},{4,8},{8,12},{1,5},{5,9},{9,13},{2,6},{6,10},{10,14},{3,7},{... | collective-permute-start | bytes 1572872 | tf_op jit(solution)/shard_map/ppermute | solution.py:58
  107.9 2.1 collective-permute-done.11
  110.1 8.5 %collective-permute-start.5 = (bf16[256,1024]{1,0:T(8,128)(2,1)S(1)}, bf16[256,1024]{1,0:T(8,128)(2,1)S(1)}, u32[]{:S(2)}, u32[]{:S(2)}) collective-permute-start(bf16[256,1024]{1,0:T(8,128)(2,1)S(1)} %collective-permute-done.4), channel_id=1, source_target_pairs={{0,4},{4,8},{8,12},{1,5},{5,9},{9,13},{2,6},{6,10},{10,14},{3,7},{... | collective-permute-start | bytes 1572872 | tf_op jit(solution)/shard_map/ppermute | solution.py:58
  119.9 9.2 %collective-permute-start.14 = (bf16[256,1024]{1,0:T(8,128)(2,1)}, bf16[256,1024]{1,0:T(8,128)(2,1)}, u32[]{:S(2)}, u32[]{:S(2)}) collective-permute-start(bf16[256,1024]{1,0:T(8,128)(2,1)} %collective-permute-done.13), channel_id=1, source_target_pairs={{0,4},{4,8},{8,12},{1,5},{5,9},{9,13},{2,6},{6,10},{10,14},{3,7},{... | collective-permute-start | bytes 1572872 | tf_op jit(solution)/shard_map/ppermute | solution.py:58
  130.2 1.5 collective-permute-start.26
  135.3 2.8 collective-permute-done.27
  138.2 2.0 bitcast_dynamic-update-slice_fusion.4
  140.2 3.9 %copy.70 = bf16[8,128,1024]{2,1,0:T(8,128)(2,1)} copy(bf16[8,128,1024]{1,2,0:T(8,128)(2,1)} %all-to-all-done) | data formatting | bytes 4194304 | tf_op jit(solution)/shard_map/all_to_all | solution.py:69
  144.1 5.8 %convolution_convert_fusion = bf16[1024,1024]{0,1:T(8,128)(2,1)} fusion(bf16[1024,1024]{1,0:T(8,128)(2,1)} %bitcast.263, bf16[1024,1024]{1,0:T(8,128)(2,1)} %bitcast.4), kind=kOutput, calls=%fused_computation.10 | convolution fusion | flops 2148532224 | bytes 6291456 | tf_op jit(solution)/shard_map/dot_general | solution.py:73
  150.0 4.4 %all-to-all-start.1 = ((bf16[8,128,1024]{2,1,0:T(8,128)(2,1)}), bf16[8,128,1024]{2,1,0:T(8,128)(2,1)}, u32[]{:S(2)}, u32[]{:S(2)}) async-start(bf16[8,128,1024]{2,1,0:T(8,128)(2,1)} %bitcast.266), calls=%async_computation.1 | async-start | bytes 4194304 | tf_op jit(solution)/shard_map/all_to_all | solution.py:69
  155.7 1.6 collective-permute-start.33
  158.9 1.5 broadcast_select_fusion.2
  160.4 2.8 collective-permute-start.34
  163.2 1.4 select_bitcast_fusion.1
  164.8 1.6 copy.77
  166.4 4.3 %copy.86 = bf16[8,128,1024]{1,0,2:T(8,128)(2,1)} copy(bf16[8,128,1024]{1,2,0:T(8,128)(2,1)} %all-to-all-done) | data formatting | bytes 4194304 | tf_op jit(solution)/shard_map/all_to_all | solution.py:69
  170.7 4.2 %reshape.367 = bf16[1024,4,256]{0,2,1:T(8,128)(2,1)} reshape(bf16[8,128,1024]{1,0,2:T(8,128)(2,1)} %copy.86) | data formatting | bytes 4194304 | tf_op jit(solution)/shard_map/reshape | solution.py:118
  174.9 1.6 bitcast_dynamic-update-slice_fusion.10
  177.1 1.6 bitcast_dynamic-update-slice_fusion.8
  180.2 4.5 %all-to-all-start.4 = ((bf16[4,1024,256]{1,2,0:T(8,128)(2,1)}), bf16[4,1024,256]{1,2,0:T(8,128)(2,1)}, u32[]{:S(2)}, u32[]{:S(2)}) async-start(bf16[4,1024,256]{1,2,0:T(8,128)(2,1)} %bitcast.245), calls=%async_computation.4 | async-start | bytes 4194304 | tf_op jit(solution)/shard_map/all_to_all | solution.py:69
  184.6 2.3 broadcast_select_fusion
  187.4 2.2 bitcast_dynamic-update-slice_fusion.2
  189.6 2.0 bitcast_dynamic-update-slice_fusion.1
  192.6 4.0 %select_reduce_fusion = f32[64,1024]{1,0:T(8,128)S(1)} fusion(pred[16,1024]{1,0:T(8,128)(4,1)S(1)} %iota_compare_fusion.2, bf16[16,64,1024]{2,1,0:T(8,128)(2,1)} %bitcast.261, bf16[1024,1024,1]{1,0,2:T(8,128)(2,1)S(1)} %bitcast.264), kind=kOutput, calls=%fused_computation.1 | convolution fusion | flops 2149515264 | bytes 4472832 | tf_op jit(solution)/shard_map/dot_general | solution.py:73
  197.1 2.0 collective-permute-start.15
  199.1 4.8 %fusion.13 = f32[1024,1024]{1,0:T(8,128)S(1)} fusion(bf16[1024,1024]{1,0:T(8,128)(2,1)} %bitcast.265, bf16[1024,1024]{1,0:T(8,128)(2,1)} %bitcast.262), kind=kOutput, calls=%fused_computation.108 | convolution fusion | flops 2147483648 | bytes 8388608 | tf_op jit(solution)/shard_map/dot_general | solution.py:73
  203.9 5.3 %add_convert_fusion = bf16[1024,1024]{1,0:T(8,128)(2,1)} fusion(f32[1024,1024]{1,0:T(8,128)S(1)} %fusion.13, bf16[1024,1024]{1,0:T(8,128)(2,1)S(1)} %bitcast.252, bf16[1024,1024]{1,0:T(8,128)(2,1)} %bitcast.4), kind=kOutput, calls=%fused_computation | convolution fusion | flops 2149580800 | bytes 10485760 | tf_op jit(solution)/shard_map/dot_general | solution.py:73
  209.2 1.5 collective-permute-start.16
  210.7 22.3 %all-to-all-done.4 = bf16[4,1024,256]{1,2,0:T(8,128)(2,1)} async-done(((bf16[4,1024,256]{1,2,0:T(8,128)(2,1)}), bf16[4,1024,256]{1,2,0:T(8,128)(2,1)}, u32[]{:S(2)}, u32[]{:S(2)}) %all-to-all-start.4) | async-done | bytes 2097184 | tf_op jit(solution)/shard_map/all_to_all | solution.py:69
  233.0 4.6 %all-to-all-start.3 = ((bf16[8,128,1024]{2,1,0:T(8,128)(2,1)}), bf16[8,128,1024]{2,1,0:T(8,128)(2,1)}, u32[]{:S(2)}, u32[]{:S(2)}) async-start(bf16[8,128,1024]{2,1,0:T(8,128)(2,1)} %bitcast.267), calls=%async_computation.3 | async-start | bytes 4194304 | tf_op jit(solution)/shard_map/all_to_all | solution.py:69
  237.6 2.4 broadcast_select_fusion.1
  240.2 3.9 %copy.87 = bf16[4,1024,256]{2,1,0:T(8,128)(2,1)} copy(bf16[4,1024,256]{1,2,0:T(8,128)(2,1)} %all-to-all-done.4) | data formatting | bytes 4194304 | tf_op jit(solution)/shard_map/all_to_all | solution.py:69
  244.2 1.8 fusion.10
  251.5 11.6 %all-to-all-done.3 = bf16[8,128,1024]{2,1,0:T(8,128)(2,1)} async-done(((bf16[8,128,1024]{2,1,0:T(8,128)(2,1)}), bf16[8,128,1024]{2,1,0:T(8,128)(2,1)}, u32[]{:S(2)}, u32[]{:S(2)}) %all-to-all-start.3) | async-done | bytes 2097184 | tf_op jit(solution)/shard_map/all_to_all | solution.py:69
  263.1 2.7 all-to-all-start.5
  265.9 1.7 convolution_multiply_fusion
  267.7 3.7 %collective-permute-start.37 = (bf16[64,1024]{1,0:T(8,128)(2,1)S(1)}, bf16[64,1024]{1,0:T(8,128)(2,1)S(1)}, u32[]{:S(2)}, u32[]{:S(2)}) collective-permute-start(bf16[64,1024]{1,0:T(8,128)(2,1)S(1)} %get-tuple-element.17), channel_id=1, source_target_pairs={{0,12},{4,0},{8,4},{12,8},{1,13},{5,1},{9,5},{13,9},{2,14},{6,2},{... | collective-permute-start | bytes 393224 | tf_op jit(solution)/shard_map/ppermute | solution.py:22
  272.5 14.2 %collective-permute-done.37 = bf16[64,1024]{1,0:T(8,128)(2,1)S(1)} collective-permute-done((bf16[64,1024]{1,0:T(8,128)(2,1)S(1)}, bf16[64,1024]{1,0:T(8,128)(2,1)S(1)}, u32[]{:S(2)}, u32[]{:S(2)}) %collective-permute-start.37) | collective-permute-done | bytes 131104 | tf_op jit(solution)/shard_map/ppermute | solution.py:22
  286.7 16.6 %collective-permute-done.36 = bf16[64,1024]{1,0:T(8,128)(2,1)S(1)} collective-permute-done((bf16[64,1024]{1,0:T(8,128)(2,1)S(1)}, bf16[64,1024]{1,0:T(8,128)(2,1)S(1)}, u32[]{:S(2)}, u32[]{:S(2)}) %collective-permute-start.36) | collective-permute-done | bytes 131104 | tf_op jit(solution)/shard_map/ppermute | solution.py:22
  304.0 2.0 convert_reduce_fusion
  307.2 3.3 %reshape.362 = bf16[2,4,128,4,256]{4,3,2,1,0:T(4,128)(2,1)S(1)} reshape(bf16[8,128,1024]{2,1,0:T(8,128)(2,1)} %all-to-all-done.3) | data formatting | bytes 4194304 | tf_op jit(solution)/shard_map/reshape | solution.py:192
  310.6 4.6 %copy.103 = bf16[2,4,128,4,256]{4,0,1,3,2:T(2,128)(2,1)} copy(bf16[2,4,128,4,256]{4,3,2,1,0:T(4,128)(2,1)S(1)} %reshape.362) | data formatting | bytes 4194304 | tf_op jit(solution)/shard_map/reshape | solution.py:192
  315.1 4.5 %reshape.363 = bf16[128,8192]{1,0:T(8,128)(2,1)} reshape(bf16[128,4,4,2,256]{4,3,2,1,0:T(2,128)(2,1)} %bitcast.247) | data formatting | bytes 4194304 | tf_op jit(solution)/shard_map/reshape | solution.py:193
  320.7 2.7 reshape.371
  (172 shorter events, 42.5 us)
Async XLA Ops:
  0.6 1.6 copy-start.10
  0.6 9.7 %copy-start.11 = (bf16[1,64,1024]{2,1,0:T(8,128)(2,1)S(1)}, bf16[1,64,1024]{2,1,0:T(8,128)(2,1)}, u32[]{:S(2)}) copy-start(bf16[1,64,1024]{2,1,0:T(8,128)(2,1)} %param.11) | copy-start | bytes 393220
  0.7 15.0 %copy-start.15 = (s32[128]{0:T(128)S(1)}, s32[128]{0:T(128)}, u32[]{:S(2)}) copy-start(s32[128]{0:T(128)} %param.8) | copy-start | bytes 1540
  0.7 16.5 %copy-start.5 = (bf16[1,8192,64]{1,2,0:T(8,128)(2,1)S(1)}, bf16[1,8192,64]{1,2,0:T(8,128)(2,1)}, u32[]{:S(2)}) copy-start(bf16[1,8192,64]{1,2,0:T(8,128)(2,1)} %param.10) | copy-start | bytes 3145732
  3.4 74.5 %collective-permute-start = (bf16[256,1024]{1,0:T(8,128)(2,1)}, bf16[256,1024]{1,0:T(8,128)(2,1)}, u32[]{:S(2)}, u32[]{:S(2)}) collective-permute-start(bf16[256,1024]{1,0:T(8,128)(2,1)} %get-tuple-element.5), channel_id=1, source_target_pairs={{0,4},{4,8},{8,12},{1,5},{5,9},{9,13},{2,6},{6,10},{10,14},{3,7},{... | collective-permute-start | bytes 1572872 | tf_op jit(solution)/shard_map/ppermute | solution.py:58
  9.1 69.0 %collective-permute-start.1 = (bf16[256,1024]{1,0:T(8,128)(2,1)}, bf16[256,1024]{1,0:T(8,128)(2,1)}, u32[]{:S(2)}, u32[]{:S(2)}) collective-permute-start(bf16[256,1024]{1,0:T(8,128)(2,1)} %get-tuple-element.5), channel_id=1, source_target_pairs={{4,0},{8,4},{12,8},{5,1},{9,5},{13,9},{6,2},{10,6},{14,10},{7,3},{... | collective-permute-start | bytes 1572872 | tf_op jit(solution)/shard_map/ppermute | solution.py:59
  10.4 45.6 %collective-permute-start.18 = (bf16[64,1024]{1,0:T(8,128)(2,1)S(1)}, bf16[64,1024]{1,0:T(8,128)(2,1)}, u32[]{:S(2)}, u32[]{:S(2)}) collective-permute-start(bf16[64,1024]{1,0:T(8,128)(2,1)S(1)} %bitcast.286), channel_id=1, source_target_pairs={{0,4},{4,8},{8,12},{12,0},{1,5},{5,9},{9,13},{13,1},{2,6},{6,10},{... | collective-permute-start | bytes 393224 | tf_op jit(solution)/shard_map/ppermute | solution.py:22
  13.1 44.5 %collective-permute-start.19 = (bf16[64,1024]{1,0:T(8,128)(2,1)S(1)}, bf16[64,1024]{1,0:T(8,128)(2,1)}, u32[]{:S(2)}, u32[]{:S(2)}) collective-permute-start(bf16[64,1024]{1,0:T(8,128)(2,1)S(1)} %bitcast.287), channel_id=1, source_target_pairs={{0,8},{4,12},{8,0},{12,4},{1,9},{5,13},{9,1},{13,5},{2,10},{6,14},... | collective-permute-start | bytes 393224 | tf_op jit(solution)/shard_map/ppermute | solution.py:22
  15.6 9.9 %collective-permute-start.6 = (s32[1,128]{1,0:T(1,128)S(1)}, s32[1,128]{1,0:T(1,128)S(1)}, u32[]{:S(2)}, u32[]{:S(2)}) collective-permute-start(s32[1,128]{1,0:T(1,128)S(1)} %bitcast.301), channel_id=1, source_target_pairs={{0,16},{16,0},{1,17},{17,1},{2,18},{18,2},{3,19},{19,3},{4,20},{20... | collective-permute-start | bytes 1544 | tf_op jit(solution)/shard_map/ppermute | solution.py:17
  20.6 42.4 %all-to-all-start.2 = ((bf16[4,64,1024]{2,1,0:T(8,128)(2,1)}), bf16[4,64,1024]{2,1,0:T(8,128)(2,1)S(1)}, u32[]{:S(2)}, u32[]{:S(2)}) async-start(bf16[4,64,1024]{2,1,0:T(8,128)(2,1)} %bitcast.119), calls=%async_computation.2 | async-start | bytes 1048576 | tf_op jit(solution)/shard_map/all_to_all | solution.py:69
  25.6 7.4 %collective-permute-start.7 = (s32[2,128]{1,0:T(2,128)S(1)}, s32[2,128]{1,0:T(2,128)S(1)}, u32[]{:S(2)}, u32[]{:S(2)}) collective-permute-start(s32[2,128]{1,0:T(2,128)S(1)} %add_bitcast_fusion), channel_id=1, source_target_pairs={{0,2},{1,3},{2,0},{3,1},{4,6},{5,7},{6,4},{7,5},{8,10},{9,11},{10,... | collective-permute-start | bytes 3080 | tf_op jit(solution)/shard_map/ppermute | solution.py:17
  33.0 7.6 %collective-permute-start.8 = (s32[4,128]{1,0:T(4,128)S(1)}, s32[4,128]{1,0:T(4,128)S(1)}, u32[]{:S(2)}, u32[]{:S(2)}) collective-permute-start(s32[4,128]{1,0:T(4,128)S(1)} %bitcast.298), channel_id=1, source_target_pairs={{0,1},{1,0},{2,3},{3,2},{4,5},{5,4},{6,7},{7,6},{8,9},{9,8},{10,11... | collective-permute-start | bytes 6152 | tf_op jit(solution)/shard_map/ppermute | solution.py:17
  36.4 19.6 %copy-start.6 = (bf16[128,1024]{1,0:T(8,128)(2,1)S(1)}, bf16[128,1024]{1,0:T(8,128)(2,1)}, u32[]{:S(2)}) copy-start(bf16[128,1024]{1,0:T(8,128)(2,1)} %param.7) | copy-start | bytes 786436
  40.6 5.5 %collective-permute-start.29 = (s32[8,128]{1,0:T(8,128)S(1)}, s32[8,128]{1,0:T(8,128)S(1)}, u32[]{:S(2)}, u32[]{:S(2)}) collective-permute-start(s32[8,128]{1,0:T(8,128)S(1)} %bitcast.291), channel_id=1, source_target_pairs={{0,4},{4,8},{8,12},{12,0},{1,5},{5,9},{9,13},{13,1},{2,6},{6,10},{... | collective-permute-start | bytes 12296 | tf_op jit(solution)/shard_map/ppermute | solution.py:22
  46.1 4.5 %collective-permute-start.30 = (s32[8,128]{1,0:T(8,128)S(1)}, s32[8,128]{1,0:T(8,128)S(1)}, u32[]{:S(2)}, u32[]{:S(2)}) collective-permute-start(s32[8,128]{1,0:T(8,128)S(1)} %bitcast.293), channel_id=1, source_target_pairs={{0,8},{4,12},{8,0},{12,4},{1,9},{5,13},{9,1},{13,5},{2,10},{6,14},... | collective-permute-start | bytes 12296 | tf_op jit(solution)/shard_map/ppermute | solution.py:22
  50.6 3.6 %collective-permute-start.31 = (s32[8,128]{1,0:T(8,128)S(1)}, s32[8,128]{1,0:T(8,128)S(1)}, u32[]{:S(2)}, u32[]{:S(2)}) collective-permute-start(s32[8,128]{1,0:T(8,128)S(1)} %bitcast.294), channel_id=1, source_target_pairs={{0,12},{4,0},{8,4},{12,8},{1,13},{5,1},{9,5},{13,9},{2,14},{6,2},{... | collective-permute-start | bytes 12296 | tf_op jit(solution)/shard_map/ppermute | solution.py:22
  54.2 5.0 %collective-permute-start.20 = (bf16[64,1024]{1,0:T(8,128)(2,1)S(1)}, bf16[64,1024]{1,0:T(8,128)(2,1)S(1)}, u32[]{:S(2)}, u32[]{:S(2)}) collective-permute-start(bf16[64,1024]{1,0:T(8,128)(2,1)S(1)} %bitcast.288), channel_id=1, source_target_pairs={{0,12},{4,0},{8,4},{12,8},{1,13},{5,1},{9,5},{13,9},{2,14},{6,2},{... | collective-permute-start | bytes 393224 | tf_op jit(solution)/shard_map/ppermute | solution.py:22
  56.0 6.4 %collective-permute-start.23 = (bf16[1,128,1024]{2,1,0:T(8,128)(2,1)S(1)}, bf16[1,128,1024]{2,1,0:T(8,128)(2,1)S(1)}, u32[]{:S(2)}, u32[]{:S(2)}) collective-permute-start(bf16[1,128,1024]{2,1,0:T(8,128)(2,1)S(1)} %bitcast.283), channel_id=1, source_target_pairs={{0,16},{16,0},{1,17},{17,1},{2,18},{18,2},{3,19},{19,3},{4,20},{20... | collective-permute-start | bytes 786440 | tf_op jit(solution)/shard_map/ppermute | solution.py:17
  59.2 17.2 %collective-permute-start.21 = (bf16[1,256,1024]{2,1,0:T(8,128)(2,1)S(1)}, bf16[1,256,1024]{2,1,0:T(8,128)(2,1)S(1)}, u32[]{:S(2)}, u32[]{:S(2)}) collective-permute-start(bf16[1,256,1024]{2,1,0:T(8,128)(2,1)S(1)} %bitcast.259), channel_id=1, source_target_pairs={{0,2},{1,3},{2,0},{3,1},{4,6},{5,7},{6,4},{7,5},{8,10},{9,11},{10,... | collective-permute-start | bytes 1572872 | tf_op jit(solution)/shard_map/ppermute | solution.py:17
  62.6 34.0 %collective-permute-start.24 = (bf16[2,128,1024]{2,1,0:T(8,128)(2,1)S(1)}, bf16[2,128,1024]{2,1,0:T(8,128)(2,1)S(1)}, u32[]{:S(2)}, u32[]{:S(2)}) collective-permute-start(bf16[2,128,1024]{2,1,0:T(8,128)(2,1)S(1)} %maximum_bitcast_fusion.1), channel_id=1, source_target_pairs={{0,2},{1,3},{2,0},{3,1},{4,6},{5,7},{6,4},{7,5},{8,10},{9,11},{10,... | collective-permute-start | bytes 1572872 | tf_op jit(solution)/shard_map/ppermute | solution.py:17
  63.0 77.2 %all-to-all-start = ((bf16[8,128,1024]{1,2,0:T(8,128)(2,1)}), bf16[8,128,1024]{1,2,0:T(8,128)(2,1)}, u32[]{:S(2)}, u32[]{:S(2)}) async-start(bf16[8,128,1024]{1,2,0:T(8,128)(2,1)} %bitcast.6), calls=%async_computation | async-start | bytes 4194304 | tf_op jit(solution)/shard_map/all_to_all | solution.py:69
  67.4 32.2 %collective-permute-start.9 = (bf16[256,1024]{1,0:T(8,128)(2,1)S(1)}, bf16[256,1024]{1,0:T(8,128)(2,1)S(1)}, u32[]{:S(2)}, u32[]{:S(2)}) collective-permute-start(bf16[256,1024]{1,0:T(8,128)(2,1)S(1)} %bitcast.269), channel_id=1, source_target_pairs={{0,4},{4,8},{8,12},{1,5},{5,9},{9,13},{2,6},{6,10},{10,14},{3,7},{... | collective-permute-start | bytes 1572872 | tf_op jit(solution)/shard_map/ppermute | solution.py:58
  76.4 21.8 %collective-permute-start.10 = (bf16[256,1024]{1,0:T(8,128)(2,1)S(1)}, bf16[256,1024]{1,0:T(8,128)(2,1)S(1)}, u32[]{:S(2)}, u32[]{:S(2)}) collective-permute-start(bf16[256,1024]{1,0:T(8,128)(2,1)S(1)} %bitcast.270), channel_id=1, source_target_pairs={{4,0},{8,4},{12,8},{5,1},{9,5},{13,9},{6,2},{10,6},{14,10},{7,3},{... | collective-permute-start | bytes 1572872 | tf_op jit(solution)/shard_map/ppermute | solution.py:59
  77.9 42.0 %collective-permute-start.22 = (bf16[2,256,1024]{2,1,0:T(8,128)(2,1)S(1)}, bf16[2,256,1024]{2,1,0:T(8,128)(2,1)S(1)}, u32[]{:S(2)}, u32[]{:S(2)}) collective-permute-start(bf16[2,256,1024]{2,1,0:T(8,128)(2,1)S(1)} %maximum_bitcast_fusion), channel_id=1, source_target_pairs={{0,1},{1,0},{2,3},{3,2},{4,5},{5,4},{6,7},{7,6},{8,9},{9,8},{10,11... | collective-permute-start | bytes 3145736 | tf_op jit(solution)/shard_map/ppermute | solution.py:17
  78.1 28.6 %collective-permute-start.2 = (bf16[256,1024]{1,0:T(8,128)(2,1)}, bf16[256,1024]{1,0:T(8,128)(2,1)S(1)}, u32[]{:S(2)}, u32[]{:S(2)}) collective-permute-start(bf16[256,1024]{1,0:T(8,128)(2,1)} %collective-permute-done.1), channel_id=1, source_target_pairs={{4,0},{8,4},{12,8},{5,1},{9,5},{13,9},{6,2},{10,6},{14,10},{7,3},{... | collective-permute-start | bytes 1572872 | tf_op jit(solution)/shard_map/ppermute | solution.py:59
  96.6 10.0 %collective-permute-start.4 = (bf16[256,1024]{1,0:T(8,128)(2,1)}, bf16[256,1024]{1,0:T(8,128)(2,1)S(1)}, u32[]{:S(2)}, u32[]{:S(2)}) collective-permute-start(bf16[256,1024]{1,0:T(8,128)(2,1)} %collective-permute-done), channel_id=1, source_target_pairs={{0,4},{4,8},{8,12},{1,5},{5,9},{9,13},{2,6},{6,10},{10,14},{3,7},{... | collective-permute-start | bytes 1572872 | tf_op jit(solution)/shard_map/ppermute | solution.py:58
  98.3 7.1 %copy-start.7 = (bf16[256,1024]{1,0:T(8,128)(2,1)}, bf16[256,1024]{1,0:T(8,128)(2,1)S(1)}, u32[]{:S(2)}) copy-start(bf16[256,1024]{1,0:T(8,128)(2,1)S(1)} %collective-permute-done.10) | copy-start | bytes 1572868
  98.3 11.8 %collective-permute-start.11 = (bf16[256,1024]{1,0:T(8,128)(2,1)S(1)}, bf16[256,1024]{1,0:T(8,128)(2,1)}, u32[]{:S(2)}, u32[]{:S(2)}) collective-permute-start(bf16[256,1024]{1,0:T(8,128)(2,1)S(1)} %collective-permute-done.10), channel_id=1, source_target_pairs={{4,0},{8,4},{12,8},{5,1},{9,5},{13,9},{6,2},{10,6},{14,10},{7,3},{... | collective-permute-start | bytes 1572872 | tf_op jit(solution)/shard_map/ppermute | solution.py:59
  99.6 5.8 %copy-start.9 = (bf16[256,1024]{1,0:T(8,128)(2,1)}, bf16[256,1024]{1,0:T(8,128)(2,1)S(1)}, u32[]{:S(2)}) copy-start(bf16[256,1024]{1,0:T(8,128)(2,1)S(1)} %collective-permute-done.9) | copy-start | bytes 1572868
  99.6 19.0 %collective-permute-start.13 = (bf16[256,1024]{1,0:T(8,128)(2,1)S(1)}, bf16[256,1024]{1,0:T(8,128)(2,1)}, u32[]{:S(2)}, u32[]{:S(2)}) collective-permute-start(bf16[256,1024]{1,0:T(8,128)(2,1)S(1)} %collective-permute-done.9), channel_id=1, source_target_pairs={{0,4},{4,8},{8,12},{1,5},{5,9},{9,13},{2,6},{6,10},{10,14},{3,7},{... | collective-permute-start | bytes 1572872 | tf_op jit(solution)/shard_map/ppermute | solution.py:58
  105.3 1.4 copy-start.3
  106.6 53.8 %collective-permute-start.25 = (bf16[4,128,1024]{2,1,0:T(8,128)(2,1)S(1)}, bf16[4,128,1024]{2,1,0:T(8,128)(2,1)}, u32[]{:S(2)}, u32[]{:S(2)}) collective-permute-start(bf16[4,128,1024]{2,1,0:T(8,128)(2,1)S(1)} %bitcast.253), channel_id=1, source_target_pairs={{0,1},{1,0},{2,3},{3,2},{4,5},{5,4},{6,7},{7,6},{8,9},{9,8},{10,11... | collective-permute-start | bytes 3145736 | tf_op jit(solution)/shard_map/ppermute | solution.py:17
  106.6 23.6 %collective-permute-start.3 = (bf16[256,1024]{1,0:T(8,128)(2,1)S(1)}, bf16[256,1024]{1,0:T(8,128)(2,1)S(1)}, u32[]{:S(2)}, u32[]{:S(2)}) collective-permute-start(bf16[256,1024]{1,0:T(8,128)(2,1)S(1)} %collective-permute-done.2), channel_id=1, source_target_pairs={{4,0},{8,4},{12,8},{5,1},{9,5},{13,9},{6,2},{10,6},{14,10},{7,3},{... | collective-permute-start | bytes 1572872 | tf_op jit(solution)/shard_map/ppermute | solution.py:59
  110.1 28.1 %collective-permute-start.5 = (bf16[256,1024]{1,0:T(8,128)(2,1)S(1)}, bf16[256,1024]{1,0:T(8,128)(2,1)S(1)}, u32[]{:S(2)}, u32[]{:S(2)}) collective-permute-start(bf16[256,1024]{1,0:T(8,128)(2,1)S(1)} %collective-permute-done.4), channel_id=1, source_target_pairs={{0,4},{4,8},{8,12},{1,5},{5,9},{9,13},{2,6},{6,10},{10,14},{3,7},{... | collective-permute-start | bytes 1572872 | tf_op jit(solution)/shard_map/ppermute | solution.py:58
  118.6 68.8 %collective-permute-start.12 = (bf16[256,1024]{1,0:T(8,128)(2,1)}, bf16[256,1024]{1,0:T(8,128)(2,1)}, u32[]{:S(2)}, u32[]{:S(2)}) collective-permute-start(bf16[256,1024]{1,0:T(8,128)(2,1)} %collective-permute-done.11), channel_id=1, source_target_pairs={{4,0},{8,4},{12,8},{5,1},{9,5},{13,9},{6,2},{10,6},{14,10},{7,3},{... | collective-permute-start | bytes 1572872 | tf_op jit(solution)/shard_map/ppermute | solution.py:59
  119.9 71.7 %collective-permute-start.14 = (bf16[256,1024]{1,0:T(8,128)(2,1)}, bf16[256,1024]{1,0:T(8,128)(2,1)}, u32[]{:S(2)}, u32[]{:S(2)}) collective-permute-start(bf16[256,1024]{1,0:T(8,128)(2,1)} %collective-permute-done.13), channel_id=1, source_target_pairs={{0,4},{4,8},{8,12},{1,5},{5,9},{9,13},{2,6},{6,10},{10,14},{3,7},{... | collective-permute-start | bytes 1572872 | tf_op jit(solution)/shard_map/ppermute | solution.py:58
  129.4 0.7 copy-start.12
  130.2 3.8 %collective-permute-start.26 = (bf16[1,64,128]{2,1,0:T(8,128)(2,1)S(1)}, bf16[1,64,128]{2,1,0:T(8,128)(2,1)S(1)}, u32[]{:S(2)}, u32[]{:S(2)}) collective-permute-start(bf16[1,64,128]{2,1,0:T(8,128)(2,1)S(1)} %bitcast.295), channel_id=1, source_target_pairs={{0,16},{16,0},{1,17},{17,1},{2,18},{18,2},{3,19},{19,3},{4,20},{20... | collective-permute-start | bytes 49160 | tf_op jit(solution)/shard_map/ppermute | solution.py:17
  134.0 4.0 %collective-permute-start.27 = (bf16[2,64,128]{2,1,0:T(8,128)(2,1)S(1)}, bf16[2,64,128]{2,1,0:T(8,128)(2,1)S(1)}, u32[]{:S(2)}, u32[]{:S(2)}) collective-permute-start(bf16[2,64,128]{2,1,0:T(8,128)(2,1)S(1)} %maximum_bitcast_fusion.2), channel_id=1, source_target_pairs={{0,2},{1,3},{2,0},{3,1},{4,6},{5,7},{6,4},{7,5},{8,10},{9,11},{10,... | collective-permute-start | bytes 98312 | tf_op jit(solution)/shard_map/ppermute | solution.py:17
  138.1 2.1 collective-permute-start.28
  150.0 30.2 %all-to-all-start.1 = ((bf16[8,128,1024]{2,1,0:T(8,128)(2,1)}), bf16[8,128,1024]{2,1,0:T(8,128)(2,1)}, u32[]{:S(2)}, u32[]{:S(2)}) async-start(bf16[8,128,1024]{2,1,0:T(8,128)(2,1)} %bitcast.266), calls=%async_computation.1 | async-start | bytes 4194304 | tf_op jit(solution)/shard_map/all_to_all | solution.py:69
  154.4 20.4 %collective-permute-start.32 = (bf16[8,64,128]{2,1,0:T(8,128)(2,1)S(1)}, bf16[8,64,128]{2,1,0:T(8,128)(2,1)}, u32[]{:S(2)}, u32[]{:S(2)}) collective-permute-start(bf16[8,64,128]{2,1,0:T(8,128)(2,1)S(1)} %bitcast.273), channel_id=1, source_target_pairs={{0,4},{4,8},{8,12},{12,0},{1,5},{5,9},{9,13},{13,1},{2,6},{6,10},{... | collective-permute-start | bytes 393224 | tf_op jit(solution)/shard_map/ppermute | solution.py:22
  155.7 20.8 %collective-permute-start.33 = (bf16[8,64,128]{2,1,0:T(8,128)(2,1)S(1)}, bf16[8,64,128]{2,1,0:T(8,128)(2,1)S(1)}, u32[]{:S(2)}, u32[]{:S(2)}) collective-permute-start(bf16[8,64,128]{2,1,0:T(8,128)(2,1)S(1)} %bitcast.274), channel_id=1, source_target_pairs={{0,8},{4,12},{8,0},{12,4},{1,9},{5,13},{9,1},{13,5},{2,10},{6,14},... | collective-permute-start | bytes 393224 | tf_op jit(solution)/shard_map/ppermute | solution.py:22
  160.4 16.7 %collective-permute-start.34 = (bf16[8,64,128]{2,1,0:T(8,128)(2,1)S(1)}, bf16[8,64,128]{2,1,0:T(8,128)(2,1)}, u32[]{:S(2)}, u32[]{:S(2)}) collective-permute-start(bf16[8,64,128]{2,1,0:T(8,128)(2,1)S(1)} %bitcast.277), channel_id=1, source_target_pairs={{0,12},{4,0},{8,4},{12,8},{1,13},{5,1},{9,5},{13,9},{2,14},{6,2},{... | collective-permute-start | bytes 393224 | tf_op jit(solution)/shard_map/ppermute | solution.py:22
  180.2 52.8 %all-to-all-start.4 = ((bf16[4,1024,256]{1,2,0:T(8,128)(2,1)}), bf16[4,1024,256]{1,2,0:T(8,128)(2,1)}, u32[]{:S(2)}, u32[]{:S(2)}) async-start(bf16[4,1024,256]{1,2,0:T(8,128)(2,1)} %bitcast.245), calls=%async_computation.4 | async-start | bytes 4194304 | tf_op jit(solution)/shard_map/all_to_all | solution.py:69
  187.0 4.7 %copy-start.8 = (bf16[256,1024]{1,0:T(8,128)(2,1)S(1)}, bf16[256,1024]{1,0:T(8,128)(2,1)}, u32[]{:S(2)}) copy-start(bf16[256,1024]{1,0:T(8,128)(2,1)} %copy-done.7) | copy-start | bytes 1572868
  187.4 5.3 %copy-start.4 = (bf16[8,128,1024]{2,1,0:T(8,128)(2,1)S(1)}, bf16[8,128,1024]{2,1,0:T(8,128)(2,1)}, u32[]{:S(2)}) copy-start(bf16[8,128,1024]{2,1,0:T(8,128)(2,1)} %copy.70) | copy-start | bytes 6291460
  197.1 12.1 %collective-permute-start.15 = (f32[64,512]{1,0:T(8,128)S(1)}, f32[64,512]{1,0:T(8,128)S(1)}, u32[]{:S(2)}, u32[]{:S(2)}) collective-permute-start(f32[64,512]{1,0:T(8,128)S(1)} %bitcast.289), channel_id=1, source_target_pairs={{0,16},{16,0},{1,17},{17,1},{2,18},{18,2},{3,19},{19,3},{4,20},{20... | collective-permute-start | bytes 393224 | tf_op jit(solution)/shard_map/ppermute | solution.py:22
  199.1 4.8 %copy-start = (bf16[4,2,128,1024]{3,2,1,0:T(8,128)(2,1)S(1)}, bf16[4,2,128,1024]{3,2,1,0:T(8,128)(2,1)}, u32[]{:S(2)}) copy-start(bf16[4,2,128,1024]{3,2,1,0:T(8,128)(2,1)} %copy.77) | copy-start | bytes 6291460
  209.2 30.8 %collective-permute-start.16 = (f32[64,512]{1,0:T(8,128)S(1)}, f32[64,512]{1,0:T(8,128)S(1)}, u32[]{:S(2)}, u32[]{:S(2)}) collective-permute-start(f32[64,512]{1,0:T(8,128)S(1)} %bitcast_add_fusion.1), channel_id=1, source_target_pairs={{0,2},{1,3},{2,0},{3,1},{4,6},{5,7},{6,4},{7,5},{8,10},{9,11},{10,... | collective-permute-start | bytes 393224 | tf_op jit(solution)/shard_map/ppermute | solution.py:17
  233.0 30.1 %all-to-all-start.3 = ((bf16[8,128,1024]{2,1,0:T(8,128)(2,1)}), bf16[8,128,1024]{2,1,0:T(8,128)(2,1)}, u32[]{:S(2)}, u32[]{:S(2)}) async-start(bf16[8,128,1024]{2,1,0:T(8,128)(2,1)} %bitcast.267), calls=%async_computation.3 | async-start | bytes 4194304 | tf_op jit(solution)/shard_map/all_to_all | solution.py:69
  240.0 25.8 %collective-permute-start.17 = (f32[64,512]{1,0:T(8,128)S(1)}, f32[64,512]{1,0:T(8,128)S(1)}, u32[]{:S(2)}, u32[]{:S(2)}) collective-permute-start(f32[64,512]{1,0:T(8,128)S(1)} %add.183), channel_id=1, source_target_pairs={{0,1},{1,0},{2,3},{3,2},{4,5},{5,4},{6,7},{7,6},{8,9},{9,8},{10,11... | collective-permute-start | bytes 393224 | tf_op jit(solution)/shard_map/ppermute | solution.py:17
  244.2 2.8 copy-start.1
  247.0 2.2 copy-start.2
  250.4 15.3 %copy-start.14 = (s32[1,512]{1,0:T(1,128)S(1)}, s32[1,512]{1,0:T(1,128)}, u32[]{:S(2)}) copy-start(s32[1,512]{1,0:T(1,128)} %constant_dynamic-slice_fusion) | copy-start | bytes 6148
  250.4 15.3 %copy-start.16 = (s32[4]{0:T(128)S(1)}, s32[4]{0:T(128)}, u32[]{:S(2)}) copy-start(s32[4]{0:T(128)} %broadcast_add_fusion) | copy-start | bytes 52
  263.1 56.5 %all-to-all-start.5 = ((bf16[32,64,256]{2,1,0:T(8,128)(2,1)}), bf16[32,64,256]{2,1,0:T(8,128)(2,1)S(1)}, u32[]{:S(2)}, u32[]{:S(2)}) async-start(bf16[32,64,256]{2,1,0:T(8,128)(2,1)} %bitcast.257), calls=%async_computation.5 | async-start | bytes 2097152 | tf_op jit(solution)/shard_map/all_to_all | solution.py:69
  265.9 6.6 %copy-start.13 = (pred[16,128]{1,0:T(8,128)(4,1)S(1)}, pred[16,128]{1,0:T(8,128)(4,1)}, u32[]{:S(2)}) copy-start(pred[16,128]{1,0:T(8,128)(4,1)} %broadcast_compare_fusion.1) | copy-start | bytes 6148
  267.7 19.0 %collective-permute-start.37 = (bf16[64,1024]{1,0:T(8,128)(2,1)S(1)}, bf16[64,1024]{1,0:T(8,128)(2,1)S(1)}, u32[]{:S(2)}, u32[]{:S(2)}) collective-permute-start(bf16[64,1024]{1,0:T(8,128)(2,1)S(1)} %get-tuple-element.17), channel_id=1, source_target_pairs={{0,12},{4,0},{8,4},{12,8},{1,13},{5,1},{9,5},{13,9},{2,14},{6,2},{... | collective-permute-start | bytes 393224 | tf_op jit(solution)/shard_map/ppermute | solution.py:22
  271.4 31.9 %collective-permute-start.36 = (bf16[64,1024]{1,0:T(8,128)(2,1)S(1)}, bf16[64,1024]{1,0:T(8,128)(2,1)S(1)}, u32[]{:S(2)}, u32[]{:S(2)}) collective-permute-start(bf16[64,1024]{1,0:T(8,128)(2,1)S(1)} %get-tuple-element.18), channel_id=1, source_target_pairs={{0,8},{4,12},{8,0},{12,4},{1,9},{5,13},{9,1},{13,5},{2,10},{6,14},... | collective-permute-start | bytes 393224 | tf_op jit(solution)/shard_map/ppermute | solution.py:22
  271.4 31.9 %collective-permute-start.35 = (bf16[64,1024]{1,0:T(8,128)(2,1)S(1)}, bf16[64,1024]{1,0:T(8,128)(2,1)S(1)}, u32[]{:S(2)}, u32[]{:S(2)}) collective-permute-start(bf16[64,1024]{1,0:T(8,128)(2,1)S(1)} %get-tuple-element.16), channel_id=1, source_target_pairs={{0,4},{4,8},{8,12},{12,0},{1,5},{5,9},{9,13},{13,1},{2,6},{6,10},{... | collective-permute-start | bytes 393224 | tf_op jit(solution)/shard_map/ppermute | solution.py:22

commit v2 on v1

--- a/solution.py
+++ b/solution.py
@@ -3,6 +3,8 @@
 import jax
 import jax.numpy as jnp
 from jax import lax
+from jax.experimental import pallas as pl
+from jax.experimental.pallas import tpu as pltpu
 from jax.sharding import Mesh
 from jax.sharding import PartitionSpec as P
 
@@ -37,15 +39,8 @@
     return stack
 
 
-def straight_gather(array, axis):
-    peers = lax.axis_size(axis)
-    me = lax.axis_index(axis)
-    stack = jnp.zeros((peers,) + array.shape, array.dtype)
-    stack = lax.dynamic_update_index_in_dim(stack, array, me, 0)
-    for by in range(1, peers):
-        got = shifted(array, axis, by)
-        stack = lax.dynamic_update_index_in_dim(stack, got, (me - by) % peers, 0)
-    return stack
+def relative(array, axis):
+    return [array] + [shifted(array, axis, by) for by in range(1, lax.axis_size(axis))]
 
 
 def line_gather(array, axis):
@@ -63,6 +58,23 @@
         block = jnp.where(me >= by, rising[by], falling[peers - by])
         stack = lax.dynamic_update_index_in_dim(stack, block, (me - by) % peers, 0)
     return stack
+
+
+def repacked(array, shape, moves):
+    def kernel(source, target):
+        for (r, c), (to_r, to_c), (high, wide) in moves:
+            target[pl.ds(to_r, high), pl.ds(to_c, wide)] = source[pl.ds(r, high), pl.ds(c, wide)]
+
+    return pl.pallas_call(
+        kernel,
+        out_shape=jax.ShapeDtypeStruct(shape, array.dtype),
+        in_specs=[pl.BlockSpec(memory_space=pltpu.VMEM)],
+        out_specs=pl.BlockSpec(memory_space=pltpu.VMEM),
+        compiler_params=pltpu.CompilerParams(vmem_limit_bytes=16 << 20),
+        cost_estimate=pl.CostEstimate(
+            flops=0, bytes_accessed=2 * array.size * array.dtype.itemsize, transcendentals=0
+        ),
+    )(array)
 
 
 def exchanged(array, axes):
@@ -100,23 +112,31 @@
         wide = jnp.where(hit, values[None], jnp.zeros((), values.dtype))
         return wide.reshape(count * rank, -1)
 
-    def gathered_in(wide, labels, order):
-        hit = labels[None, None, :] == order[:, None, None]
-        return jnp.sum(jnp.where(hit, wide.reshape(order.shape[0], rank, -1), 0.0), axis=0)
-
-    up_line = straight_gather(adapter_up_weight[0], "z")
-    up_all = cube_gather(up_line.reshape(outer * rank, out_width), ("q",))
-    up_all = up_all.reshape(jobs * rank, out_width)
-    up_order = (
-        jnp.arange(outer, dtype=jnp.int32)[None, :] * inner
-        + jnp.arange(inner, dtype=jnp.int32)[:, None]
-    ).reshape(-1)
-
-    act_send = activations.reshape(rows, outer, inner, groups, piece)
-    act_send = act_send.transpose(3, 2, 0, 1, 4).reshape(plane_rows, flat)
+    def own_of(wide, labels, first, count):
+        wanted = first + jnp.arange(count, dtype=jnp.int32)
+        hit = labels[None, None, :] == wanted[:, None, None]
+        return jnp.sum(jnp.where(hit, wide.reshape(count, rank, -1), 0.0), axis=0)
+
+    aligned = piece % 128 == 0 and rows % 16 == 0
+    moves = []
+    for g in range(groups):
+        for p in range(inner):
+            for o in range(outer):
+                wide_at = (0, ((o * inner + p) * groups + g) * piece)
+                flat_at = ((g * inner + p) * rows, o * piece)
+                moves.append((wide_at, flat_at, (rows, piece)))
+
+    if aligned:
+        act_send = repacked(activations, (plane_rows, flat), moves)
+    else:
+        act_send = activations.reshape(rows, outer, inner, groups, piece)
+        act_send = act_send.transpose(3, 2, 0, 1, 4).reshape(plane_rows, flat)
+    act_send, value_projection_weight, adapter_down_weight, upstream, adapter_up_weight = (
+        lax.optimization_barrier(
+            (act_send, value_projection_weight, adapter_down_weight, upstream, adapter_up_weight)
+        )
+    )
     act_plane = exchanged(act_send, PLANE)
-    act_deep = act_plane.reshape(plane_rows, outer, piece).transpose(1, 0, 2)
-    act_deep = exchanged(act_deep.reshape(outer * plane_rows, piece), "z")
 
     part = value_projection_weight.shape[0] // groups
     weight_half = lax.dynamic_slice_in_dim(value_projection_weight, group * part, part, 0)
@@ -127,27 +147,34 @@
     down_block = exchanged(down_send, "q")
     down = line_gather(down_block, "z")
 
-    labels_plane = cube_gather(row_job_labels, PLANE)
-    labels_deep = straight_gather(labels_plane, "z")
-    labels_plane = labels_plane.reshape(-1)
-    upstream_plane = cube_gather(upstream, PLANE)
+    up_all = lax.all_gather(adapter_up_weight[0], ("z", "q"), axis=0, tiled=True)
+    upstream_plane = lax.all_gather(upstream, PLANE, axis=0, tiled=True)
 
     wide = ADAPTER_SCALE * dot(up_all, upstream, 1, 1)
-    scaled = gathered_in(wide, row_job_labels, up_order).astype(BF16)
-    scaled_plane = cube_gather(scaled, PLANE)
-    scaled_deep = straight_gather(scaled_plane, "z")
-    scaled_plane = scaled_plane.transpose(1, 0, 2).reshape(rank, plane_rows)
-
-    act_deep = act_deep.reshape(outer, groups, inner * rows, piece)
-    scaled_deep = scaled_deep.reshape(outer, groups, inner, rank, rows)
-    scaled_deep = scaled_deep.transpose(1, 3, 0, 2, 4).reshape(groups, rank, -1)
-    labels_deep = labels_deep.reshape(outer, groups, inner * rows)
+    scaled = own_of(wide, row_job_labels, 0, jobs).astype(BF16)
+    label_rows = jnp.broadcast_to(row_job_labels.astype(BF16)[None], (16, rows))
+    packet = cube_gather(jnp.concatenate([scaled, label_rows], axis=0), PLANE)
+    packet = packet.transpose(1, 0, 2).reshape(rank + 16, plane_rows)
+    packets = relative(packet, "z")
+    scaled_plane = packet[:rank]
+    labels_plane = packet[rank].astype(jnp.int32)
+
+    blocks = []
+    for by in range(outer):
+        at = (level + by) % outer * piece
+        block = lax.dynamic_slice_in_dim(act_plane, at, piece, 1)
+        blocks.append(shifted(block, "z", by) if by else block)
+
     small = jobs * rank * outer * inner * rows <= 1 << 22
+    half = inner * rows
 
     def down_grad_part(g, first, count):
-        columns = act_deep[:, g].reshape(-1, piece)
-        wide = spread(scaled_deep[g], labels_deep[:, g].reshape(-1), first, count)
-        return dot(wide, columns, 1, 0).astype(BF16)
+        total = jnp.zeros((count * rank, piece), F32)
+        for packet, block in zip(packets, blocks):
+            packet = packet[:, g * half : (g + 1) * half]
+            wide = spread(packet[:rank], packet[rank].astype(jnp.int32), first, count)
+            total = total + dot(wide, block[g * half : (g + 1) * half], 1, 0)
+        return total.astype(BF16)
 
     if small:
         down_parts = [down_grad_part(g, 0, jobs) for g in range(groups)]
@@ -163,34 +190,46 @@
     down_parts = down_parts.reshape(groups, outer, inner, rank, piece)
     down_grad = down_parts.transpose(3, 1, 2, 0, 4).reshape(rank, width).astype(F32).T
 
-    frozen = dot(act_plane, weight, 1, 0).astype(BF16)
-    frozen = exchanged(frozen, PLANE).reshape(plane, rows, out_width)
-    frozen = jnp.sum(frozen.astype(F32), axis=0)
-
-    back = dot(upstream_plane.reshape(plane_rows, out_width), weight, 1, 1)
+    frozen = dot(act_plane, weight, 1, 0).reshape(groups, inner, rows, out_width)
+    bit = 1
+    while bit < inner:
+        pairs = frozen.reshape(groups, inner // bit // 2, 2, rows, out_width)
+        mine = (place // bit) % 2
+        kept = lax.dynamic_index_in_dim(pairs, mine, 2, keepdims=False)
+        leaving = lax.dynamic_index_in_dim(pairs, 1 - mine, 2, keepdims=False)
+        frozen = kept + swapped(leaving.astype(BF16), "q", bit).astype(F32)
+        bit *= 2
+    frozen = frozen.reshape(groups, rows, out_width)
+    total = lax.dynamic_index_in_dim(frozen, group, 0, keepdims=False)
+    for by in range(1, groups):
+        leaving = lax.dynamic_index_in_dim(frozen, (group + by) % groups, 0, keepdims=False)
+        total = total + shifted(leaving.astype(BF16), "groups", by).astype(F32)
+    frozen = total
+
+    back = dot(upstream_plane, weight, 1, 1)
     if small:
         down_all = down.reshape(jobs * rank, flat)
         back = back + dot(spread(scaled_plane, labels_plane, 0, jobs), down_all, 0, 0)
-        reduced = gathered_in(
-            dot(down_all, act_plane, 1, 1), labels_plane, jnp.arange(jobs, dtype=jnp.int32)
-        )
+        reduced = own_of(dot(down_all, act_plane, 1, 1), labels_plane, 0, jobs)
     else:
 
         def step(carry, operands):
             back, reduced = carry
             block, first = operands
-            wide = spread(scaled_plane, labels_plane, first, inner)
-            order = first + jnp.arange(inner, dtype=jnp.int32)
-            back = back + dot(wide, block, 0, 0)
-            reduced = reduced + gathered_in(dot(block, act_plane, 1, 1), labels_plane, order)
+            back = back + dot(spread(scaled_plane, labels_plane, first, inner), block, 0, 0)
+            reduced = reduced + own_of(dot(block, act_plane, 1, 1), labels_plane, first, inner)
             return (back, reduced), None
 
         firsts = jnp.arange(outer, dtype=jnp.int32) * inner
         start = (back, jnp.zeros((rank, plane_rows), F32))
         (back, reduced), _ = lax.scan(step, start, (down, firsts))
     back = exchanged(back.astype(BF16), PLANE)
-    entering_derivative = back.reshape(groups, inner, rows, outer, piece)
-    entering_derivative = entering_derivative.transpose(2, 3, 1, 0, 4).reshape(rows, width)
+    if aligned:
+        turned = [(to, at, size) for at, to, size in moves]
+        entering_derivative = repacked(back, (rows, width), turned)
+    else:
+        entering_derivative = back.reshape(groups, inner, rows, outer, piece)
+        entering_derivative = entering_derivative.transpose(2, 3, 1, 0, 4).reshape(rows, width)
 
     reduced = reduced.reshape(rank, groups, inner * rows)
     total = lax.dynamic_index_in_dim(reduced, group, 1, keepdims=False)
@@ -204,16 +243,11 @@
     reduced = total.astype(BF16)
     reduced_own = lax.dynamic_slice_in_dim(reduced, place * rows, rows, 1)
 
-    hit = row_job_labels[None, None, :] == up_order[:, None, None]
-    wide = jnp.where(hit, reduced_own[None], jnp.zeros((), BF16)).reshape(jobs * rank, rows)
+    wide = spread(reduced_own, row_job_labels, 0, jobs)
     projected = (frozen + ADAPTER_SCALE * dot(wide, up_all, 0, 0)).astype(BF16)
 
-    upstream_group = lax.dynamic_index_in_dim(
-        upstream_plane.reshape(groups, inner * rows, out_width), group, 0, keepdims=False
-    )
-    labels_group = lax.dynamic_index_in_dim(
-        labels_plane.reshape(groups, inner * rows), group, 0, keepdims=False
-    )
+    upstream_group = lax.dynamic_slice_in_dim(upstream_plane, group * half, half, 0)
+    labels_group = lax.dynamic_slice_in_dim(labels_plane, group * half, half, 0)
     wanted = jnp.arange(outer, dtype=jnp.int32) * inner + place
     hit = labels_group[None, None, :] == wanted[:, None, None]
     wide = jnp.where(hit, reduced[None], jnp.zeros((), BF16)).reshape(outer * rank, -1)

time: 325 us -> 253 us (0.78)
  local copies, waits for them, and re-layouts: 63.3 us -> 21.4 us
  waiting for transfers between devices: 117 us -> 80.6 us
  starting transfers between devices: 92.4 us -> 74.5 us
  between operations: 1.63 us -> 14.9 us
  matrix products: 26 us -> 37.9 us
  other arithmetic: 23.2 us -> 19.1 us
    all_to_all x6 -> x4, waiting for transfers between devices: 33.8 us -> 3.44 us  [exchanged(): return lax.all_to_all(array, axes, split_axis=0, concat_axis=0, tiled=True)]
    ppermute x6, waiting for transfers between devices: 2.13 us -> 28.9 us  [line_gather(): falling.append(lax.ppermute(falling[-1], axis, downward))]
    reshape x7 -> x1, local copies, waits for them, and re-layouts: 24 us -> 0.03 us  [per_device(): packet = packet.transpose(1, 0, 2).reshape(rank + 16, plane_rows)]
    ppermute x13 -> x7, waiting for transfers between devices: 36.4 us -> 13.7 us  [swapped(): return lax.ppermute(array, axis, [(i, i ^ bit) for i in range(peers)])]
    all_to_all x4 -> x1, local copies, waits for them, and re-layouts: 13 us -> 0.88 us  [exchanged(): return lax.all_to_all(array, axes, split_axis=0, concat_axis=0, tiled=True)]
    dot_general x9 -> x15, matrix products: 26 us -> 37.9 us  [dot(): lax.dot_general(left, right, (((left_dim,), (right_dim,)), ((), ())), pre...]
    ppermute x13 -> x11, waiting for transfers between devices: 44.4 us -> 34.3 us  [shifted(): lax.ppermute(array, axis, [(i, (i + by) % peers) for i in range(peers)])]
    all_to_all x6 -> x4, starting transfers between devices: 23.9 us -> 15.3 us  [exchanged(): return lax.all_to_all(array, axes, split_axis=0, concat_axis=0, tiled=True)]
  transfers between devices with their start and end apart: 44 -> 36, of which waited for: 15 -> 16; matrix products, arithmetic and copies ran while one was open for 32% -> 28% of each run, Pallas kernels for 0% -> 1%
where the time goes in v2:
time: 253 us; the launch traced here: 252 us
  waiting for transfers between devices  80.6 us (32%)
  starting transfers between devices  74.5 us (29%)
  matrix products  37.9 us (15%)
  local copies, waits for them, and re-layouts  21.4 us (8%)
  other arithmetic  19.1 us (8%)
  between operations  14.9 us (6%)
  Pallas kernels  3.19 us (1%)
    dot_general x15, matrix products, dot(): lax.dot_general(left, right, (((left_dim,), (right_dim,)), ((), ())), pre...  37.9 us
    ppermute x11, waiting for transfers between devices, shifted(): lax.ppermute(array, axis, [(i, (i + by) % peers) for i in range(peers)])  34.3 us
    ppermute x6, starting transfers between devices, line_gather(): rising.append(lax.ppermute(rising[-1], axis, upward))  30.5 us
    ppermute x6, waiting for transfers between devices, line_gather(): falling.append(lax.ppermute(falling[-1], axis, downward))  28.9 us
    all_to_all x4, starting transfers between devices, exchanged(): return lax.all_to_all(array, axes, split_axis=0, concat_axis=0, tiled=True)  15.3 us
    ppermute x11, starting transfers between devices, shifted(): lax.ppermute(array, axis, [(i, (i + by) % peers) for i in range(peers)])  15.2 us
    ppermute x7, waiting for transfers between devices, swapped(): return lax.ppermute(array, axis, [(i, i ^ bit) for i in range(peers)])  13.7 us
    dynamic_update_slice x6, other arithmetic, line_gather(): stack = lax.dynamic_update_index_in_dim(stack, block, (me - by) % peers, 0)  11.2 us
  transfers between devices with their start and end apart: 36, of which 16 were waited for; matrix products, arithmetic and copies ran while one was open for 28% of the time, Pallas kernels for 1%

profile of v2, /device:TPU:0, one launch (start us, length us, event | category | flops | bytes accessed | tf_op | source)
XLA Modules:
  0.0 251.5 jit_solution(15899418140169984948)
XLA Ops:
  7.2 1.6 copy-done
  8.8 1.6 shard_map.93
  10.7 2.0 bitcast_dynamic-update-slice_fusion.7
  14.8 1.3 constant_dynamic-slice_fusion.6
  17.6 4.2 %all-to-all-start.1 = ((bf16[4,64,1024]{2,1,0:T(8,128)(2,1)}), bf16[4,64,1024]{2,1,0:T(8,128)(2,1)S(1)}, u32[]{:S(2)}, u32[]{:S(2)}) async-start(bf16[4,64,1024]{2,1,0:T(8,128)(2,1)} %bitcast.83), calls=%async_computation.1 | async-start | bytes 1048576 | tf_op jit(solution)/shard_map/all_to_all | solution.py:81
  21.8 5.6 %collective-permute-start = (bf16[256,1024]{1,0:T(8,128)(2,1)}, bf16[256,1024]{1,0:T(8,128)(2,1)}, u32[]{:S(2)}, u32[]{:S(2)}) collective-permute-start(bf16[256,1024]{1,0:T(8,128)(2,1)} %get-tuple-element.15), channel_id=1, source_target_pairs={{0,4},{4,8},{8,12},{1,5},{5,9},{9,13},{2,6},{6,10},{10,14},{3,7},{... | collective-permute-start | bytes 1572872 | tf_op jit(solution)/shard_map/ppermute | solution.py:53
  27.4 3.4 %all-to-all-done.1 = bf16[4,64,1024]{2,1,0:T(8,128)(2,1)S(1)} async-done(((bf16[4,64,1024]{2,1,0:T(8,128)(2,1)}), bf16[4,64,1024]{2,1,0:T(8,128)(2,1)S(1)}, u32[]{:S(2)}, u32[]{:S(2)}) %all-to-all-start.1) | async-done | bytes 524320 | tf_op jit(solution)/shard_map/all_to_all | solution.py:81
  30.9 1.3 collective-permute-start.13
  32.1 1.5 collective-permute-done.1
  33.7 1.3 collective-permute-start.2
  35.0 4.2 %all-to-all-start = ((bf16[8,128,1024]{2,1,0:T(8,128)(2,1)}), bf16[8,128,1024]{2,1,0:T(8,128)(2,1)S(1)}, u32[]{:S(2)}, u32[]{:S(2)}) async-start(bf16[8,128,1024]{2,1,0:T(8,128)(2,1)} %bitcast), calls=%async_computation | async-start | bytes 4194304 | tf_op jit(solution)/shard_map/all_to_all | solution.py:81
  39.2 5.4 %collective-permute-start.12 = (bf16[256,1024]{1,0:T(8,128)(2,1)S(1)}, bf16[256,1024]{1,0:T(8,128)(2,1)}, u32[]{:S(2)}, u32[]{:S(2)}) collective-permute-start(bf16[256,1024]{1,0:T(8,128)(2,1)S(1)} %bitcast.201), channel_id=1, source_target_pairs={{0,4},{4,8},{8,12},{1,5},{5,9},{9,13},{2,6},{6,10},{10,14},{3,7},{... | collective-permute-start | bytes 1572872 | tf_op jit(solution)/shard_map/ppermute | solution.py:53
  44.6 3.6 %collective-permute-start.4 = (bf16[256,1024]{1,0:T(8,128)(2,1)}, bf16[256,1024]{1,0:T(8,128)(2,1)}, u32[]{:S(2)}, u32[]{:S(2)}) collective-permute-start(bf16[256,1024]{1,0:T(8,128)(2,1)} %collective-permute-done), channel_id=1, source_target_pairs={{0,4},{4,8},{8,12},{1,5},{5,9},{9,13},{2,6},{6,10},{10,14},{3,7},{... | collective-permute-start | bytes 1572872 | tf_op jit(solution)/shard_map/ppermute | solution.py:53
  48.1 5.0 %collective-permute-done.13 = bf16[256,1024]{1,0:T(8,128)(2,1)S(1)} collective-permute-done((bf16[256,1024]{1,0:T(8,128)(2,1)S(1)}, bf16[256,1024]{1,0:T(8,128)(2,1)S(1)}, u32[]{:S(2)}, u32[]{:S(2)}) %collective-permute-start.13) | collective-permute-done | bytes 524320 | tf_op jit(solution)/shard_map/ppermute | solution.py:54
  53.1 1.3 collective-permute-start.14
  54.4 10.8 %collective-permute-done.2 = bf16[256,1024]{1,0:T(8,128)(2,1)} collective-permute-done((bf16[256,1024]{1,0:T(8,128)(2,1)}, bf16[256,1024]{1,0:T(8,128)(2,1)}, u32[]{:S(2)}, u32[]{:S(2)}) %collective-permute-start.2) | collective-permute-done | bytes 524320 | tf_op jit(solution)/shard_map/ppermute | solution.py:54
  65.1 1.3 collective-permute-start.3
  66.6 6.6 %collective-permute-start.16 = (bf16[256,1024]{1,0:T(8,128)(2,1)}, bf16[256,1024]{1,0:T(8,128)(2,1)}, u32[]{:S(2)}, u32[]{:S(2)}) collective-permute-start(bf16[256,1024]{1,0:T(8,128)(2,1)} %collective-permute-done.12), channel_id=1, source_target_pairs={{0,4},{4,8},{8,12},{1,5},{5,9},{9,13},{2,6},{6,10},{10,14},{3,7},{... | collective-permute-start | bytes 1572872 | tf_op jit(solution)/shard_map/ppermute | solution.py:53
  73.2 4.3 %collective-permute-start.5 = (bf16[256,1024]{1,0:T(8,128)(2,1)}, bf16[256,1024]{1,0:T(8,128)(2,1)S(1)}, u32[]{:S(2)}, u32[]{:S(2)}) collective-permute-start(bf16[256,1024]{1,0:T(8,128)(2,1)} %collective-permute-done.4), channel_id=1, source_target_pairs={{0,4},{4,8},{8,12},{1,5},{5,9},{9,13},{2,6},{6,10},{10,14},{3,7},{... | collective-permute-start | bytes 1572872 | tf_op jit(solution)/shard_map/ppermute | solution.py:53
  77.5 1.7 collective-permute-done.14
  80.5 9.9 %collective-permute-done.3 = bf16[256,1024]{1,0:T(8,128)(2,1)} collective-permute-done((bf16[256,1024]{1,0:T(8,128)(2,1)}, bf16[256,1024]{1,0:T(8,128)(2,1)}, u32[]{:S(2)}, u32[]{:S(2)}) %collective-permute-start.3) | collective-permute-done | bytes 524320 | tf_op jit(solution)/shard_map/ppermute | solution.py:54
  90.4 2.0 bitcast_dynamic-update-slice_fusion.6
  92.5 2.0 bitcast_dynamic-update-slice_fusion.5
  94.7 2.0 bitcast_dynamic-update-slice_fusion.4
  96.7 4.7 %fusion.42 = f32[2,2,2,128,1024]{4,3,2,1,0:T(8,128)S(1)} fusion(bf16[2,2,2,128,1024]{4,3,2,1,0:T(8,128)(2,1)S(1)} %bitcast.176, bf16[1024,1024,1,1,1]{1,0,4,3,2:T(8,128)(2,1)} %bitcast.195), kind=kOutput, calls=%fused_computation.121 | convolution fusion | flops 2147483648 | bytes 8388608 | tf_op jit(solution)/shard_map/dot_general | solution.py:85
  101.4 2.0 copy-done.5
  104.6 1.7 broadcast.237.clone.1
  107.1 5.1 %collective-permute-start.17 = (bf16[256,1024]{1,0:T(8,128)(2,1)}, bf16[256,1024]{1,0:T(8,128)(2,1)}, u32[]{:S(2)}, u32[]{:S(2)}) collective-permute-start(bf16[256,1024]{1,0:T(8,128)(2,1)} %collective-permute-done.16), channel_id=1, source_target_pairs={{0,4},{4,8},{8,12},{1,5},{5,9},{9,13},{2,6},{6,10},{10,14},{3,7},{... | collective-permute-start | bytes 1572872 | tf_op jit(solution)/shard_map/ppermute | solution.py:53
  113.4 2.0 collective-permute-start.22
  116.4 2.1 bitcast_dynamic-update-slice_fusion.2
  118.5 2.1 bitcast_dynamic-update-slice_fusion.1
  120.6 2.9 %bitcast_add_fusion = f32[2,2,128,1024]{3,2,1,0:T(8,128)} fusion(bf16[2,2,128,1024]{3,2,1,0:T(8,128)(2,1)} %collective-permute-done.6, f32[2,2,2,128,1024]{4,3,2,1,0:T(8,128)S(1)} %copy-done.6, s32[]{:T(128)S(6)} %select_n.317), kind=kLoop, calls=%fused_computation.6 | loop fusion | flops 1048576 | bytes 5242884 | tf_op jit(solution)/shard_map/add | solution.py:200
  123.5 2.4 fusion.8
  126.1 1.6 collective-permute-start.9
  127.8 2.1 collective-permute-done.9
  129.9 1.6 collective-permute-start.7
  133.1 10.2 %collective-permute-done.10 = bf16[2,80,128]{2,1,0:T(8,128)(2,1)S(1)} collective-permute-done((bf16[2,80,128]{2,1,0:T(8,128)(2,1)S(1)}, bf16[2,80,128]{2,1,0:T(8,128)(2,1)S(1)}, u32[]{:S(2)}, u32[]{:S(2)}) %collective-permute-start.10) | collective-permute-done | bytes 40992 | tf_op jit(solution)/shard_map/ppermute | solution.py:19
  144.8 4.0 %select_reduce_fusion = f32[64,1024]{1,0:T(8,128)S(1)} fusion(pred[16,1024]{1,0:T(8,128)(4,1)S(1)} %iota_compare_fusion, bf16[16,64,1024]{2,1,0:T(8,128)(2,1)} %bitcast.36, bf16[1024,1024,1]{1,0,2:T(8,128)(2,1)S(1)} %bitcast.178), kind=kOutput, calls=%fused_computation.1 | convolution fusion | flops 2149515264 | bytes 4472832 | tf_op jit(solution)/shard_map/dot_general | solution.py:85
  149.9 1.6 collective-permute-start.18
  151.5 2.2 collective-permute-start.25
  153.9 6.2 %fusion.43 = f32[1024,1024]{1,0:T(8,128)} fusion(bf16[1024,1024]{1,0:T(8,128)(2,1)S(1)} %bitcast.199, bf16[1024,1024]{1,0:T(8,128)(2,1)} %bitcast.42), kind=kOutput, calls=%fused_computation.122 | convolution fusion | flops 2147483648 | bytes 8388608 | tf_op jit(solution)/shard_map/dot_general | solution.py:85
  160.0 6.5 %add_convert_fusion = bf16[1024,1024]{1,0:T(8,128)(2,1)} fusion(f32[1024,1024]{1,0:T(8,128)} %fusion.43, bf16[1024,1024]{1,0:T(8,128)(2,1)} %all-gather.4.cloned.1.call-done, bf16[1024,1024]{1,0:T(8,128)(2,1)S(1)} %bitcast.196), kind=kOutput, calls=%fused_computation | convolution fusion | flops 2149580800 | bytes 10485760 | tf_op jit(solution)/shard_map/dot_general | solution.py:85
  166.5 3.6 %all-to-all-start.2 = ((bf16[8,128,1024]{2,1,0:T(8,128)(2,1)}), bf16[8,128,1024]{2,1,0:T(8,128)(2,1)S(1)}, u32[]{:S(2)}, u32[]{:S(2)}) async-start(bf16[8,128,1024]{2,1,0:T(8,128)(2,1)} %bitcast.197), calls=%async_computation.2 | async-start | bytes 4194304 | tf_op jit(solution)/shard_map/all_to_all | solution.py:81
  170.3 1.4 fusion.29
  171.7 1.4 fusion.23
  173.5 1.8 collective-permute-start.23
  177.1 5.2 %collective-permute-done.21 = bf16[80,1024]{1,0:T(8,128)(2,1)S(1)} collective-permute-done((bf16[80,1024]{1,0:T(8,128)(2,1)S(1)}, bf16[80,1024]{1,0:T(8,128)(2,1)S(1)}, u32[]{:S(2)}, u32[]{:S(2)}) %collective-permute-start.21) | collective-permute-done | bytes 163872 | tf_op jit(solution)/shard_map/ppermute | solution.py:24
  182.3 2.0 collective-permute-start.19
  184.3 3.7 %collective-permute-done.23 = bf16[80,1024]{1,0:T(8,128)(2,1)S(1)} collective-permute-done((bf16[80,1024]{1,0:T(8,128)(2,1)S(1)}, bf16[80,1024]{1,0:T(8,128)(2,1)S(1)}, u32[]{:S(2)}, u32[]{:S(2)}) %collective-permute-start.23) | collective-permute-done | bytes 163872 | tf_op jit(solution)/shard_map/ppermute | solution.py:24
  188.2 1.4 fusion.19
  189.6 1.4 fusion.25
  191.0 1.4 convolution_add_fusion.1
  192.6 1.4 convolution_add_fusion.3
  193.9 1.4 fusion.7
  195.3 1.4 fusion.6
  197.8 3.2 %all-to-all-start.3 = ((bf16[32,64,256]{2,1,0:T(8,128)(2,1)}), bf16[32,64,256]{2,1,0:T(8,128)(2,1)S(1)}, u32[]{:S(2)}, u32[]{:S(2)}) async-start(bf16[32,64,256]{2,1,0:T(8,128)(2,1)} %bitcast.186), calls=%async_computation.3 | async-start | bytes 2097152 | tf_op jit(solution)/shard_map/all_to_all | solution.py:81
  202.1 1.8 collective-permute-start.8
  205.5 1.8 convolution_multiply_fusion
  207.5 3.4 %collective-permute-start.29 = (bf16[64,1024]{1,0:T(8,128)(2,1)S(1)}, bf16[64,1024]{1,0:T(8,128)(2,1)S(1)}, u32[]{:S(2)}, u32[]{:S(2)}) collective-permute-start(bf16[64,1024]{1,0:T(8,128)(2,1)S(1)} %get-tuple-element.20), channel_id=1, source_target_pairs={{0,12},{4,0},{8,4},{12,8},{1,13},{5,1},{9,5},{13,9},{2,14},{6,2},{... | collective-permute-start | bytes 393224 | tf_op jit(solution)/shard_map/ppermute | solution.py:24
  212.0 6.0 %collective-permute-done.8 = bf16[128,1024]{1,0:T(8,128)(2,1)S(1)} collective-permute-done((bf16[128,1024]{1,0:T(8,128)(2,1)S(1)}, bf16[128,1024]{1,0:T(8,128)(2,1)S(1)}, u32[]{:S(2)}, u32[]{:S(2)}) %collective-permute-start.8) | collective-permute-done | bytes 262176 | tf_op jit(solution)/shard_map/ppermute | solution.py:24
  219.1 2.8 %collective-permute-done.29 = bf16[64,1024]{1,0:T(8,128)(2,1)S(1)} collective-permute-done((bf16[64,1024]{1,0:T(8,128)(2,1)S(1)}, bf16[64,1024]{1,0:T(8,128)(2,1)S(1)}, u32[]{:S(2)}, u32[]{:S(2)}) %collective-permute-start.29) | collective-permute-done | bytes 131104 | tf_op jit(solution)/shard_map/ppermute | solution.py:24
  222.0 16.6 %collective-permute-done.28 = bf16[64,1024]{1,0:T(8,128)(2,1)S(1)} collective-permute-done((bf16[64,1024]{1,0:T(8,128)(2,1)S(1)}, bf16[64,1024]{1,0:T(8,128)(2,1)S(1)}, u32[]{:S(2)}, u32[]{:S(2)}) %collective-permute-start.28) | collective-permute-done | bytes 131104 | tf_op jit(solution)/shard_map/ppermute | solution.py:24
  239.3 1.6 shard_map.94
  242.0 2.7 %reshape.484 = f32[64,8192]{1,0:T(8,128)} reshape(f32[64,4,4,2,256]{4,3,2,1,0:T(2,128)S(1)} %bitcast.181) | data formatting | bytes 4194304 | tf_op jit(solution)/shard_map/broadcast_in_dim | solution.py:260
  (131 shorter events, 24.6 us)
Async XLA Ops:
  7.2 116.4 %all-gather.6.cloned.1.call-start = ((), (), s32[]{:S(2)}) async-start(), calls=%async_computation.5 | async-start | bytes 2228224 | tf_op jit(solution)/shard_map/all_gather | solution.py:150
  7.2 1.6 copy-start
  10.4 3.6 %copy-start.9 = (bf16[1,8192,64]{1,2,0:T(8,128)(2,1)S(1)}, bf16[1,8192,64]{1,2,0:T(8,128)(2,1)}, u32[]{:S(2)}) copy-start(bf16[1,8192,64]{1,2,0:T(8,128)(2,1)} %param.10) | copy-start | bytes 3145732
  12.7 1.3 copy-start.7
  12.7 21.0 %collective-permute-start.1 = (bf16[256,1024]{1,0:T(8,128)(2,1)}, bf16[256,1024]{1,0:T(8,128)(2,1)}, u32[]{:S(2)}, u32[]{:S(2)}) collective-permute-start(bf16[256,1024]{1,0:T(8,128)(2,1)} %get-tuple-element.15), channel_id=1, source_target_pairs={{4,0},{8,4},{12,8},{5,1},{9,5},{13,9},{6,2},{10,6},{14,10},{7,3},{... | collective-permute-start | bytes 1572872 | tf_op jit(solution)/shard_map/ppermute | solution.py:54
  17.6 13.3 %all-to-all-start.1 = ((bf16[4,64,1024]{2,1,0:T(8,128)(2,1)}), bf16[4,64,1024]{2,1,0:T(8,128)(2,1)S(1)}, u32[]{:S(2)}, u32[]{:S(2)}) async-start(bf16[4,64,1024]{2,1,0:T(8,128)(2,1)} %bitcast.83), calls=%async_computation.1 | async-start | bytes 1048576 | tf_op jit(solution)/shard_map/all_to_all | solution.py:81
  21.8 22.8 %collective-permute-start = (bf16[256,1024]{1,0:T(8,128)(2,1)}, bf16[256,1024]{1,0:T(8,128)(2,1)}, u32[]{:S(2)}, u32[]{:S(2)}) collective-permute-start(bf16[256,1024]{1,0:T(8,128)(2,1)} %get-tuple-element.15), channel_id=1, source_target_pairs={{0,4},{4,8},{8,12},{1,5},{5,9},{9,13},{2,6},{6,10},{10,14},{3,7},{... | collective-permute-start | bytes 1572872 | tf_op jit(solution)/shard_map/ppermute | solution.py:53
  30.9 22.2 %collective-permute-start.13 = (bf16[256,1024]{1,0:T(8,128)(2,1)S(1)}, bf16[256,1024]{1,0:T(8,128)(2,1)S(1)}, u32[]{:S(2)}, u32[]{:S(2)}) collective-permute-start(bf16[256,1024]{1,0:T(8,128)(2,1)S(1)} %bitcast.200), channel_id=1, source_target_pairs={{4,0},{8,4},{12,8},{5,1},{9,5},{13,9},{6,2},{10,6},{14,10},{7,3},{... | collective-permute-start | bytes 1572872 | tf_op jit(solution)/shard_map/ppermute | solution.py:54
  33.7 31.5 %collective-permute-start.2 = (bf16[256,1024]{1,0:T(8,128)(2,1)}, bf16[256,1024]{1,0:T(8,128)(2,1)}, u32[]{:S(2)}, u32[]{:S(2)}) collective-permute-start(bf16[256,1024]{1,0:T(8,128)(2,1)} %collective-permute-done.1), channel_id=1, source_target_pairs={{4,0},{8,4},{12,8},{5,1},{9,5},{13,9},{6,2},{10,6},{14,10},{7,3},{... | collective-permute-start | bytes 1572872 | tf_op jit(solution)/shard_map/ppermute | solution.py:54
  35.0 61.7 %all-to-all-start = ((bf16[8,128,1024]{2,1,0:T(8,128)(2,1)}), bf16[8,128,1024]{2,1,0:T(8,128)(2,1)S(1)}, u32[]{:S(2)}, u32[]{:S(2)}) async-start(bf16[8,128,1024]{2,1,0:T(8,128)(2,1)} %bitcast), calls=%async_computation | async-start | bytes 4194304 | tf_op jit(solution)/shard_map/all_to_all | solution.py:81
  39.2 120.8 %all-gather.4.cloned.1.call-start = ((), (), s32[]{:S(2)}) async-start(), calls=%async_computation.4 | async-start | bytes 2359296 | tf_op jit(solution)/shard_map/all_gather | solution.py:151
  39.2 27.3 %collective-permute-start.12 = (bf16[256,1024]{1,0:T(8,128)(2,1)S(1)}, bf16[256,1024]{1,0:T(8,128)(2,1)}, u32[]{:S(2)}, u32[]{:S(2)}) collective-permute-start(bf16[256,1024]{1,0:T(8,128)(2,1)S(1)} %bitcast.201), channel_id=1, source_target_pairs={{0,4},{4,8},{8,12},{1,5},{5,9},{9,13},{2,6},{6,10},{10,14},{3,7},{... | collective-permute-start | bytes 1572872 | tf_op jit(solution)/shard_map/ppermute | solution.py:53
  44.6 28.6 %collective-permute-start.4 = (bf16[256,1024]{1,0:T(8,128)(2,1)}, bf16[256,1024]{1,0:T(8,128)(2,1)}, u32[]{:S(2)}, u32[]{:S(2)}) collective-permute-start(bf16[256,1024]{1,0:T(8,128)(2,1)} %collective-permute-done), channel_id=1, source_target_pairs={{0,4},{4,8},{8,12},{1,5},{5,9},{9,13},{2,6},{6,10},{10,14},{3,7},{... | collective-permute-start | bytes 1572872 | tf_op jit(solution)/shard_map/ppermute | solution.py:53
  53.1 43.6 %copy-start.11 = (bf16[256,1024]{1,0:T(8,128)(2,1)}, bf16[256,1024]{1,0:T(8,128)(2,1)S(1)}, u32[]{:S(2)}) copy-start(bf16[256,1024]{1,0:T(8,128)(2,1)S(1)} %collective-permute-done.13) | copy-start | bytes 1572868
  53.1 26.1 %collective-permute-start.14 = (bf16[256,1024]{1,0:T(8,128)(2,1)S(1)}, bf16[256,1024]{1,0:T(8,128)(2,1)}, u32[]{:S(2)}, u32[]{:S(2)}) collective-permute-start(bf16[256,1024]{1,0:T(8,128)(2,1)S(1)} %collective-permute-done.13), channel_id=1, source_target_pairs={{4,0},{8,4},{12,8},{5,1},{9,5},{13,9},{6,2},{10,6},{14,10},{7,3},{... | collective-permute-start | bytes 1572872 | tf_op jit(solution)/shard_map/ppermute | solution.py:54
  65.1 25.3 %collective-permute-start.3 = (bf16[256,1024]{1,0:T(8,128)(2,1)}, bf16[256,1024]{1,0:T(8,128)(2,1)}, u32[]{:S(2)}, u32[]{:S(2)}) collective-permute-start(bf16[256,1024]{1,0:T(8,128)(2,1)} %collective-permute-done.2), channel_id=1, source_target_pairs={{4,0},{8,4},{12,8},{5,1},{9,5},{13,9},{6,2},{10,6},{14,10},{7,3},{... | collective-permute-start | bytes 1572872 | tf_op jit(solution)/shard_map/ppermute | solution.py:54
  66.6 40.6 %collective-permute-start.16 = (bf16[256,1024]{1,0:T(8,128)(2,1)}, bf16[256,1024]{1,0:T(8,128)(2,1)}, u32[]{:S(2)}, u32[]{:S(2)}) collective-permute-start(bf16[256,1024]{1,0:T(8,128)(2,1)} %collective-permute-done.12), channel_id=1, source_target_pairs={{0,4},{4,8},{8,12},{1,5},{5,9},{9,13},{2,6},{6,10},{10,14},{3,7},{... | collective-permute-start | bytes 1572872 | tf_op jit(solution)/shard_map/ppermute | solution.py:53
  73.2 21.5 %collective-permute-start.5 = (bf16[256,1024]{1,0:T(8,128)(2,1)}, bf16[256,1024]{1,0:T(8,128)(2,1)S(1)}, u32[]{:S(2)}, u32[]{:S(2)}) collective-permute-start(bf16[256,1024]{1,0:T(8,128)(2,1)} %collective-permute-done.4), channel_id=1, source_target_pairs={{0,4},{4,8},{8,12},{1,5},{5,9},{9,13},{2,6},{6,10},{10,14},{3,7},{... | collective-permute-start | bytes 1572872 | tf_op jit(solution)/shard_map/ppermute | solution.py:53
  79.2 36.2 %collective-permute-start.15 = (bf16[256,1024]{1,0:T(8,128)(2,1)}, bf16[256,1024]{1,0:T(8,128)(2,1)}, u32[]{:S(2)}, u32[]{:S(2)}) collective-permute-start(bf16[256,1024]{1,0:T(8,128)(2,1)} %collective-permute-done.14), channel_id=1, source_target_pairs={{4,0},{8,4},{12,8},{5,1},{9,5},{13,9},{6,2},{10,6},{14,10},{7,3},{... | collective-permute-start | bytes 1572872 | tf_op jit(solution)/shard_map/ppermute | solution.py:54
  96.7 48.1 %copy-start.1 = (bf16[8,128,1024]{2,1,0:T(8,128)(2,1)}, bf16[8,128,1024]{2,1,0:T(8,128)(2,1)S(1)}, u32[]{:S(2)}) copy-start(bf16[8,128,1024]{2,1,0:T(8,128)(2,1)S(1)} %all-to-all-done) | copy-start | bytes 6291460
  101.4 2.0 copy-start.5
  103.4 1.1 copy-start.13
  104.5 16.1 %collective-permute-start.6 = (bf16[2,2,128,1024]{3,2,1,0:T(8,128)(2,1)}, bf16[2,2,128,1024]{3,2,1,0:T(8,128)(2,1)}, u32[]{:S(2)}, u32[]{:S(2)}) collective-permute-start(bf16[2,2,128,1024]{3,2,1,0:T(8,128)(2,1)} %fusion.14), channel_id=1, source_target_pairs={{0,1},{1,0},{2,3},{3,2},{4,5},{5,4},{6,7},{7,6},{8,9},{9,8},{10,11... | collective-permute-start | bytes 3145736 | tf_op jit(solution)/shard_map/ppermute | solution.py:19
  107.1 24.4 %collective-permute-start.17 = (bf16[256,1024]{1,0:T(8,128)(2,1)}, bf16[256,1024]{1,0:T(8,128)(2,1)}, u32[]{:S(2)}, u32[]{:S(2)}) collective-permute-start(bf16[256,1024]{1,0:T(8,128)(2,1)} %collective-permute-done.16), channel_id=1, source_target_pairs={{0,4},{4,8},{8,12},{1,5},{5,9},{9,13},{2,6},{6,10},{10,14},{3,7},{... | collective-permute-start | bytes 1572872 | tf_op jit(solution)/shard_map/ppermute | solution.py:53
  112.2 8.4 %copy-start.6 = (f32[2,2,2,128,1024]{4,3,2,1,0:T(8,128)S(1)}, f32[2,2,2,128,1024]{4,3,2,1,0:T(8,128)}, u32[]{:S(2)}) copy-start(f32[2,2,2,128,1024]{4,3,2,1,0:T(8,128)} %copy-done.5) | copy-start | bytes 12582916
  113.4 74.8 %collective-permute-start.26 = (bf16[1024,256]{1,0:T(8,128)(2,1)}, bf16[1024,256]{1,0:T(8,128)(2,1)}, u32[]{:S(2)}, u32[]{:S(2)}) collective-permute-start(bf16[1024,256]{1,0:T(8,128)(2,1)} %get-tuple-element.18), channel_id=1, source_target_pairs={{0,12},{4,0},{8,4},{12,8},{1,13},{5,1},{9,5},{13,9},{2,14},{6,2},{... | collective-permute-start | bytes 1572872 | tf_op jit(solution)/shard_map/ppermute | solution.py:24
  113.4 77.6 %collective-permute-start.22 = (bf16[1024,256]{1,0:T(8,128)(2,1)}, bf16[1024,256]{1,0:T(8,128)(2,1)}, u32[]{:S(2)}, u32[]{:S(2)}) collective-permute-start(bf16[1024,256]{1,0:T(8,128)(2,1)} %get-tuple-element.17), channel_id=1, source_target_pairs={{0,4},{4,8},{8,12},{12,0},{1,5},{5,9},{9,13},{13,1},{2,6},{6,10},{... | collective-permute-start | bytes 1572872 | tf_op jit(solution)/shard_map/ppermute | solution.py:24
  115.4 78.5 %collective-permute-start.24 = (bf16[1024,256]{1,0:T(8,128)(2,1)S(1)}, bf16[1024,256]{1,0:T(8,128)(2,1)}, u32[]{:S(2)}, u32[]{:S(2)}) collective-permute-start(bf16[1024,256]{1,0:T(8,128)(2,1)S(1)} %get-tuple-element.16), channel_id=1, source_target_pairs={{0,8},{4,12},{8,0},{12,4},{1,9},{5,13},{9,1},{13,5},{2,10},{6,14},... | collective-permute-start | bytes 1572872 | tf_op jit(solution)/shard_map/ppermute | solution.py:24
  120.6 2.9 %copy-start.10 = (bf16[128,1024]{1,0:T(8,128)(2,1)S(1)}, bf16[128,1024]{1,0:T(8,128)(2,1)}, u32[]{:S(2)}) copy-start(bf16[128,1024]{1,0:T(8,128)(2,1)} %param.7) | copy-start | bytes 786436
  123.5 4.2 %copy-start.3 = (f32[2,2,128,1024]{3,2,1,0:T(8,128)S(1)}, f32[2,2,128,1024]{3,2,1,0:T(8,128)}, u32[]{:S(2)}) copy-start(f32[2,2,128,1024]{3,2,1,0:T(8,128)} %bitcast_add_fusion) | copy-start | bytes 6291460
  123.5 8.5 %copy-start.12 = (bf16[256,1024]{1,0:T(8,128)(2,1)S(1)}, bf16[256,1024]{1,0:T(8,128)(2,1)}, u32[]{:S(2)}) copy-start(bf16[256,1024]{1,0:T(8,128)(2,1)} %copy-done.11) | copy-start | bytes 1572868
  126.1 3.8 %collective-permute-start.9 = (bf16[1,80,128]{2,1,0:T(8,128)(2,1)S(1)}, bf16[1,80,128]{2,1,0:T(8,128)(2,1)S(1)}, u32[]{:S(2)}, u32[]{:S(2)}) collective-permute-start(bf16[1,80,128]{2,1,0:T(8,128)(2,1)S(1)} %maximum_bitcast_fusion.1), channel_id=1, source_target_pairs={{0,16},{16,0},{1,17},{17,1},{2,18},{18,2},{3,19},{19,3},{4,20},{20... | collective-permute-start | bytes 61448 | tf_op jit(solution)/shard_map/ppermute | solution.py:19
  129.9 13.5 %collective-permute-start.7 = (bf16[2,1,128,1024]{3,2,1,0:T(8,128)(2,1)S(1)}, bf16[2,1,128,1024]{3,2,1,0:T(8,128)(2,1)S(1)}, u32[]{:S(2)}, u32[]{:S(2)}) collective-permute-start(bf16[2,1,128,1024]{3,2,1,0:T(8,128)(2,1)S(1)} %dynamic-slice_convert_fusion.1), channel_id=1, source_target_pairs={{0,2},{1,3},{2,0},{3,1},{4,6},{5,7},{6,4},{7,5},{8,10},{9,11},{10,... | collective-permute-start | bytes 1572872 | tf_op jit(solution)/shard_map/ppermute | solution.py:19
  131.5 11.7 %collective-permute-start.10 = (bf16[2,80,128]{2,1,0:T(8,128)(2,1)S(1)}, bf16[2,80,128]{2,1,0:T(8,128)(2,1)S(1)}, u32[]{:S(2)}, u32[]{:S(2)}) collective-permute-start(bf16[2,80,128]{2,1,0:T(8,128)(2,1)S(1)} %maximum_bitcast_fusion), channel_id=1, source_target_pairs={{0,2},{1,3},{2,0},{3,1},{4,6},{5,7},{6,4},{7,5},{8,10},{9,11},{10,... | collective-permute-start | bytes 122888 | tf_op jit(solution)/shard_map/ppermute | solution.py:19
  143.3 1.3 collective-permute-start.11
  149.9 23.3 %collective-permute-start.18 = (f32[64,512]{1,0:T(8,128)}, f32[64,512]{1,0:T(8,128)S(1)}, u32[]{:S(2)}, u32[]{:S(2)}) collective-permute-start(f32[64,512]{1,0:T(8,128)} %bitcast.173), channel_id=1, source_target_pairs={{0,16},{16,0},{1,17},{17,1},{2,18},{18,2},{3,19},{19,3},{4,20},{20... | collective-permute-start | bytes 393224 | tf_op jit(solution)/shard_map/ppermute | solution.py:24
  151.5 22.0 %collective-permute-start.25 = (bf16[80,1024]{1,0:T(8,128)(2,1)S(1)}, bf16[80,1024]{1,0:T(8,128)(2,1)}, u32[]{:S(2)}, u32[]{:S(2)}) collective-permute-start(bf16[80,1024]{1,0:T(8,128)(2,1)S(1)} %bitcast.210), channel_id=1, source_target_pairs={{0,12},{4,0},{8,4},{12,8},{1,13},{5,1},{9,5},{13,9},{2,14},{6,2},{... | collective-permute-start | bytes 491528 | tf_op jit(solution)/shard_map/ppermute | solution.py:24
  153.9 6.2 %copy-start.8 = (bf16[4,256,1024]{2,1,0:T(8,128)(2,1)S(1)}, bf16[4,256,1024]{2,1,0:T(8,128)(2,1)}, u32[]{:S(2)}) copy-start(bf16[4,256,1024]{2,1,0:T(8,128)(2,1)} %bitcast_dynamic-update-slice_fusion.4) | copy-start | bytes 6291460
  166.5 31.3 %all-to-all-start.2 = ((bf16[8,128,1024]{2,1,0:T(8,128)(2,1)}), bf16[8,128,1024]{2,1,0:T(8,128)(2,1)S(1)}, u32[]{:S(2)}, u32[]{:S(2)}) async-start(bf16[8,128,1024]{2,1,0:T(8,128)(2,1)} %bitcast.197), calls=%async_computation.2 | async-start | bytes 4194304 | tf_op jit(solution)/shard_map/all_to_all | solution.py:81
  173.1 9.2 %collective-permute-start.21 = (bf16[80,1024]{1,0:T(8,128)(2,1)S(1)}, bf16[80,1024]{1,0:T(8,128)(2,1)S(1)}, u32[]{:S(2)}, u32[]{:S(2)}) collective-permute-start(bf16[80,1024]{1,0:T(8,128)(2,1)S(1)} %bitcast.213), channel_id=1, source_target_pairs={{0,4},{4,8},{8,12},{12,0},{1,5},{5,9},{9,13},{13,1},{2,6},{6,10},{... | collective-permute-start | bytes 491528 | tf_op jit(solution)/shard_map/ppermute | solution.py:24
  173.5 14.5 %collective-permute-start.23 = (bf16[80,1024]{1,0:T(8,128)(2,1)S(1)}, bf16[80,1024]{1,0:T(8,128)(2,1)S(1)}, u32[]{:S(2)}, u32[]{:S(2)}) collective-permute-start(bf16[80,1024]{1,0:T(8,128)(2,1)S(1)} %bitcast.214), channel_id=1, source_target_pairs={{0,8},{4,12},{8,0},{12,4},{1,9},{5,13},{9,1},{13,5},{2,10},{6,14},... | collective-permute-start | bytes 491528 | tf_op jit(solution)/shard_map/ppermute | solution.py:24
  182.3 21.7 %collective-permute-start.19 = (f32[64,512]{1,0:T(8,128)S(1)}, f32[64,512]{1,0:T(8,128)S(1)}, u32[]{:S(2)}, u32[]{:S(2)}) collective-permute-start(f32[64,512]{1,0:T(8,128)S(1)} %bitcast_add_fusion.3), channel_id=1, source_target_pairs={{0,2},{1,3},{2,0},{3,1},{4,6},{5,7},{6,4},{7,5},{8,10},{9,11},{10,... | collective-permute-start | bytes 393224 | tf_op jit(solution)/shard_map/ppermute | solution.py:19
  197.8 43.1 %all-to-all-start.3 = ((bf16[32,64,256]{2,1,0:T(8,128)(2,1)}), bf16[32,64,256]{2,1,0:T(8,128)(2,1)S(1)}, u32[]{:S(2)}, u32[]{:S(2)}) async-start(bf16[32,64,256]{2,1,0:T(8,128)(2,1)} %bitcast.186), calls=%async_computation.3 | async-start | bytes 2097152 | tf_op jit(solution)/shard_map/all_to_all | solution.py:81
  202.1 15.8 %collective-permute-start.8 = (bf16[128,1024]{1,0:T(8,128)(2,1)S(1)}, bf16[128,1024]{1,0:T(8,128)(2,1)S(1)}, u32[]{:S(2)}, u32[]{:S(2)}) collective-permute-start(bf16[128,1024]{1,0:T(8,128)(2,1)S(1)} %fusion.18), channel_id=1, source_target_pairs={{0,16},{16,0},{1,17},{17,1},{2,18},{18,2},{3,19},{19,3},{4,20},{20... | collective-permute-start | bytes 786440 | tf_op jit(solution)/shard_map/ppermute | solution.py:24
  204.1 1.4 collective-permute-start.20
  205.5 12.4 %copy-start.2 = (bf16[1,1024,1024]{2,1,0:T(8,128)(2,1)S(1)}, bf16[1,1024,1024]{2,1,0:T(8,128)(2,1)}, u32[]{:S(2)}) copy-start(bf16[1,1024,1024]{2,1,0:T(8,128)(2,1)} %all-gather.6.cloned.1.call-done) | copy-start | bytes 6291460
  205.5 12.4 %copy-start.4 = (f32[2,1,128,1024]{3,2,1,0:T(8,128)S(1)}, f32[2,1,128,1024]{3,2,1,0:T(8,128)}, u32[]{:S(2)}) copy-start(f32[2,1,128,1024]{3,2,1,0:T(8,128)} %convert_add_fusion) | copy-start | bytes 3145732
  207.5 14.5 %collective-permute-start.29 = (bf16[64,1024]{1,0:T(8,128)(2,1)S(1)}, bf16[64,1024]{1,0:T(8,128)(2,1)S(1)}, u32[]{:S(2)}, u32[]{:S(2)}) collective-permute-start(bf16[64,1024]{1,0:T(8,128)(2,1)S(1)} %get-tuple-element.20), channel_id=1, source_target_pairs={{0,12},{4,0},{8,4},{12,8},{1,13},{5,1},{9,5},{13,9},{2,14},{6,2},{... | collective-permute-start | bytes 393224 | tf_op jit(solution)/shard_map/ppermute | solution.py:24
  210.9 27.6 %collective-permute-start.28 = (bf16[64,1024]{1,0:T(8,128)(2,1)S(1)}, bf16[64,1024]{1,0:T(8,128)(2,1)S(1)}, u32[]{:S(2)}, u32[]{:S(2)}) collective-permute-start(bf16[64,1024]{1,0:T(8,128)(2,1)S(1)} %get-tuple-element.21), channel_id=1, source_target_pairs={{0,8},{4,12},{8,0},{12,4},{1,9},{5,13},{9,1},{13,5},{2,10},{6,14},... | collective-permute-start | bytes 393224 | tf_op jit(solution)/shard_map/ppermute | solution.py:24
  210.9 27.6 %collective-permute-start.27 = (bf16[64,1024]{1,0:T(8,128)(2,1)S(1)}, bf16[64,1024]{1,0:T(8,128)(2,1)S(1)}, u32[]{:S(2)}, u32[]{:S(2)}) collective-permute-start(bf16[64,1024]{1,0:T(8,128)(2,1)S(1)} %get-tuple-element.19), channel_id=1, source_target_pairs={{0,4},{4,8},{8,12},{12,0},{1,5},{5,9},{9,13},{13,1},{2,6},{6,10},{... | collective-permute-start | bytes 393224 | tf_op jit(solution)/shard_map/ppermute | solution.py:24
Sparse Core Ops, SparseCore 0:
  10.5 61.2 all-gather.5
  73.7 28.1 all-gather.3

commit v3 on v2

v3 whole, which is shorter than its diff:
```python
import functools

import jax
import jax.numpy as jnp
import numpy as np
from jax import lax
from jax.experimental import pallas as pl
from jax.experimental.pallas import tpu as pltpu
from jax.sharding import Mesh
from jax.sharding import PartitionSpec as P

ADAPTER_SCALE = 2.0
PLANE = ("groups", "q")
F32 = jnp.float32
BF16 = jnp.bfloat16


def swapped(array, axis, bit):
    peers = lax.axis_size(axis)
    return lax.ppermute(array, axis, [(i, i ^ bit) for i in range(peers)])


def shifted(array, axis, by):
    peers = lax.axis_size(axis)
    return lax.ppermute(array, axis, [(i, (i + by) % peers) for i in range(peers)])


def cube_gather(array, axes):
    stack = array[None]
    for axis in axes:
        bit = lax.axis_size(axis) // 2
        while bit:
            mine = (lax.axis_index(axis) & bit) > 0
            other = swapped(stack, axis, bit)
            pair = jnp.stack(
                [jnp.where(mine, other, stack), jnp.where(mine, stack, other)], axis=1
            )
            stack = pair.reshape((-1,) + array.shape)
            bit //= 2
    return stack


def relative(array, axis):
    return [array] + [shifted(array, axis, by) for by in range(1, lax.axis_size(axis))]


def placed(blocks, axis):
    me = lax.axis_index(axis)
    stack = jnp.zeros((len(blocks),) + blocks[0].shape, blocks[0].dtype)
    for by, block in enumerate(blocks):
        stack = lax.dynamic_update_index_in_dim(stack, block, (me - by) % len(blocks), 0)
    return stack


def repacked(array, shape, moves):
    def kernel(source, target):
        for (r, c), (to_r, to_c), (high, wide) in moves:
            target[pl.ds(to_r, high), pl.ds(to_c, wide)] = source[pl.ds(r, high), pl.ds(c, wide)]

    return pl.pallas_call(
        kernel,
        out_shape=jax.ShapeDtypeStruct(shape, array.dtype),
        in_specs=[pl.BlockSpec(memory_space=pltpu.VMEM)],
        out_specs=pl.BlockSpec(memory_space=pltpu.VMEM),
        compiler_params=pltpu.CompilerParams(vmem_limit_bytes=16 << 20),
        cost_estimate=pl.CostEstimate(
            flops=0, bytes_accessed=2 * array.size * array.dtype.itemsize, transcendentals=0
        ),
    )(array)


def exchanged(array, axes):
    return lax.all_to_all(array, axes, split_axis=0, concat_axis=0, tiled=True)


def dot(left, right, left_dim, right_dim):
    return lax.dot_general(
        left, right, (((left_dim,), (right_dim,)), ((), ())), preferred_element_type=F32
    )


def per_device(
    activations,
    upstream,
    row_job_labels,
    value_projection_weight,
    adapter_down_weight,
    adapter_up_weight,
):
    rows, width = activations.shape
    out_width = upstream.shape[1]
    rank = adapter_down_weight.shape[2]
    groups, outer, inner = (lax.axis_size(a) for a in ("groups", "z", "q"))
    group, level, place = (lax.axis_index(a) for a in ("groups", "z", "q"))
    plane = groups * inner
    jobs = outer * inner
    piece = width // (jobs * groups)
    flat = outer * piece
    plane_rows = plane * rows

    def spread(values, keys, wanted):
        hit = keys[None, None, :] == wanted.astype(np.int32)[:, None, None]
        wide = jnp.where(hit, values[None], jnp.zeros((), values.dtype))
        return wide.reshape(wanted.shape[0] * rank, -1)

    def own_of(wide, keys, wanted):
        hit = keys[None, None, :] == wanted.astype(np.int32)[:, None, None]
        wide = wide.reshape(wanted.shape[0], rank, -1)
        return jnp.sum(jnp.where(hit, wide, 0.0), axis=0)

    aligned = piece % 128 == 0 and rows % 16 == 0
    moves = []
    for g in range(groups):
        for p in range(inner):
            for o in range(outer):
                wide_at = (0, ((o * inner + p) * groups + g) * piece)
                flat_at = ((g * inner + p) * rows, o * piece)
                moves.append((wide_at, flat_at, (rows, piece)))

    if aligned:
        act_send = repacked(activations, (plane_rows, flat), moves)
    else:
        act_send = activations.reshape(rows, outer, inner, groups, piece)
        act_send = act_send.transpose(3, 2, 0, 1, 4).reshape(plane_rows, flat)
    part = value_projection_weight.shape[0] // groups
    weight_half = lax.dynamic_slice_in_dim(value_projection_weight, group * part, part, 0)
    down_send = adapter_down_weight[0].T.reshape(rank, outer, inner, groups, piece)
    down_send = lax.dynamic_index_in_dim(down_send, group, 3, keepdims=False)
    down_send = down_send.transpose(2, 0, 1, 3).reshape(inner, rank, flat)
    down_block = []
    for other in range(inner):
        leaving = lax.dynamic_index_in_dim(down_send, place ^ other, 0, keepdims=False)
        down_block.append(swapped(leaving, "q", other) if other else leaving)
    down_block = jnp.concatenate(down_block, axis=0).reshape(-1, out_width)

    both = jnp.concatenate([weight_half, down_block], axis=0)

    up_own, *up_others = relative(adapter_up_weight[0], "z")
    both, act_send, *up_others = lax.optimization_barrier((both, act_send, *up_others))
    up_all = placed([up_own, *up_others], "z").reshape(1, outer * rank, out_width)
    up_other = swapped(up_all, "q", inner // 2)
    up_jobs = (np.arange(outer)[None, :] * inner + np.arange(inner)[:, None]).reshape(-1)
    act_plane = exchanged(act_send, PLANE)

    shares = {0: (weight_half, down_block)}
    rising, falling = shifted(both, "z", by=1), shifted(both, "z", by=-1)
    act_plane, rising, falling, upstream, up_other = lax.optimization_barrier(
        (act_plane, rising, falling, upstream, up_other)
    )
    for by in range(1, outer // 2):
        if by > 1:
            rising, falling = shifted(rising, "z", by=1), shifted(falling, "z", by=-1)
        shares[by] = rising[:part], rising[part:]
        shares[outer - by] = falling[:part], falling[part:]
    shares[outer // 2] = shifted(rising[:part], "z", by=1), shifted(falling[part:], "z", by=-1)

    bit = inner // 2
    while bit:
        mine = (place & bit) > 0
        other = up_other if bit == inner // 2 else swapped(up_all, "q", bit)
        pair = [jnp.where(mine, other, up_all), jnp.where(mine, up_all, other)]
        up_all = jnp.stack(pair, axis=1).reshape(-1, outer * rank, out_width)
        bit //= 2
    up_all = up_all.reshape(jobs * rank, out_width)

    wide = ADAPTER_SCALE * dot(up_all, upstream, 1, 1)
    scaled = own_of(wide, row_job_labels, up_jobs).astype(BF16)
    label_rows = jnp.broadcast_to(row_job_labels.astype(BF16)[None], (16, rows))
    packet = jnp.concatenate([scaled, label_rows], axis=0)
    act_plane, packet, upstream = lax.optimization_barrier((act_plane, packet, upstream))
    packets = jnp.stack(relative(packet, "z"))

    weight = placed([shares[by][0] for by in range(outer)], "z").reshape(flat, out_width)
    down_all = jnp.concatenate([shares[by][1] for by in range(outer)], axis=0)
    down_all = down_all.reshape(jobs * rank, flat)

    upstream_plane = cube_gather(upstream, PLANE).reshape(plane_rows, out_width)
    packets = cube_gather(packets, PLANE).transpose(1, 2, 0, 3)
    packets = packets.reshape(outer, rank + 16, plane_rows)
    scaled_plane = packets[0, :rank]
    labels_plane = packets[0, rank].astype(jnp.int32)

    blocks = []
    for by in range(outer):
        at = (level + by) % outer * piece
        block = lax.dynamic_slice_in_dim(act_plane, at, piece, 1)
        blocks.append(shifted(block, "z", by) if by else block)

    small = jobs * rank * outer * inner * rows <= 1 << 22
    half = inner * rows

    frozen = dot(act_plane, weight, 1, 0).reshape(groups, inner, rows, out_width)
    pairs = frozen.reshape(groups, inner // 2, 2, rows, out_width)
    kept = lax.dynamic_index_in_dim(pairs, place % 2, 2, keepdims=False)
    leaving = lax.dynamic_index_in_dim(pairs, 1 - place % 2, 2, keepdims=False)
    frozen = kept + swapped(leaving.astype(BF16), "q", 1).astype(F32)

    back = dot(upstream_plane, weight, 1, 1)
    reduced = jnp.zeros((rank, plane_rows), F32)
    turned_labels = labels_plane ^ place

    def step(carry, operands, keys=turned_labels, wanted=np.arange(inner)):
        back, reduced = carry
        block, first = operands
        keys = keys - first
        back = back + dot(spread(scaled_plane, keys, wanted), block, 0, 0)
        reduced = reduced + own_of(dot(block, act_plane, 1, 1), keys, wanted)
        return (back, reduced), None

    if small:
        turn = (level - turned_labels // inner) % outer * inner + turned_labels % inner
        (back, reduced), _ = step((back, reduced), (down_all, 0), turn, np.arange(jobs))
    else:
        firsts = (level - jnp.arange(outer, dtype=jnp.int32)) % outer * inner
        stack = (down_all.reshape(outer, inner * rank, flat), firsts)
        (back, reduced), _ = lax.scan(step, (back, reduced), stack)
    back = back.astype(BF16)

    reduced = reduced.reshape(rank, groups, inner * rows)
    total = lax.dynamic_index_in_dim(reduced, group, 1, keepdims=False)
    for by in range(1, groups):
        leaving = lax.dynamic_index_in_dim(reduced, (group + by) % groups, 1, keepdims=False)
        total = total + shifted(leaving, "groups", by)
    bit = inner // 2
    while bit:
        other = swapped(total, "q", bit)
        if bit == inner // 2:
            *blocks, packets, back, other = lax.optimization_barrier(
                (*blocks, packets, back, other)
            )
        total = total + other
        bit //= 2
    back = exchanged(back, PLANE)
    if aligned:
        turned = [(to, at, size) for at, to, size in moves]
        entering_derivative = repacked(back, (rows, width), turned)
    else:
        entering_derivative = back.reshape(groups, inner, rows, outer, piece)
        entering_derivative = entering_derivative.transpose(2, 3, 1, 0, 4).reshape(rows, width)
    reduced = total.astype(BF16)
    reduced_own = lax.dynamic_slice_in_dim(reduced, place * rows, rows, 1)

    upstream_group = lax.dynamic_slice_in_dim(upstream_plane, group * half, half, 0)
    labels_group = lax.dynamic_slice_in_dim(labels_plane, group * half, half, 0)
    wide = spread(reduced, labels_group - place, np.arange(outer) * inner)
    up_part = (ADAPTER_SCALE * dot(wide, upstream_group, 1, 0)).reshape(outer, rank, out_width)
    up_grad = lax.dynamic_index_in_dim(up_part, level, 0, keepdims=False)
    up_send = up_part.astype(BF16)
    *blocks, up_send = lax.optimization_barrier((*blocks, up_send))
    up_got = []
    for by in range(1, outer):
        leaving = lax.dynamic_index_in_dim(up_send, (level + by) % outer, 0, keepdims=False)
        up_got.append(shifted(leaving, "z", by))

    def down_grad_part(g, first, count):
        total = jnp.zeros((count * rank, piece), F32)
        for packet, block in zip(packets, blocks):
            packet = packet[:, g * half : (g + 1) * half]
            keys = packet[rank].astype(jnp.int32) - first
            wide = spread(packet[:rank], keys, np.arange(count))
            total = total + dot(wide, block[g * half : (g + 1) * half], 1, 0)
        return total.astype(BF16)

    if small:
        down_parts = [down_grad_part(g, 0, jobs) for g in range(groups)]
    else:
        down_parts = [
            lax.map(
                functools.partial(lambda g, b: down_grad_part(g, b * inner, inner), g),
                jnp.arange(outer, dtype=jnp.int32),
            ).reshape(jobs * rank, piece)
            for g in range(groups)
        ]
    down_parts = jnp.concatenate(down_parts, axis=0)
    down_parts, *up_got = lax.optimization_barrier((down_parts, *up_got))
    for got in up_got:
        up_grad = up_grad + got.astype(F32)

    bit = 2
    while bit < inner:
        pairs = frozen.reshape(groups, inner // bit // 2, 2, rows, out_width)
        mine = (place // bit) % 2
        kept = lax.dynamic_index_in_dim(pairs, mine, 2, keepdims=False)
        leaving = lax.dynamic_index_in_dim(pairs, 1 - mine, 2, keepdims=False)
        other = swapped(leaving.astype(BF16), "q", bit)
        if bit == 2:
            other, down_parts = lax.optimization_barrier((other, down_parts))
        frozen = kept + other.astype(F32)
        bit *= 2
    frozen = frozen.reshape(groups, rows, out_width)
    total = lax.dynamic_index_in_dim(frozen, group, 0, keepdims=False)
    for by in range(1, groups):
        leaving = lax.dynamic_index_in_dim(frozen, (group + by) % groups, 0, keepdims=False)
        total = total + shifted(leaving.astype(BF16), "groups", by).astype(F32)
    frozen = total

    down_parts = exchanged(down_parts, ("groups", "z", "q"))
    down_parts = down_parts.reshape(groups, outer, inner, rank, piece)
    down_grad = down_parts.transpose(3, 1, 2, 0, 4).reshape(rank, width).astype(F32).T
    wide = spread(reduced_own, row_job_labels, up_jobs)
    projected = (frozen + ADAPTER_SCALE * dot(wide, up_all, 0, 0)).astype(BF16)

    return (projected, entering_derivative, down_grad[None], up_grad[None])


def solution(mesh):
    groups, devices = mesh.devices.shape
    inner = 1
    while inner * inner < devices:
        inner *= 2
    fine = Mesh(
        mesh.devices.reshape(groups, devices // inner, inner), ("groups", "z", "q")
    )
    every = ("groups", "z", "q")
    owner = ("z", "q")
    return jax.shard_map(
        per_device,
        mesh=fine,
        in_specs=(
            P(every, None),
            P(every, None),
            P(every),
            P(owner, None),
            P(owner, None, None),
            P(owner, None, None),
        ),
        out_specs=(
            P(every, None),
            P(every, None),
            P(every, None, None),
            P(every, None, None),
        ),
        check_vma=False,
    )
```

time: 253 us -> 232 us (0.917)
  waiting for transfers between devices: 80.6 us -> 112 us
  starting transfers between devices: 74.5 us -> 51 us
  matrix products: 37.9 us -> 20.6 us
  between operations: 14.9 us -> 1.75 us
  local copies, waits for them, and re-layouts: 21.4 us -> 31.9 us
  other arithmetic: 19.1 us -> 10.6 us
    ppermute x12 -> x0, starting transfers between devices: 38.2 us -> none  [the longest x6 30.5 us: line_gather(): rising.append(lax.ppermute(rising[-1], axis, upward))]
    ppermute x12 -> x0, waiting for transfers between devices: 29.1 us -> none  [the longest x6 28.9 us: line_gather(): falling.append(lax.ppermute(falling[-1], axis, downward))]
    ppermute x7 -> x15, waiting for transfers between devices: 13.7 us -> 38.6 us  [swapped(): return lax.ppermute(array, axis, [(i, i ^ bit) for i in range(peers)])]
    ppermute x11 -> x18, waiting for transfers between devices: 34.3 us -> 57.3 us  [shifted(): lax.ppermute(array, axis, [(i, (i + by) % peers) for i in range(peers)])]
    dot_general x15, matrix products: 37.9 us -> 20.6 us  [dot(): lax.dot_general(left, right, (((left_dim,), (right_dim,)), ((), ())), pre...]
    ppermute x11 -> x18, starting transfers between devices: 15.2 us -> 29 us  [shifted(): lax.ppermute(array, axis, [(i, (i + by) % peers) for i in range(peers)])]
    all_to_all x4 -> x3, waiting for transfers between devices: 3.44 us -> 15.8 us  [exchanged(): return lax.all_to_all(array, axes, split_axis=0, concat_axis=0, tiled=True)]
    dynamic_update_slice x6 -> x0, other arithmetic: 11.2 us -> none  [line_gather(): stack = lax.dynamic_update_index_in_dim(stack, block, (me - by) % peers, 0)]
  transfers between devices with their start and end apart: 36 -> 36, of which waited for: 16 -> 13; matrix products, arithmetic and copies ran while one was open for 28% -> 21% of each run, Pallas kernels for 1% -> 1%
where the time goes in v3:
time: 232 us; the launch traced here: 231 us
  waiting for transfers between devices  112 us (48%)
  starting transfers between devices  51 us (22%)
  local copies, waits for them, and re-layouts  31.9 us (14%)
  matrix products  20.6 us (9%)
  other arithmetic  10.6 us (5%)
  Pallas kernels  3.19 us (1%)
    ppermute x18, waiting for transfers between devices, shifted(): lax.ppermute(array, axis, [(i, (i + by) % peers) for i in range(peers)])  57.3 us
    ppermute x15, waiting for transfers between devices, swapped(): return lax.ppermute(array, axis, [(i, i ^ bit) for i in range(peers)])  38.6 us
    ppermute x18, starting transfers between devices, shifted(): lax.ppermute(array, axis, [(i, (i + by) % peers) for i in range(peers)])  29 us
    dot_general x15, matrix products, dot(): lax.dot_general(left, right, (((left_dim,), (right_dim,)), ((), ())), pre...  20.6 us
    all_to_all x3, waiting for transfers between devices, exchanged(): return lax.all_to_all(array, axes, split_axis=0, concat_axis=0, tiled=True)  15.8 us
    unnamed x60, local copies, waits for them, and re-layouts  13.9 us
    ppermute x15, starting transfers between devices, swapped(): return lax.ppermute(array, axis, [(i, i ^ bit) for i in range(peers)])  11.1 us
    all_to_all x3, starting transfers between devices, exchanged(): return lax.all_to_all(array, axes, split_axis=0, concat_axis=0, tiled=True)  11 us
  transfers between devices with their start and end apart: 36, of which 13 were waited for; matrix products, arithmetic and copies ran while one was open for 21% of the time, Pallas kernels for 1%

profile of v3, /device:TPU:0, one launch (start us, length us, event | category | flops | bytes accessed | tf_op | source)
XLA Modules:
  0.0 230.7 jit_solution(592382884517355659)
XLA Ops:
  0.6 3.1 %collective-permute-start.3 = (bf16[64,1024]{1,0:T(8,128)(2,1)}, bf16[64,1024]{1,0:T(8,128)(2,1)S(1)}, u32[]{:S(2)}, u32[]{:S(2)}) collective-permute-start(bf16[64,1024]{1,0:T(8,128)(2,1)} %bitcast.270), channel_id=1, source_target_pairs={{0,4},{4,8},{8,12},{12,0},{1,5},{5,9},{9,13},{13,1},{2,6},{6,10},{... | collective-permute-start | bytes 393224 | tf_op jit(solution)/shard_map/ppermute | solution.py:25
  3.7 2.6 %collective-permute-start.4 = (bf16[64,1024]{1,0:T(8,128)(2,1)}, bf16[64,1024]{1,0:T(8,128)(2,1)S(1)}, u32[]{:S(2)}, u32[]{:S(2)}) collective-permute-start(bf16[64,1024]{1,0:T(8,128)(2,1)} %bitcast.271), channel_id=1, source_target_pairs={{0,8},{4,12},{8,0},{12,4},{1,9},{5,13},{9,1},{13,5},{2,10},{6,14},... | collective-permute-start | bytes 393224 | tf_op jit(solution)/shard_map/ppermute | solution.py:25
  6.3 1.3 collective-permute-start.5
  7.6 1.8 reshape.611
  9.5 1.2 constant_dynamic-slice_fusion.8
  12.1 1.5 collective-permute-start.1
  13.6 1.9 dynamic-slice_dynamic-update-slice_fusion
  16.2 1.6 shard_map.210
  19.6 3.7 %collective-permute-done.2 = bf16[64,1024]{1,0:T(8,128)(2,1)S(1)} collective-permute-done((bf16[64,1024]{1,0:T(8,128)(2,1)S(1)}, bf16[64,1024]{1,0:T(8,128)(2,1)S(1)}, u32[]{:S(2)}, u32[]{:S(2)}) %collective-permute-start.2) | collective-permute-done | bytes 131104 | tf_op jit(solution)/shard_map/ppermute | solution.py:20
  24.0 3.7 %all-to-all-start = ((bf16[8,128,1024]{2,1,0:T(8,128)(2,1)}), bf16[8,128,1024]{2,1,0:T(8,128)(2,1)S(1)}, u32[]{:S(2)}, u32[]{:S(2)}) async-start(bf16[8,128,1024]{2,1,0:T(8,128)(2,1)} %bitcast.9), calls=%async_computation | async-start | bytes 4194304 | tf_op jit(solution)/shard_map/all_to_all | solution.py:73
  27.9 0.9 broadcast_in_dim.257
  30.1 3.2 %collective-permute-start.7 = (bf16[512,1024]{1,0:T(8,128)(2,1)}, bf16[512,1024]{1,0:T(8,128)(2,1)S(1)}, u32[]{:S(2)}, u32[]{:S(2)}) collective-permute-start(bf16[512,1024]{1,0:T(8,128)(2,1)} %get-tuple-element.36), channel_id=1, source_target_pairs={{0,12},{4,0},{8,4},{12,8},{1,13},{5,1},{9,5},{13,9},{2,14},{6,2},{... | collective-permute-start | bytes 3145736 | tf_op jit(solution)/shard_map/ppermute | solution.py:25
  35.2 1.8 collective-permute-start.8
  37.4 1.0 copy-done.13
  38.4 26.3 %collective-permute-done.8 = bf16[1,256,1024]{2,1,0:T(8,128)(2,1)} collective-permute-done((bf16[1,256,1024]{2,1,0:T(8,128)(2,1)}, bf16[1,256,1024]{2,1,0:T(8,128)(2,1)}, u32[]{:S(2)}, u32[]{:S(2)}) %collective-permute-start.8) | collective-permute-done | bytes 524320 | tf_op jit(solution)/shard_map/ppermute | solution.py:20
  64.7 13.1 %collective-permute-done.7 = bf16[512,1024]{1,0:T(8,128)(2,1)S(1)} collective-permute-done((bf16[512,1024]{1,0:T(8,128)(2,1)}, bf16[512,1024]{1,0:T(8,128)(2,1)S(1)}, u32[]{:S(2)}, u32[]{:S(2)}) %collective-permute-start.7) | collective-permute-done | bytes 1048608 | tf_op jit(solution)/shard_map/ppermute | solution.py:25
  77.9 2.1 collective-permute-start.25
  80.1 1.4 select_bitcast_fusion.7
  82.0 1.4 slice_dynamic-update-slice_fusion
  83.5 1.1 bitcast_dynamic-update-slice_fusion.2
  84.5 7.9 %collective-permute-done.25 = bf16[256,1024]{1,0:T(8,128)(2,1)S(1)} collective-permute-done((bf16[256,1024]{1,0:T(8,128)(2,1)S(1)}, bf16[256,1024]{1,0:T(8,128)(2,1)S(1)}, u32[]{:S(2)}, u32[]{:S(2)}) %collective-permute-start.25) | collective-permute-done | bytes 524320 | tf_op jit(solution)/shard_map/ppermute | solution.py:25
  92.6 11.5 %collective-permute-done.10 = bf16[256,1024]{1,0:T(8,128)(2,1)S(1)} collective-permute-done((bf16[256,1024]{1,0:T(8,128)(2,1)S(1)}, bf16[256,1024]{1,0:T(8,128)(2,1)S(1)}, u32[]{:S(2)}, u32[]{:S(2)}) %collective-permute-start.10) | collective-permute-done | bytes 524320 | tf_op jit(solution)/shard_map/ppermute | solution.py:25
  104.5 1.3 copy-done.1
  107.3 2.4 %collective-permute-start.17 = (bf16[80,128]{1,0:T(8,128)(2,1)S(1)}, bf16[80,128]{1,0:T(8,128)(2,1)S(1)}, u32[]{:S(2)}, u32[]{:S(2)}) collective-permute-start(bf16[80,128]{1,0:T(8,128)(2,1)S(1)} %pad_maximum_fusion.6), channel_id=1, source_target_pairs={{0,8},{4,12},{8,0},{12,4},{1,9},{5,13},{9,1},{13,5},{2,10},{6,14},... | collective-permute-start | bytes 61448 | tf_op jit(solution)/shard_map/ppermute | solution.py:25
  109.7 1.4 collective-permute-start.18
  111.1 1.5 collective-permute-start.22
  112.6 2.4 %fusion.31 = f32[1024,1024]{1,0:T(8,128)S(1)} fusion(bf16[1024,1024]{1,0:T(8,128)(2,1)S(1)} %constant_dynamic-update-slice_fusion.3, bf16[1024,1024]{1,0:T(8,128)(2,1)S(1)} %bitcast.230), kind=kOutput, calls=%fused_computation.163 | convolution fusion | flops 2147483648 | bytes 8388608 | tf_op jit(solution)/shard_map/dot_general | solution.py:77
  115.7 1.4 constant_dynamic-slice_fusion.4
  117.9 2.4 %collective-permute-start.14 = (bf16[1024,256]{1,0:T(8,128)(2,1)}, bf16[1024,256]{1,0:T(8,128)(2,1)}, u32[]{:S(2)}, u32[]{:S(2)}) collective-permute-start(bf16[1024,256]{1,0:T(8,128)(2,1)} %get-tuple-element.69), channel_id=1, source_target_pairs={{0,8},{4,12},{8,0},{12,4},{1,9},{5,13},{9,1},{13,5},{2,10},{6,14},... | collective-permute-start | bytes 1572872 | tf_op jit(solution)/shard_map/ppermute | solution.py:25
  120.3 1.5 collective-permute-start.20
  121.9 2.4 %fusion.29 = f32[2,2,2,128,1024]{4,3,2,1,0:T(8,128)S(1)} fusion(bf16[2,2,2,128,1024]{4,3,2,1,0:T(8,128)(2,1)S(1)} %bitcast.232, bf16[1024,1024,1,1,1]{1,0,4,3,2:T(8,128)(2,1)S(1)} %bitcast.255), kind=kOutput, calls=%fused_computation.161 | convolution fusion | flops 2147483648 | bytes 8388608 | tf_op jit(solution)/shard_map/dot_general | solution.py:77
  124.5 1.2 collective-permute-done.20
  126.2 0.9 maximum_bitcast_fusion.1
  127.1 1.2 collective-permute-start.23
  129.8 1.6 collective-permute-start.26
  131.5 2.4 %fusion.30 = f32[1024,1024]{1,0:T(8,128)S(1)} fusion(bf16[1024,1024]{1,0:T(8,128)(2,1)S(1)} %bitcast.259, bf16[1024,1024]{1,0:T(8,128)(2,1)S(1)} %copy-done.23), kind=kOutput, calls=%fused_computation.162 | convolution fusion | flops 2147483648 | bytes 8388608 | tf_op jit(solution)/shard_map/dot_general | solution.py:77
  133.9 7.4 %collective-permute-done.23 = bf16[2,128,1024]{2,1,0:T(8,128)(2,1)S(1)} collective-permute-done((bf16[2,128,1024]{2,1,0:T(8,128)(2,1)}, bf16[2,128,1024]{2,1,0:T(8,128)(2,1)S(1)}, u32[]{:S(2)}, u32[]{:S(2)}) %collective-permute-start.23) | collective-permute-done | bytes 524320 | tf_op jit(solution)/shard_map/ppermute | solution.py:20
  141.7 1.3 collective-permute-start.15
  143.0 1.5 collective-permute-start.27
  144.5 1.7 bitcast_add_fusion
  146.2 1.0 dynamic-slice_convert_fusion.1
  148.5 2.1 copy-done.11
  150.6 3.7 %add_convert_fusion = bf16[1024,1024]{1,0:T(8,128)(2,1)} fusion(f32[1024,1024]{1,0:T(8,128)S(1)} %fusion.30, bf16[1024,1024]{1,0:T(8,128)(2,1)S(1)} %bitcast.236, bf16[1024,1024]{1,0:T(8,128)(2,1)S(1)} %bitcast.256), kind=kOutput, calls=%fused_computation.1 | convolution fusion | flops 2149580800 | bytes 10485760 | tf_op jit(solution)/shard_map/dot_general | solution.py:77
  154.4 10.3 %collective-permute-done.15 = bf16[1024,256]{1,0:T(8,128)(2,1)S(1)} collective-permute-done((bf16[1024,256]{1,0:T(8,128)(2,1)S(1)}, bf16[1024,256]{1,0:T(8,128)(2,1)S(1)}, u32[]{:S(2)}, u32[]{:S(2)}) %collective-permute-start.15) | collective-permute-done | bytes 524320 | tf_op jit(solution)/shard_map/ppermute | solution.py:25
  165.8 3.8 %all-to-all-start.1 = ((bf16[8,128,1024]{2,1,0:T(8,128)(2,1)}), bf16[8,128,1024]{2,1,0:T(8,128)(2,1)S(1)}, u32[]{:S(2)}, u32[]{:S(2)}) async-start(bf16[8,128,1024]{2,1,0:T(8,128)(2,1)} %bitcast.257), calls=%async_computation.1 | async-start | bytes 4194304 | tf_op jit(solution)/shard_map/all_to_all | solution.py:73
  170.4 1.3 copy-done.5
  173.8 3.1 %collective-permute-start.31 = (bf16[64,1024]{1,0:T(8,128)(2,1)S(1)}, bf16[64,1024]{1,0:T(8,128)(2,1)S(1)}, u32[]{:S(2)}, u32[]{:S(2)}) collective-permute-start(bf16[64,1024]{1,0:T(8,128)(2,1)S(1)} %get-tuple-element.86), channel_id=1, source_target_pairs={{0,12},{4,0},{8,4},{12,8},{1,13},{5,1},{9,5},{13,9},{2,14},{6,2},{... | collective-permute-start | bytes 393224 | tf_op jit(solution)/shard_map/ppermute | solution.py:25
  177.0 1.4 convolution_add_fusion.5
  178.4 1.4 convolution_add_fusion.4
  180.3 1.4 convolution_add_fusion.2
  181.7 1.4 convolution_add_fusion.1
  183.5 1.1 pad_maximum_fusion.3
  184.6 1.9 collective-permute-done.30
  187.2 8.1 %all-to-all-done.1 = bf16[8,128,1024]{2,1,0:T(8,128)(2,1)S(1)} async-done(((bf16[8,128,1024]{2,1,0:T(8,128)(2,1)}), bf16[8,128,1024]{2,1,0:T(8,128)(2,1)S(1)}, u32[]{:S(2)}, u32[]{:S(2)}) %all-to-all-start.1) | async-done | bytes 2097184 | tf_op jit(solution)/shard_map/all_to_all | solution.py:73
  195.2 3.4 %all-to-all-start.2 = ((bf16[32,64,256]{2,1,0:T(8,128)(2,1)}), bf16[32,64,256]{2,1,0:T(8,128)(2,1)}, u32[]{:S(2)}, u32[]{:S(2)}) async-start(bf16[32,64,256]{2,1,0:T(8,128)(2,1)} %bitcast.240), calls=%async_computation.2 | async-start | bytes 2097152 | tf_op jit(solution)/shard_map/all_to_all | solution.py:73
  198.7 1.7 convert_add_fusion
  200.4 1.6 collective-permute-start.32
  202.0 0.8 fusion.9
  202.8 12.4 %collective-permute-done.32 = bf16[128,1024]{1,0:T(8,128)(2,1)S(1)} collective-permute-done((bf16[128,1024]{1,0:T(8,128)(2,1)S(1)}, bf16[128,1024]{1,0:T(8,128)(2,1)S(1)}, u32[]{:S(2)}, u32[]{:S(2)}) %collective-permute-start.32) | collective-permute-done | bytes 262176 | tf_op jit(solution)/shard_map/ppermute | solution.py:25
  215.3 1.2 fusion.5
  216.4 1.6 shard_map.211
  218.0 7.7 %all-to-all-done.2 = bf16[32,64,256]{2,1,0:T(8,128)(2,1)} async-done(((bf16[32,64,256]{2,1,0:T(8,128)(2,1)}), bf16[32,64,256]{2,1,0:T(8,128)(2,1)}, u32[]{:S(2)}, u32[]{:S(2)}) %all-to-all-start.2) | async-done | bytes 1048608 | tf_op jit(solution)/shard_map/all_to_all | solution.py:73
  225.8 2.3 copy.58
  228.1 2.7 %reshape.635 = f32[64,8192]{1,0:T(8,128)} reshape(f32[64,4,4,2,256]{4,3,2,1,0:T(2,128)S(1)} %bitcast.233) | data formatting | bytes 4194304 | tf_op jit(solution)/shard_map/broadcast_in_dim | solution.py:303
  (178 shorter events, 21.5 us)
Async XLA Ops:
  0.6 23.4 %collective-permute-start.3 = (bf16[64,1024]{1,0:T(8,128)(2,1)}, bf16[64,1024]{1,0:T(8,128)(2,1)S(1)}, u32[]{:S(2)}, u32[]{:S(2)}) collective-permute-start(bf16[64,1024]{1,0:T(8,128)(2,1)} %bitcast.270), channel_id=1, source_target_pairs={{0,4},{4,8},{8,12},{12,0},{1,5},{5,9},{9,13},{13,1},{2,6},{6,10},{... | collective-permute-start | bytes 393224 | tf_op jit(solution)/shard_map/ppermute | solution.py:25
  3.7 20.3 %collective-permute-start.4 = (bf16[64,1024]{1,0:T(8,128)(2,1)}, bf16[64,1024]{1,0:T(8,128)(2,1)S(1)}, u32[]{:S(2)}, u32[]{:S(2)}) collective-permute-start(bf16[64,1024]{1,0:T(8,128)(2,1)} %bitcast.271), channel_id=1, source_target_pairs={{0,8},{4,12},{8,0},{12,4},{1,9},{5,13},{9,1},{13,5},{2,10},{6,14},... | collective-permute-start | bytes 393224 | tf_op jit(solution)/shard_map/ppermute | solution.py:25
  6.3 17.7 %collective-permute-start.5 = (bf16[64,1024]{1,0:T(8,128)(2,1)}, bf16[64,1024]{1,0:T(8,128)(2,1)S(1)}, u32[]{:S(2)}, u32[]{:S(2)}) collective-permute-start(bf16[64,1024]{1,0:T(8,128)(2,1)} %bitcast.272), channel_id=1, source_target_pairs={{0,12},{4,0},{8,4},{12,8},{1,13},{5,1},{9,5},{13,9},{2,14},{6,2},{... | collective-permute-start | bytes 393224 | tf_op jit(solution)/shard_map/ppermute | solution.py:25
  10.7 5.5 %copy-start = (bf16[128,8192]{1,0:T(8,128)(2,1)S(1)}, bf16[128,8192]{1,0:T(8,128)(2,1)}, u32[]{:S(2)}) copy-start(bf16[128,8192]{1,0:T(8,128)(2,1)} %source.1) | copy-start | bytes 6291460
  12.1 5.7 %collective-permute-start = (bf16[64,1024]{1,0:T(8,128)(2,1)}, bf16[64,1024]{1,0:T(8,128)(2,1)S(1)}, u32[]{:S(2)}, u32[]{:S(2)}) collective-permute-start(bf16[64,1024]{1,0:T(8,128)(2,1)} %get-tuple-element.95), channel_id=1, source_target_pairs={{0,1},{1,0},{2,3},{3,2},{4,5},{5,4},{6,7},{7,6},{8,9},{9,8},{10,11... | collective-permute-start | bytes 393224 | tf_op jit(solution)/shard_map/ppermute | solution.py:20
  12.1 6.8 %collective-permute-start.1 = (bf16[64,1024]{1,0:T(8,128)(2,1)S(1)}, bf16[64,1024]{1,0:T(8,128)(2,1)S(1)}, u32[]{:S(2)}, u32[]{:S(2)}) collective-permute-start(bf16[64,1024]{1,0:T(8,128)(2,1)S(1)} %get-tuple-element.94), channel_id=1, source_target_pairs={{0,2},{1,3},{2,0},{3,1},{4,6},{5,7},{6,4},{7,5},{8,10},{9,11},{10,... | collective-permute-start | bytes 393224 | tf_op jit(solution)/shard_map/ppermute | solution.py:20
  17.8 5.5 %collective-permute-start.2 = (bf16[64,1024]{1,0:T(8,128)(2,1)S(1)}, bf16[64,1024]{1,0:T(8,128)(2,1)S(1)}, u32[]{:S(2)}, u32[]{:S(2)}) collective-permute-start(bf16[64,1024]{1,0:T(8,128)(2,1)S(1)} %get-tuple-element.93), channel_id=1, source_target_pairs={{0,3},{1,2},{2,1},{3,0},{4,7},{5,6},{6,5},{7,4},{8,11},{9,10},{10,... | collective-permute-start | bytes 393224 | tf_op jit(solution)/shard_map/ppermute | solution.py:20
  24.0 4.7 %copy-start.20 = (bf16[1,64,1024]{2,1,0:T(8,128)(2,1)S(1)}, bf16[1,64,1024]{2,1,0:T(8,128)(2,1)}, u32[]{:S(2)}) copy-start(bf16[1,64,1024]{2,1,0:T(8,128)(2,1)} %param.24) | copy-start | bytes 393220
  24.0 13.0 %copy-start.24 = (s32[128]{0:T(128)S(1)}, s32[128]{0:T(128)}, u32[]{:S(2)}) copy-start(s32[128]{0:T(128)} %param.21) | copy-start | bytes 1540
  24.0 53.8 %all-to-all-start = ((bf16[8,128,1024]{2,1,0:T(8,128)(2,1)}), bf16[8,128,1024]{2,1,0:T(8,128)(2,1)S(1)}, u32[]{:S(2)}, u32[]{:S(2)}) async-start(bf16[8,128,1024]{2,1,0:T(8,128)(2,1)} %bitcast.9), calls=%async_computation | async-start | bytes 4194304 | tf_op jit(solution)/shard_map/all_to_all | solution.py:73
  29.4 8.9 %copy-start.25 = (s32[16]{0:T(128)S(1)}, s32[16]{0:T(128)}, u32[]{:S(2)}) copy-start(s32[16]{0:T(128)} %constant.233) | copy-start | bytes 196
  29.4 35.3 %collective-permute-start.6 = (bf16[512,1024]{1,0:T(8,128)(2,1)}, bf16[512,1024]{1,0:T(8,128)(2,1)}, u32[]{:S(2)}, u32[]{:S(2)}) collective-permute-start(bf16[512,1024]{1,0:T(8,128)(2,1)} %get-tuple-element.36), channel_id=1, source_target_pairs={{0,4},{4,8},{8,12},{12,0},{1,5},{5,9},{9,13},{13,1},{2,6},{6,10},{... | collective-permute-start | bytes 3145736 | tf_op jit(solution)/shard_map/ppermute | solution.py:25
  30.1 47.8 %collective-permute-start.7 = (bf16[512,1024]{1,0:T(8,128)(2,1)}, bf16[512,1024]{1,0:T(8,128)(2,1)S(1)}, u32[]{:S(2)}, u32[]{:S(2)}) collective-permute-start(bf16[512,1024]{1,0:T(8,128)(2,1)} %get-tuple-element.36), channel_id=1, source_target_pairs={{0,12},{4,0},{8,4},{12,8},{1,13},{5,1},{9,5},{13,9},{2,14},{6,2},{... | collective-permute-start | bytes 3145736 | tf_op jit(solution)/shard_map/ppermute | solution.py:25
  35.2 29.5 %collective-permute-start.8 = (bf16[1,256,1024]{2,1,0:T(8,128)(2,1)}, bf16[1,256,1024]{2,1,0:T(8,128)(2,1)}, u32[]{:S(2)}, u32[]{:S(2)}) collective-permute-start(bf16[1,256,1024]{2,1,0:T(8,128)(2,1)} %bitcast.14), channel_id=1, source_target_pairs={{0,2},{1,3},{2,0},{3,1},{4,6},{5,7},{6,4},{7,5},{8,10},{9,11},{10,... | collective-permute-start | bytes 1572872 | tf_op jit(solution)/shard_map/ppermute | solution.py:20
  37.1 1.2 copy-start.13
  38.4 26.4 %copy-start.8 = (bf16[4,256,1024]{2,1,0:T(8,128)(2,1)}, bf16[4,256,1024]{2,1,0:T(8,128)(2,1)S(1)}, u32[]{:S(2)}) copy-start(bf16[4,256,1024]{2,1,0:T(8,128)(2,1)S(1)} %bitcast_dynamic-update-slice_fusion.3) | copy-start | bytes 6291460
  77.9 14.5 %collective-permute-start.25 = (bf16[256,1024]{1,0:T(8,128)(2,1)S(1)}, bf16[256,1024]{1,0:T(8,128)(2,1)S(1)}, u32[]{:S(2)}, u32[]{:S(2)}) collective-permute-start(bf16[256,1024]{1,0:T(8,128)(2,1)S(1)} %slice.121), channel_id=1, source_target_pairs={{0,12},{4,0},{8,4},{12,8},{1,13},{5,1},{9,5},{13,9},{2,14},{6,2},{... | collective-permute-start | bytes 1572872 | tf_op jit(solution)/shard_map/ppermute | solution.py:25
  80.0 1.9 copy-start.21
  81.5 2.0 copy-start.9
  81.6 22.5 %collective-permute-start.9 = (bf16[2,256,1024]{2,1,0:T(8,128)(2,1)S(1)}, bf16[2,256,1024]{2,1,0:T(8,128)(2,1)S(1)}, u32[]{:S(2)}, u32[]{:S(2)}) collective-permute-start(bf16[2,256,1024]{2,1,0:T(8,128)(2,1)S(1)} %maximum_bitcast_fusion), channel_id=1, source_target_pairs={{0,1},{1,0},{2,3},{3,2},{4,5},{5,4},{6,7},{7,6},{8,9},{9,8},{10,11... | collective-permute-start | bytes 3145736 | tf_op jit(solution)/shard_map/ppermute | solution.py:20
  83.4 20.6 %collective-permute-start.10 = (bf16[256,1024]{1,0:T(8,128)(2,1)S(1)}, bf16[256,1024]{1,0:T(8,128)(2,1)S(1)}, u32[]{:S(2)}, u32[]{:S(2)}) collective-permute-start(bf16[256,1024]{1,0:T(8,128)(2,1)S(1)} %get-tuple-element.77), channel_id=1, source_target_pairs={{0,4},{4,8},{8,12},{12,0},{1,5},{5,9},{9,13},{13,1},{2,6},{6,10},{... | collective-permute-start | bytes 1572872 | tf_op jit(solution)/shard_map/ppermute | solution.py:25
  92.5 20.1 %copy-start.22 = (bf16[1024,1024]{1,0:T(8,128)(2,1)}, bf16[1024,1024]{1,0:T(8,128)(2,1)S(1)}, u32[]{:S(2)}) copy-start(bf16[1024,1024]{1,0:T(8,128)(2,1)S(1)} %constant_dynamic-update-slice_fusion.3) | copy-start | bytes 6291460
  104.1 17.7 %copy-start.10 = (bf16[4,256,1024]{2,1,0:T(8,128)(2,1)}, bf16[4,256,1024]{2,1,0:T(8,128)(2,1)S(1)}, u32[]{:S(2)}) copy-start(bf16[4,256,1024]{2,1,0:T(8,128)(2,1)S(1)} %bitcast_dynamic-update-slice_fusion) | copy-start | bytes 6291460
  104.3 1.5 copy-start.14
  104.5 1.3 copy-start.1
  106.6 8.4 %collective-permute-start.16 = (bf16[80,128]{1,0:T(8,128)(2,1)S(1)}, bf16[80,128]{1,0:T(8,128)(2,1)S(1)}, u32[]{:S(2)}, u32[]{:S(2)}) collective-permute-start(bf16[80,128]{1,0:T(8,128)(2,1)S(1)} %pad_maximum_fusion.6), channel_id=1, source_target_pairs={{0,4},{4,8},{8,12},{12,0},{1,5},{5,9},{9,13},{13,1},{2,6},{6,10},{... | collective-permute-start | bytes 61448 | tf_op jit(solution)/shard_map/ppermute | solution.py:25
  107.3 7.7 %collective-permute-start.17 = (bf16[80,128]{1,0:T(8,128)(2,1)S(1)}, bf16[80,128]{1,0:T(8,128)(2,1)S(1)}, u32[]{:S(2)}, u32[]{:S(2)}) collective-permute-start(bf16[80,128]{1,0:T(8,128)(2,1)S(1)} %pad_maximum_fusion.6), channel_id=1, source_target_pairs={{0,8},{4,12},{8,0},{12,4},{1,9},{5,13},{9,1},{13,5},{2,10},{6,14},... | collective-permute-start | bytes 61448 | tf_op jit(solution)/shard_map/ppermute | solution.py:25
  109.7 5.4 %collective-permute-start.18 = (bf16[80,128]{1,0:T(8,128)(2,1)S(1)}, bf16[80,128]{1,0:T(8,128)(2,1)S(1)}, u32[]{:S(2)}, u32[]{:S(2)}) collective-permute-start(bf16[80,128]{1,0:T(8,128)(2,1)S(1)} %pad_maximum_fusion.6), channel_id=1, source_target_pairs={{0,12},{4,0},{8,4},{12,8},{1,13},{5,1},{9,5},{13,9},{2,14},{6,2},{... | collective-permute-start | bytes 61448 | tf_op jit(solution)/shard_map/ppermute | solution.py:25
  111.1 14.8 %collective-permute-start.22 = (bf16[1,128,1024]{2,1,0:T(8,128)(2,1)S(1)}, bf16[1,128,1024]{2,1,0:T(8,128)(2,1)S(1)}, u32[]{:S(2)}, u32[]{:S(2)}) collective-permute-start(bf16[1,128,1024]{2,1,0:T(8,128)(2,1)S(1)} %bitcast.267), channel_id=1, source_target_pairs={{0,16},{16,0},{1,17},{17,1},{2,18},{18,2},{3,19},{19,3},{4,20},{20... | collective-permute-start | bytes 786440 | tf_op jit(solution)/shard_map/ppermute | solution.py:20
  115.1 5.2 %collective-permute-start.19 = (bf16[1,4,80,128]{3,2,1,0:T(8,128)(2,1)S(1)}, bf16[1,4,80,128]{3,2,1,0:T(8,128)(2,1)S(1)}, u32[]{:S(2)}, u32[]{:S(2)}) collective-permute-start(bf16[1,4,80,128]{3,2,1,0:T(8,128)(2,1)S(1)} %maximum_bitcast_fusion.3), channel_id=1, source_target_pairs={{0,16},{16,0},{1,17},{17,1},{2,18},{18,2},{3,19},{19,3},{4,20},{20... | collective-permute-start | bytes 245768 | tf_op jit(solution)/shard_map/ppermute | solution.py:20
  117.1 37.2 %collective-permute-start.13 = (bf16[1024,256]{1,0:T(8,128)(2,1)}, bf16[1024,256]{1,0:T(8,128)(2,1)}, u32[]{:S(2)}, u32[]{:S(2)}) collective-permute-start(bf16[1024,256]{1,0:T(8,128)(2,1)} %get-tuple-element.70), channel_id=1, source_target_pairs={{0,4},{4,8},{8,12},{12,0},{1,5},{5,9},{9,13},{13,1},{2,6},{6,10},{... | collective-permute-start | bytes 1572872 | tf_op jit(solution)/shard_map/ppermute | solution.py:25
  117.9 36.5 %collective-permute-start.14 = (bf16[1024,256]{1,0:T(8,128)(2,1)}, bf16[1024,256]{1,0:T(8,128)(2,1)}, u32[]{:S(2)}, u32[]{:S(2)}) collective-permute-start(bf16[1024,256]{1,0:T(8,128)(2,1)} %get-tuple-element.69), channel_id=1, source_target_pairs={{0,8},{4,12},{8,0},{12,4},{1,9},{5,13},{9,1},{13,5},{2,10},{6,14},... | collective-permute-start | bytes 1572872 | tf_op jit(solution)/shard_map/ppermute | solution.py:25
  120.3 5.4 %collective-permute-start.20 = (bf16[2,4,80,128]{3,2,1,0:T(8,128)(2,1)S(1)}, bf16[2,4,80,128]{3,2,1,0:T(8,128)(2,1)S(1)}, u32[]{:S(2)}, u32[]{:S(2)}) collective-permute-start(bf16[2,4,80,128]{3,2,1,0:T(8,128)(2,1)S(1)} %maximum_bitcast_fusion.2), channel_id=1, source_target_pairs={{0,2},{1,3},{2,0},{3,1},{4,6},{5,7},{6,4},{7,5},{8,10},{9,11},{10,... | collective-permute-start | bytes 491528 | tf_op jit(solution)/shard_map/ppermute | solution.py:20
  124.2 2.0 copy-start.6
  124.4 18.6 %collective-permute-start.11 = (bf16[2,2,128,1024]{3,2,1,0:T(8,128)(2,1)S(1)}, bf16[2,2,128,1024]{3,2,1,0:T(8,128)(2,1)}, u32[]{:S(2)}, u32[]{:S(2)}) collective-permute-start(bf16[2,2,128,1024]{3,2,1,0:T(8,128)(2,1)S(1)} %fusion.2), channel_id=1, source_target_pairs={{0,1},{1,0},{2,3},{3,2},{4,5},{5,4},{6,7},{7,6},{8,9},{9,8},{10,11... | collective-permute-start | bytes 3145736 | tf_op jit(solution)/shard_map/ppermute | solution.py:20
  125.8 2.5 %collective-permute-start.21 = (bf16[4,4,80,128]{3,2,1,0:T(8,128)(2,1)S(1)}, bf16[4,4,80,128]{3,2,1,0:T(8,128)(2,1)S(1)}, u32[]{:S(2)}, u32[]{:S(2)}) collective-permute-start(bf16[4,4,80,128]{3,2,1,0:T(8,128)(2,1)S(1)} %bitcast.263), channel_id=1, source_target_pairs={{0,1},{1,0},{2,3},{3,2},{4,5},{5,4},{6,7},{7,6},{8,9},{9,8},{10,11... | collective-permute-start | bytes 983048 | tf_op jit(solution)/shard_map/ppermute | solution.py:20
  127.1 14.3 %collective-permute-start.23 = (bf16[2,128,1024]{2,1,0:T(8,128)(2,1)}, bf16[2,128,1024]{2,1,0:T(8,128)(2,1)S(1)}, u32[]{:S(2)}, u32[]{:S(2)}) collective-permute-start(bf16[2,128,1024]{2,1,0:T(8,128)(2,1)} %maximum_bitcast_fusion.1), channel_id=1, source_target_pairs={{0,2},{1,3},{2,0},{3,1},{4,6},{5,7},{6,4},{7,5},{8,10},{9,11},{10,... | collective-permute-start | bytes 1572872 | tf_op jit(solution)/shard_map/ppermute | solution.py:20
  129.5 2.0 copy-start.23
  129.8 11.9 %collective-permute-start.26 = (f32[64,512]{1,0:T(8,128)S(1)}, f32[64,512]{1,0:T(8,128)S(1)}, u32[]{:S(2)}, u32[]{:S(2)}) collective-permute-start(f32[64,512]{1,0:T(8,128)S(1)} %bitcast.273), channel_id=1, source_target_pairs={{0,16},{16,0},{1,17},{17,1},{2,18},{18,2},{3,19},{19,3},{4,20},{20... | collective-permute-start | bytes 393224 | tf_op jit(solution)/shard_map/ppermute | solution.py:25
  131.5 10.2 %copy-start.17 = (bf16[1024,256]{1,0:T(8,128)(2,1)S(1)}, bf16[1024,256]{1,0:T(8,128)(2,1)}, u32[]{:S(2)}) copy-start(bf16[1024,256]{1,0:T(8,128)(2,1)} %get-tuple-element.68) | copy-start | bytes 1572868
  133.9 10.6 %copy-start.7 = (f32[2,2,2,128,1024]{4,3,2,1,0:T(8,128)S(1)}, f32[2,2,2,128,1024]{4,3,2,1,0:T(8,128)}, u32[]{:S(2)}) copy-start(f32[2,2,2,128,1024]{4,3,2,1,0:T(8,128)} %copy-done.6) | copy-start | bytes 12582916
  141.5 5.8 %collective-permute-start.24 = (bf16[4,128,1024]{2,1,0:T(8,128)(2,1)S(1)}, bf16[4,128,1024]{2,1,0:T(8,128)(2,1)S(1)}, u32[]{:S(2)}, u32[]{:S(2)}) collective-permute-start(bf16[4,128,1024]{2,1,0:T(8,128)(2,1)S(1)} %bitcast.238), channel_id=1, source_target_pairs={{0,1},{1,0},{2,3},{3,2},{4,5},{5,4},{6,7},{7,6},{8,9},{9,8},{10,11... | collective-permute-start | bytes 3145736 | tf_op jit(solution)/shard_map/ppermute | solution.py:20
  141.7 23.0 %collective-permute-start.15 = (bf16[1024,256]{1,0:T(8,128)(2,1)S(1)}, bf16[1024,256]{1,0:T(8,128)(2,1)S(1)}, u32[]{:S(2)}, u32[]{:S(2)}) collective-permute-start(bf16[1024,256]{1,0:T(8,128)(2,1)S(1)} %copy-done.17), channel_id=1, source_target_pairs={{0,12},{4,0},{8,4},{12,8},{1,13},{5,1},{9,5},{13,9},{2,14},{6,2},{... | collective-permute-start | bytes 1572872 | tf_op jit(solution)/shard_map/ppermute | solution.py:25
  143.0 21.7 %collective-permute-start.27 = (f32[64,512]{1,0:T(8,128)S(1)}, f32[64,512]{1,0:T(8,128)S(1)}, u32[]{:S(2)}, u32[]{:S(2)}) collective-permute-start(f32[64,512]{1,0:T(8,128)S(1)} %bitcast_add_fusion.3), channel_id=1, source_target_pairs={{0,2},{1,3},{2,0},{3,1},{4,6},{5,7},{6,4},{7,5},{8,10},{9,11},{10,... | collective-permute-start | bytes 393224 | tf_op jit(solution)/shard_map/ppermute | solution.py:20
  146.2 1.8 copy-start.3
  147.3 39.9 %collective-permute-start.12 = (bf16[2,1,128,1024]{3,2,1,0:T(8,128)(2,1)}, bf16[2,1,128,1024]{3,2,1,0:T(8,128)(2,1)}, u32[]{:S(2)}, u32[]{:S(2)}) collective-permute-start(bf16[2,1,128,1024]{3,2,1,0:T(8,128)(2,1)} %dynamic-slice_convert_fusion.1), channel_id=1, source_target_pairs={{0,2},{1,3},{2,0},{3,1},{4,6},{5,7},{6,4},{7,5},{8,10},{9,11},{10,... | collective-permute-start | bytes 1572872 | tf_op jit(solution)/shard_map/ppermute | solution.py:20
  148.3 2.3 %copy-start.11 = (bf16[4,256,1024]{2,1,0:T(8,128)(2,1)S(1)}, bf16[4,256,1024]{2,1,0:T(8,128)(2,1)}, u32[]{:S(2)}) copy-start(bf16[4,256,1024]{2,1,0:T(8,128)(2,1)} %copy-done.10) | copy-start | bytes 6291460
  148.4 5.9 %copy-start.4 = (bf16[4,2,128,1024]{3,2,1,0:T(8,128)(2,1)}, bf16[4,2,128,1024]{3,2,1,0:T(8,128)(2,1)S(1)}, u32[]{:S(2)}) copy-start(bf16[4,2,128,1024]{3,2,1,0:T(8,128)(2,1)S(1)} %copy.46) | copy-start | bytes 6291460
  164.7 0.8 copy-start.15
  165.6 4.7 %collective-permute-start.28 = (f32[64,512]{1,0:T(8,128)S(1)}, f32[64,512]{1,0:T(8,128)S(1)}, u32[]{:S(2)}, u32[]{:S(2)}) collective-permute-start(f32[64,512]{1,0:T(8,128)S(1)} %add.264), channel_id=1, source_target_pairs={{0,1},{1,0},{2,3},{3,2},{4,5},{5,4},{6,7},{7,6},{8,9},{9,8},{10,11... | collective-permute-start | bytes 393224 | tf_op jit(solution)/shard_map/ppermute | solution.py:20
  165.8 29.4 %all-to-all-start.1 = ((bf16[8,128,1024]{2,1,0:T(8,128)(2,1)}), bf16[8,128,1024]{2,1,0:T(8,128)(2,1)S(1)}, u32[]{:S(2)}, u32[]{:S(2)}) async-start(bf16[8,128,1024]{2,1,0:T(8,128)(2,1)} %bitcast.257), calls=%async_computation.1 | async-start | bytes 4194304 | tf_op jit(solution)/shard_map/all_to_all | solution.py:73
  170.0 1.6 copy-start.5
  170.3 1.8 copy-start.12
  173.1 11.5 %collective-permute-start.29 = (bf16[64,1024]{1,0:T(8,128)(2,1)S(1)}, bf16[64,1024]{1,0:T(8,128)(2,1)S(1)}, u32[]{:S(2)}, u32[]{:S(2)}) collective-permute-start(bf16[64,1024]{1,0:T(8,128)(2,1)S(1)} %get-tuple-element.88), channel_id=1, source_target_pairs={{0,4},{4,8},{8,12},{12,0},{1,5},{5,9},{9,13},{13,1},{2,6},{6,10},{... | collective-permute-start | bytes 393224 | tf_op jit(solution)/shard_map/ppermute | solution.py:25
  173.7 12.8 %collective-permute-start.30 = (bf16[64,1024]{1,0:T(8,128)(2,1)S(1)}, bf16[64,1024]{1,0:T(8,128)(2,1)S(1)}, u32[]{:S(2)}, u32[]{:S(2)}) collective-permute-start(bf16[64,1024]{1,0:T(8,128)(2,1)S(1)} %get-tuple-element.87), channel_id=1, source_target_pairs={{0,8},{4,12},{8,0},{12,4},{1,9},{5,13},{9,1},{13,5},{2,10},{6,14},... | collective-permute-start | bytes 393224 | tf_op jit(solution)/shard_map/ppermute | solution.py:25
  173.8 12.7 %collective-permute-start.31 = (bf16[64,1024]{1,0:T(8,128)(2,1)S(1)}, bf16[64,1024]{1,0:T(8,128)(2,1)S(1)}, u32[]{:S(2)}, u32[]{:S(2)}) collective-permute-start(bf16[64,1024]{1,0:T(8,128)(2,1)S(1)} %get-tuple-element.86), channel_id=1, source_target_pairs={{0,12},{4,0},{8,4},{12,8},{1,13},{5,1},{9,5},{13,9},{2,14},{6,2},{... | collective-permute-start | bytes 393224 | tf_op jit(solution)/shard_map/ppermute | solution.py:25
  178.4 1.5 copy-start.16
  186.5 0.7 copy-start.18
  195.2 30.5 %all-to-all-start.2 = ((bf16[32,64,256]{2,1,0:T(8,128)(2,1)}), bf16[32,64,256]{2,1,0:T(8,128)(2,1)}, u32[]{:S(2)}, u32[]{:S(2)}) async-start(bf16[32,64,256]{2,1,0:T(8,128)(2,1)} %bitcast.240), calls=%async_computation.2 | async-start | bytes 2097152 | tf_op jit(solution)/shard_map/all_to_all | solution.py:73
  198.6 3.4 %copy-start.19 = (bf16[64,1024]{1,0:T(8,128)(2,1)S(1)}, bf16[64,1024]{1,0:T(8,128)(2,1)}, u32[]{:S(2)}) copy-start(bf16[64,1024]{1,0:T(8,128)(2,1)} %copy-done.18) | copy-start | bytes 393220
  198.7 16.6 %copy-start.2 = (bf16[2,2,256,1024]{3,2,1,0:T(8,128)(2,1)S(1)}, bf16[2,2,256,1024]{3,2,1,0:T(8,128)(2,1)}, u32[]{:S(2)}) copy-start(bf16[2,2,256,1024]{3,2,1,0:T(8,128)(2,1)} %copy-done.1) | copy-start | bytes 6291460
  200.4 14.9 %collective-permute-start.32 = (bf16[128,1024]{1,0:T(8,128)(2,1)S(1)}, bf16[128,1024]{1,0:T(8,128)(2,1)S(1)}, u32[]{:S(2)}, u32[]{:S(2)}) collective-permute-start(bf16[128,1024]{1,0:T(8,128)(2,1)S(1)} %fusion.6), channel_id=1, source_target_pairs={{0,16},{16,0},{1,17},{17,1},{2,18},{18,2},{3,19},{19,3},{4,20},{20... | collective-permute-start | bytes 786440 | tf_op jit(solution)/shard_map/ppermute | solution.py:25

commit v4 on v3

--- a/solution.py
+++ b/solution.py
@@ -52,14 +52,15 @@
     return stack
 
 
-def repacked(array, shape, moves):
+def repacked(array, shape, moves, kind=BF16):
     def kernel(source, target):
         for (r, c), (to_r, to_c), (high, wide) in moves:
-            target[pl.ds(to_r, high), pl.ds(to_c, wide)] = source[pl.ds(r, high), pl.ds(c, wide)]
+            block = source[pl.ds(r, high), pl.ds(c, wide)]
+            target[pl.ds(to_r, high), pl.ds(to_c, wide)] = block.astype(kind)
 
     return pl.pallas_call(
         kernel,
-        out_shape=jax.ShapeDtypeStruct(shape, array.dtype),
+        out_shape=jax.ShapeDtypeStruct(shape, kind),
         in_specs=[pl.BlockSpec(memory_space=pltpu.VMEM)],
         out_specs=pl.BlockSpec(memory_space=pltpu.VMEM),
         compiler_params=pltpu.CompilerParams(vmem_limit_bytes=16 << 20),
@@ -71,6 +72,10 @@
 
 def exchanged(array, axes):
     return lax.all_to_all(array, axes, split_axis=0, concat_axis=0, tiled=True)
+
+
+def after(values, *earlier):
+    return lax.optimization_barrier((values, earlier))[0]
 
 
 def dot(left, right, left_dim, right_dim):
@@ -124,9 +129,34 @@
         act_send = act_send.transpose(3, 2, 0, 1, 4).reshape(plane_rows, flat)
     part = value_projection_weight.shape[0] // groups
     weight_half = lax.dynamic_slice_in_dim(value_projection_weight, group * part, part, 0)
-    down_send = adapter_down_weight[0].T.reshape(rank, outer, inner, groups, piece)
-    down_send = lax.dynamic_index_in_dim(down_send, group, 3, keepdims=False)
-    down_send = down_send.transpose(2, 0, 1, 3).reshape(inner, rank, flat)
+    if aligned and rank % 16 == 0:
+
+        def pick(which, source, target):
+            for p in range(inner):
+                for o in range(outer):
+                    at = pl.multiple_of(((o * inner + p) * groups + which[0]) * piece, 128)
+                    target[pl.ds(p * rank, rank), pl.ds(o * piece, piece)] = source[
+                        :, pl.ds(at, piece)
+                    ]
+
+        down_send = pl.pallas_call(
+            pick,
+            out_shape=jax.ShapeDtypeStruct((inner * rank, flat), BF16),
+            in_specs=[
+                pl.BlockSpec(memory_space=pltpu.SMEM),
+                pl.BlockSpec(memory_space=pltpu.VMEM),
+            ],
+            out_specs=pl.BlockSpec(memory_space=pltpu.VMEM),
+            compiler_params=pltpu.CompilerParams(vmem_limit_bytes=16 << 20),
+            cost_estimate=pl.CostEstimate(
+                flops=0, bytes_accessed=3 * rank * width, transcendentals=0
+            ),
+        )(group.astype(jnp.int32)[None], adapter_down_weight[0].T)
+        down_send = down_send.reshape(inner, rank, flat)
+    else:
+        down_send = adapter_down_weight[0].T.reshape(rank, outer, inner, groups, piece)
+        down_send = lax.dynamic_index_in_dim(down_send, group, 3, keepdims=False)
+        down_send = down_send.transpose(2, 0, 1, 3).reshape(inner, rank, flat)
     down_block = []
     for other in range(inner):
         leaving = lax.dynamic_index_in_dim(down_send, place ^ other, 0, keepdims=False)
@@ -168,6 +198,7 @@
     label_rows = jnp.broadcast_to(row_job_labels.astype(BF16)[None], (16, rows))
     packet = jnp.concatenate([scaled, label_rows], axis=0)
     act_plane, packet, upstream = lax.optimization_barrier((act_plane, packet, upstream))
+    shares[outer // 2] = after(shares[outer // 2], packet)
     packets = jnp.stack(relative(packet, "z"))
 
     weight = placed([shares[by][0] for by in range(outer)], "z").reshape(flat, out_width)
@@ -225,9 +256,8 @@
     while bit:
         other = swapped(total, "q", bit)
         if bit == inner // 2:
-            *blocks, packets, back, other = lax.optimization_barrier(
-                (*blocks, packets, back, other)
-            )
+            packets = after(packets, back)
+            back = after(back, other)
         total = total + other
         bit //= 2
     back = exchanged(back, PLANE)
@@ -246,7 +276,7 @@
     up_part = (ADAPTER_SCALE * dot(wide, upstream_group, 1, 0)).reshape(outer, rank, out_width)
     up_grad = lax.dynamic_index_in_dim(up_part, level, 0, keepdims=False)
     up_send = up_part.astype(BF16)
-    *blocks, up_send = lax.optimization_barrier((*blocks, up_send))
+    packets = after(packets, up_send)
     up_got = []
     for by in range(1, outer):
         leaving = lax.dynamic_index_in_dim(up_send, (level + by) % outer, 0, keepdims=False)
@@ -272,7 +302,7 @@
             for g in range(groups)
         ]
     down_parts = jnp.concatenate(down_parts, axis=0)
-    down_parts, *up_got = lax.optimization_barrier((down_parts, *up_got))
+    down_parts = after(down_parts, up_got, back)
     for got in up_got:
         up_grad = up_grad + got.astype(F32)
 
@@ -295,8 +325,17 @@
     frozen = total
 
     down_parts = exchanged(down_parts, ("groups", "z", "q"))
-    down_parts = down_parts.reshape(groups, outer, inner, rank, piece)
-    down_grad = down_parts.transpose(3, 1, 2, 0, 4).reshape(rank, width).astype(F32).T
+    if aligned and rank % 16 == 0:
+        homes = []
+        for g in range(groups):
+            for j in range(jobs):
+                at = ((g * jobs + j) * rank, 0)
+                homes.append((at, (0, (j * groups + g) * piece), (rank, piece)))
+        down_grad = repacked(down_parts, (rank, width), homes, F32).T
+    else:
+        down_parts = down_parts.reshape(groups, outer, inner, rank, piece)
+        down_grad = down_parts.transpose(3, 1, 2, 0, 4).reshape(rank, width).astype(F32).T
+
     wide = spread(reduced_own, row_job_labels, up_jobs)
     projected = (frozen + ADAPTER_SCALE * dot(wide, up_all, 0, 0)).astype(BF16)
 

time: 232 us -> 225 us (0.970)
  waiting for transfers between devices: 112 us -> 96.6 us
  local copies, waits for them, and re-layouts: 31.9 us -> 22 us
  other arithmetic: 10.6 us -> 19.2 us
  starting transfers between devices: 51 us -> 55 us
  matrix products: 20.6 us -> 24.5 us
    ppermute x18, waiting for transfers between devices: 57.3 us -> 41.4 us  [shifted(): lax.ppermute(array, axis, [(i, (i + by) % peers) for i in range(peers)])]
    broadcast_in_dim x2 -> x0, local copies, waits for them, and re-layouts: 4.98 us -> none  [per_device(): return (projected, entering_derivative, down_grad[None], up_grad[None])]
    dot_general x15, matrix products: 20.6 us -> 24.5 us  [dot(): lax.dot_general(left, right, (((left_dim,), (right_dim,)), ((), ())), pre...]
    eq x11, other arithmetic: 0.17 us -> 3.49 us  [spread(): hit = keys[None, None, :] == wanted.astype(np.int32)[:, None, None]]
    ppermute x18, starting transfers between devices: 29 us -> 31.8 us  [shifted(): lax.ppermute(array, axis, [(i, (i + by) % peers) for i in range(peers)])]
    ppermute x15, waiting for transfers between devices: 38.6 us -> 41 us  [swapped(): return lax.ppermute(array, axis, [(i, i ^ bit) for i in range(peers)])]
    pallas_call x2 -> x4, Pallas kernels: 3.19 us -> 4.72 us  [the longest x3 4.65 us: repacked(): pl.pallas_call(kernel, out_shape=jax.ShapeDtypeStruct(shape, kind), in_sp...]
  transfers between devices with their start and end apart: 36 -> 36, of which waited for: 13 -> 13; matrix products, arithmetic and copies ran while one was open for 21% -> 25% of each run, Pallas kernels for 1% -> 1%
where the time goes in v4:
time: 225 us; the launch traced here: 224 us
  waiting for transfers between devices  96.6 us (43%)
  starting transfers between devices  55 us (24%)
  matrix products  24.5 us (11%)
  local copies, waits for them, and re-layouts  22 us (10%)
  other arithmetic  19.2 us (9%)
  Pallas kernels  4.72 us (2%)
    ppermute x18, waiting for transfers between devices, shifted(): lax.ppermute(array, axis, [(i, (i + by) % peers) for i in range(peers)])  41.4 us
    ppermute x15, waiting for transfers between devices, swapped(): return lax.ppermute(array, axis, [(i, i ^ bit) for i in range(peers)])  41 us
    ppermute x18, starting transfers between devices, shifted(): lax.ppermute(array, axis, [(i, (i + by) % peers) for i in range(peers)])  31.8 us
    dot_general x15, matrix products, dot(): lax.dot_general(left, right, (((left_dim,), (right_dim,)), ((), ())), pre...  24.5 us
    all_to_all x3, waiting for transfers between devices, exchanged(): return lax.all_to_all(array, axes, split_axis=0, concat_axis=0, tiled=True)  14.3 us
    unnamed x60, local copies, waits for them, and re-layouts  12.4 us
    all_to_all x3, starting transfers between devices, exchanged(): return lax.all_to_all(array, axes, split_axis=0, concat_axis=0, tiled=True)  12 us
    ppermute x15, starting transfers between devices, swapped(): return lax.ppermute(array, axis, [(i, i ^ bit) for i in range(peers)])  11.2 us
  transfers between devices with their start and end apart: 36, of which 13 were waited for; matrix products, arithmetic and copies ran while one was open for 25% of the time, Pallas kernels for 1%

profile of v4, /device:TPU:0, one launch (start us, length us, event | category | flops | bytes accessed | tf_op | source)
XLA Modules:
  0.0 223.7 jit_solution(17027057538907838927)
XLA Ops:
  0.6 3.1 %collective-permute-start.3 = (bf16[64,1024]{1,0:T(8,128)(2,1)}, bf16[64,1024]{1,0:T(8,128)(2,1)S(1)}, u32[]{:S(2)}, u32[]{:S(2)}) collective-permute-start(bf16[64,1024]{1,0:T(8,128)(2,1)} %bitcast.262), channel_id=1, source_target_pairs={{0,4},{4,8},{8,12},{12,0},{1,5},{5,9},{9,13},{13,1},{2,6},{6,10},{... | collective-permute-start | bytes 393224 | tf_op jit(solution)/shard_map/ppermute | solution.py:25
  3.7 2.6 %collective-permute-start.4 = (bf16[64,1024]{1,0:T(8,128)(2,1)}, bf16[64,1024]{1,0:T(8,128)(2,1)S(1)}, u32[]{:S(2)}, u32[]{:S(2)}) collective-permute-start(bf16[64,1024]{1,0:T(8,128)(2,1)} %bitcast.263), channel_id=1, source_target_pairs={{0,8},{4,12},{8,0},{12,4},{1,9},{5,13},{9,1},{13,5},{2,10},{6,14},... | collective-permute-start | bytes 393224 | tf_op jit(solution)/shard_map/ppermute | solution.py:25
  6.3 1.3 collective-permute-start.5
  7.7 1.2 copy-done.1
  9.6 1.5 collective-permute-start.1
  11.2 1.9 dynamic-slice_dynamic-update-slice_fusion
  13.8 1.6 shard_map.211
  17.2 3.7 %collective-permute-done.2 = bf16[64,1024]{1,0:T(8,128)(2,1)S(1)} collective-permute-done((bf16[64,1024]{1,0:T(8,128)(2,1)S(1)}, bf16[64,1024]{1,0:T(8,128)(2,1)S(1)}, u32[]{:S(2)}, u32[]{:S(2)}) %collective-permute-start.2) | collective-permute-done | bytes 131104 | tf_op jit(solution)/shard_map/ppermute | solution.py:20
  21.6 3.7 %all-to-all-start = ((bf16[8,128,1024]{2,1,0:T(8,128)(2,1)}), bf16[8,128,1024]{2,1,0:T(8,128)(2,1)S(1)}, u32[]{:S(2)}, u32[]{:S(2)}) async-start(bf16[8,128,1024]{2,1,0:T(8,128)(2,1)} %bitcast.9), calls=%async_computation | async-start | bytes 4194304 | tf_op jit(solution)/shard_map/all_to_all | solution.py:74
  27.6 3.2 %collective-permute-start.7 = (bf16[512,1024]{1,0:T(8,128)(2,1)}, bf16[512,1024]{1,0:T(8,128)(2,1)S(1)}, u32[]{:S(2)}, u32[]{:S(2)}) collective-permute-start(bf16[512,1024]{1,0:T(8,128)(2,1)} %get-tuple-element.26), channel_id=1, source_target_pairs={{0,12},{4,0},{8,4},{12,8},{1,13},{5,1},{9,5},{13,9},{2,14},{6,2},{... | collective-permute-start | bytes 3145736 | tf_op jit(solution)/shard_map/ppermute | solution.py:25
  32.7 1.8 collective-permute-start.8
  34.6 27.7 %collective-permute-done.8 = bf16[1,256,1024]{2,1,0:T(8,128)(2,1)} collective-permute-done((bf16[1,256,1024]{2,1,0:T(8,128)(2,1)}, bf16[1,256,1024]{2,1,0:T(8,128)(2,1)}, u32[]{:S(2)}, u32[]{:S(2)}) %collective-permute-start.8) | collective-permute-done | bytes 524320 | tf_op jit(solution)/shard_map/ppermute | solution.py:20
  62.3 13.1 %collective-permute-done.7 = bf16[512,1024]{1,0:T(8,128)(2,1)S(1)} collective-permute-done((bf16[512,1024]{1,0:T(8,128)(2,1)}, bf16[512,1024]{1,0:T(8,128)(2,1)S(1)}, u32[]{:S(2)}, u32[]{:S(2)}) %collective-permute-start.7) | collective-permute-done | bytes 1048608 | tf_op jit(solution)/shard_map/ppermute | solution.py:25
  75.4 1.0 copy-done.9
  76.4 1.4 select_bitcast_fusion.7
  77.8 1.1 maximum_bitcast_fusion
  80.8 1.3 slice_dynamic-update-slice_fusion
  82.5 3.6 %collective-permute-start.11 = (bf16[256,1024]{1,0:T(8,128)(2,1)S(1)}, bf16[256,1024]{1,0:T(8,128)(2,1)S(1)}, u32[]{:S(2)}, u32[]{:S(2)}) collective-permute-start(bf16[256,1024]{1,0:T(8,128)(2,1)S(1)} %slice.117), channel_id=1, source_target_pairs={{0,12},{4,0},{8,4},{12,8},{1,13},{5,1},{9,5},{13,9},{2,14},{6,2},{... | collective-permute-start | bytes 1572872 | tf_op jit(solution)/shard_map/ppermute | solution.py:25
  86.1 1.1 bitcast_dynamic-update-slice_fusion.2
  87.2 1.4 select_bitcast_fusion.3
  91.2 3.0 %collective-permute-start.16 = (bf16[80,128]{1,0:T(8,128)(2,1)S(1)}, bf16[80,128]{1,0:T(8,128)(2,1)S(1)}, u32[]{:S(2)}, u32[]{:S(2)}) collective-permute-start(bf16[80,128]{1,0:T(8,128)(2,1)S(1)} %pad_maximum_fusion.6), channel_id=1, source_target_pairs={{0,12},{4,0},{8,4},{12,8},{1,13},{5,1},{9,5},{13,9},{2,14},{6,2},{... | collective-permute-start | bytes 61448 | tf_op jit(solution)/shard_map/ppermute | solution.py:25
  94.2 4.6 %collective-permute-done.10 = bf16[256,1024]{1,0:T(8,128)(2,1)S(1)} collective-permute-done((bf16[256,1024]{1,0:T(8,128)(2,1)S(1)}, bf16[256,1024]{1,0:T(8,128)(2,1)S(1)}, u32[]{:S(2)}, u32[]{:S(2)}) %collective-permute-start.10) | collective-permute-done | bytes 524320 | tf_op jit(solution)/shard_map/ppermute | solution.py:25
  98.7 9.8 %collective-permute-done.11 = bf16[256,1024]{1,0:T(8,128)(2,1)S(1)} collective-permute-done((bf16[256,1024]{1,0:T(8,128)(2,1)S(1)}, bf16[256,1024]{1,0:T(8,128)(2,1)S(1)}, u32[]{:S(2)}, u32[]{:S(2)}) %collective-permute-start.11) | collective-permute-done | bytes 524320 | tf_op jit(solution)/shard_map/ppermute | solution.py:25
  108.6 1.8 collective-permute-start.20
  110.4 2.4 %fusion.36 = f32[1024,1024]{1,0:T(8,128)S(1)} fusion(bf16[1024,1024]{1,0:T(8,128)(2,1)S(1)} %constant_dynamic-update-slice_fusion.3, bf16[1024,1024]{1,0:T(8,128)(2,1)S(1)} %bitcast.225), kind=kOutput, calls=%fused_computation.162 | convolution fusion | flops 2147483648 | bytes 8388608 | tf_op jit(solution)/shard_map/dot_general | solution.py:82
  113.4 1.2 constant_dynamic-slice_fusion.2
  114.6 2.0 collective-permute-start.26
  116.6 1.8 collective-permute-start.28
  118.5 1.7 collective-permute-start.18
  120.2 2.4 %fusion.34 = f32[2,2,2,128,1024]{4,3,2,1,0:T(8,128)S(1)} fusion(bf16[2,2,2,128,1024]{4,3,2,1,0:T(8,128)(2,1)S(1)} %bitcast.227, bf16[1024,1024,1,1,1]{1,0,4,3,2:T(8,128)(2,1)S(1)} %bitcast.251), kind=kOutput, calls=%fused_computation.160 | convolution fusion | flops 2147483648 | bytes 8388608 | tf_op jit(solution)/shard_map/dot_general | solution.py:82
  122.8 1.0 collective-permute-done.18
  125.4 1.2 collective-permute-start.21
  128.1 1.5 collective-permute-start.23
  129.8 3.9 %collective-permute-done.23 = f32[64,512]{1,0:T(8,128)S(1)} collective-permute-done((f32[64,512]{1,0:T(8,128)S(1)}, f32[64,512]{1,0:T(8,128)S(1)}, u32[]{:S(2)}, u32[]{:S(2)}) %collective-permute-start.23) | collective-permute-done | bytes 131104 | tf_op jit(solution)/shard_map/ppermute | solution.py:25
  134.5 6.0 %collective-permute-done.21 = bf16[2,128,1024]{2,1,0:T(8,128)(2,1)} collective-permute-done((bf16[2,128,1024]{2,1,0:T(8,128)(2,1)}, bf16[2,128,1024]{2,1,0:T(8,128)(2,1)}, u32[]{:S(2)}, u32[]{:S(2)}) %collective-permute-start.21) | collective-permute-done | bytes 524320 | tf_op jit(solution)/shard_map/ppermute | solution.py:20
  140.5 1.3 select_bitcast_fusion.5
  142.6 2.2 collective-permute-done.25
  144.8 1.4 collective-permute-start.27
  146.3 1.6 bitcast_add_fusion
  148.0 1.2 collective-permute-start.13
  150.3 1.0 copy-done.6
  151.8 2.4 %fusion.35 = f32[1024,1024]{1,0:T(8,128)S(1)} fusion(bf16[1024,1024]{1,0:T(8,128)(2,1)S(1)} %bitcast.233, bf16[1024,1024]{1,0:T(8,128)(2,1)S(1)} %bitcast.252), kind=kOutput, calls=%fused_computation.161 | convolution fusion | flops 2147483648 | bytes 8388608 | tf_op jit(solution)/shard_map/dot_general | solution.py:82
  154.2 3.9 %add_convert_fusion = bf16[1024,1024]{1,0:T(8,128)(2,1)} fusion(f32[1024,1024]{1,0:T(8,128)S(1)} %fusion.35, bf16[1024,1024]{1,0:T(8,128)(2,1)S(1)} %bitcast.254, bf16[1024,1024]{1,0:T(8,128)(2,1)S(1)} %copy-done.23), kind=kOutput, calls=%fused_computation.1 | convolution fusion | flops 2149580800 | bytes 10485760 | tf_op jit(solution)/shard_map/dot_general | solution.py:82
  161.4 3.8 %all-to-all-start.1 = ((bf16[8,128,1024]{2,1,0:T(8,128)(2,1)}), bf16[8,128,1024]{2,1,0:T(8,128)(2,1)S(1)}, u32[]{:S(2)}, u32[]{:S(2)}) async-start(bf16[8,128,1024]{2,1,0:T(8,128)(2,1)} %bitcast.253), calls=%async_computation.1 | async-start | bytes 4194304 | tf_op jit(solution)/shard_map/all_to_all | solution.py:74
  168.9 1.4 fusion.19
  170.6 1.4 fusion.13
  172.0 3.0 %collective-permute-start.30 = (bf16[64,1024]{1,0:T(8,128)(2,1)S(1)}, bf16[64,1024]{1,0:T(8,128)(2,1)S(1)}, u32[]{:S(2)}, u32[]{:S(2)}) collective-permute-start(bf16[64,1024]{1,0:T(8,128)(2,1)S(1)} %copy-done.20), channel_id=1, source_target_pairs={{0,8},{4,12},{8,0},{12,4},{1,9},{5,13},{9,1},{13,5},{2,10},{6,14},... | collective-permute-start | bytes 393224 | tf_op jit(solution)/shard_map/ppermute | solution.py:25
  175.0 1.4 fusion.15
  176.5 1.4 fusion.9
  178.8 1.4 convolution_add_fusion.3
  180.3 1.4 convolution_add_fusion.1
  181.7 1.4 fusion.2
  183.1 1.4 fusion.3
  184.4 1.0 pad_maximum_fusion.3
  185.5 5.2 %all-to-all-done.1 = bf16[8,128,1024]{2,1,0:T(8,128)(2,1)S(1)} async-done(((bf16[8,128,1024]{2,1,0:T(8,128)(2,1)}), bf16[8,128,1024]{2,1,0:T(8,128)(2,1)S(1)}, u32[]{:S(2)}, u32[]{:S(2)}) %all-to-all-start.1) | async-done | bytes 2097184 | tf_op jit(solution)/shard_map/all_to_all | solution.py:74
  190.6 4.4 %all-to-all-start.2 = ((bf16[32,64,256]{2,1,0:T(8,128)(2,1)}), bf16[32,64,256]{2,1,0:T(8,128)(2,1)S(1)}, u32[]{:S(2)}, u32[]{:S(2)}) async-start(bf16[32,64,256]{2,1,0:T(8,128)(2,1)} %bitcast.237), calls=%async_computation.2 | async-start | bytes 2097152 | tf_op jit(solution)/shard_map/all_to_all | solution.py:74
  195.1 1.6 convert_add_fusion
  196.7 1.8 collective-permute-start.32
  198.6 1.9 fusion.23
  200.5 1.6 shard_map.212
  202.1 9.9 %collective-permute-done.32 = bf16[128,1024]{1,0:T(8,128)(2,1)S(1)} collective-permute-done((bf16[128,1024]{1,0:T(8,128)(2,1)S(1)}, bf16[128,1024]{1,0:T(8,128)(2,1)S(1)}, u32[]{:S(2)}, u32[]{:S(2)}) %collective-permute-start.32) | collective-permute-done | bytes 262176 | tf_op jit(solution)/shard_map/ppermute | solution.py:25
  212.0 1.2 fusion.7
  213.2 9.1 %all-to-all-done.2 = bf16[32,64,256]{2,1,0:T(8,128)(2,1)S(1)} async-done(((bf16[32,64,256]{2,1,0:T(8,128)(2,1)}), bf16[32,64,256]{2,1,0:T(8,128)(2,1)S(1)}, u32[]{:S(2)}, u32[]{:S(2)}) %all-to-all-start.2) | async-done | bytes 1048608 | tf_op jit(solution)/shard_map/all_to_all | solution.py:74
  222.3 1.5 shard_map.213
  (174 shorter events, 28.4 us)
Async XLA Ops:
  0.6 13.2 %copy-start = (bf16[128,8192]{1,0:T(8,128)(2,1)S(1)}, bf16[128,8192]{1,0:T(8,128)(2,1)}, u32[]{:S(2)}) copy-start(bf16[128,8192]{1,0:T(8,128)(2,1)} %source.1) | copy-start | bytes 6291460
  0.6 20.9 %collective-permute-start.3 = (bf16[64,1024]{1,0:T(8,128)(2,1)}, bf16[64,1024]{1,0:T(8,128)(2,1)S(1)}, u32[]{:S(2)}, u32[]{:S(2)}) collective-permute-start(bf16[64,1024]{1,0:T(8,128)(2,1)} %bitcast.262), channel_id=1, source_target_pairs={{0,4},{4,8},{8,12},{12,0},{1,5},{5,9},{9,13},{13,1},{2,6},{6,10},{... | collective-permute-start | bytes 393224 | tf_op jit(solution)/shard_map/ppermute | solution.py:25
  3.7 17.9 %collective-permute-start.4 = (bf16[64,1024]{1,0:T(8,128)(2,1)}, bf16[64,1024]{1,0:T(8,128)(2,1)S(1)}, u32[]{:S(2)}, u32[]{:S(2)}) collective-permute-start(bf16[64,1024]{1,0:T(8,128)(2,1)} %bitcast.263), channel_id=1, source_target_pairs={{0,8},{4,12},{8,0},{12,4},{1,9},{5,13},{9,1},{13,5},{2,10},{6,14},... | collective-permute-start | bytes 393224 | tf_op jit(solution)/shard_map/ppermute | solution.py:25
  6.3 15.3 %collective-permute-start.5 = (bf16[64,1024]{1,0:T(8,128)(2,1)}, bf16[64,1024]{1,0:T(8,128)(2,1)S(1)}, u32[]{:S(2)}, u32[]{:S(2)}) collective-permute-start(bf16[64,1024]{1,0:T(8,128)(2,1)} %bitcast.264), channel_id=1, source_target_pairs={{0,12},{4,0},{8,4},{12,8},{1,13},{5,1},{9,5},{13,9},{2,14},{6,2},{... | collective-permute-start | bytes 393224 | tf_op jit(solution)/shard_map/ppermute | solution.py:25
  7.7 1.2 copy-start.1
  9.6 5.7 %collective-permute-start = (bf16[64,1024]{1,0:T(8,128)(2,1)}, bf16[64,1024]{1,0:T(8,128)(2,1)S(1)}, u32[]{:S(2)}, u32[]{:S(2)}) collective-permute-start(bf16[64,1024]{1,0:T(8,128)(2,1)} %get-tuple-element.74), channel_id=1, source_target_pairs={{0,1},{1,0},{2,3},{3,2},{4,5},{5,4},{6,7},{7,6},{8,9},{9,8},{10,11... | collective-permute-start | bytes 393224 | tf_op jit(solution)/shard_map/ppermute | solution.py:20
  9.6 6.8 %collective-permute-start.1 = (bf16[64,1024]{1,0:T(8,128)(2,1)S(1)}, bf16[64,1024]{1,0:T(8,128)(2,1)S(1)}, u32[]{:S(2)}, u32[]{:S(2)}) collective-permute-start(bf16[64,1024]{1,0:T(8,128)(2,1)S(1)} %get-tuple-element.73), channel_id=1, source_target_pairs={{0,2},{1,3},{2,0},{3,1},{4,6},{5,7},{6,4},{7,5},{8,10},{9,11},{10,... | collective-permute-start | bytes 393224 | tf_op jit(solution)/shard_map/ppermute | solution.py:20
  15.4 5.5 %collective-permute-start.2 = (bf16[64,1024]{1,0:T(8,128)(2,1)S(1)}, bf16[64,1024]{1,0:T(8,128)(2,1)S(1)}, u32[]{:S(2)}, u32[]{:S(2)}) collective-permute-start(bf16[64,1024]{1,0:T(8,128)(2,1)S(1)} %get-tuple-element.72), channel_id=1, source_target_pairs={{0,3},{1,2},{2,1},{3,0},{4,7},{5,6},{6,5},{7,4},{8,11},{9,10},{10,... | collective-permute-start | bytes 393224 | tf_op jit(solution)/shard_map/ppermute | solution.py:20
  21.6 4.7 %copy-start.18 = (bf16[1,64,1024]{2,1,0:T(8,128)(2,1)S(1)}, bf16[1,64,1024]{2,1,0:T(8,128)(2,1)}, u32[]{:S(2)}) copy-start(bf16[1,64,1024]{2,1,0:T(8,128)(2,1)} %param.24) | copy-start | bytes 393220
  21.6 53.8 %all-to-all-start = ((bf16[8,128,1024]{2,1,0:T(8,128)(2,1)}), bf16[8,128,1024]{2,1,0:T(8,128)(2,1)S(1)}, u32[]{:S(2)}, u32[]{:S(2)}) async-start(bf16[8,128,1024]{2,1,0:T(8,128)(2,1)} %bitcast.9), calls=%async_computation | async-start | bytes 4194304 | tf_op jit(solution)/shard_map/all_to_all | solution.py:74
  27.0 35.3 %collective-permute-start.6 = (bf16[512,1024]{1,0:T(8,128)(2,1)}, bf16[512,1024]{1,0:T(8,128)(2,1)}, u32[]{:S(2)}, u32[]{:S(2)}) collective-permute-start(bf16[512,1024]{1,0:T(8,128)(2,1)} %get-tuple-element.26), channel_id=1, source_target_pairs={{0,4},{4,8},{8,12},{12,0},{1,5},{5,9},{9,13},{13,1},{2,6},{6,10},{... | collective-permute-start | bytes 3145736 | tf_op jit(solution)/shard_map/ppermute | solution.py:25
  27.6 47.8 %collective-permute-start.7 = (bf16[512,1024]{1,0:T(8,128)(2,1)}, bf16[512,1024]{1,0:T(8,128)(2,1)S(1)}, u32[]{:S(2)}, u32[]{:S(2)}) collective-permute-start(bf16[512,1024]{1,0:T(8,128)(2,1)} %get-tuple-element.26), channel_id=1, source_target_pairs={{0,12},{4,0},{8,4},{12,8},{1,13},{5,1},{9,5},{13,9},{2,14},{6,2},{... | collective-permute-start | bytes 3145736 | tf_op jit(solution)/shard_map/ppermute | solution.py:25
  32.7 29.6 %collective-permute-start.8 = (bf16[1,256,1024]{2,1,0:T(8,128)(2,1)}, bf16[1,256,1024]{2,1,0:T(8,128)(2,1)}, u32[]{:S(2)}, u32[]{:S(2)}) collective-permute-start(bf16[1,256,1024]{2,1,0:T(8,128)(2,1)} %bitcast.14), channel_id=1, source_target_pairs={{0,2},{1,3},{2,0},{3,1},{4,6},{5,7},{6,4},{7,5},{8,10},{9,11},{10,... | collective-permute-start | bytes 1572872 | tf_op jit(solution)/shard_map/ppermute | solution.py:20
  75.4 1.0 copy-start.9
  75.4 44.8 %copy-start.4 = (bf16[8,128,1024]{2,1,0:T(8,128)(2,1)}, bf16[8,128,1024]{2,1,0:T(8,128)(2,1)S(1)}, u32[]{:S(2)}) copy-start(bf16[8,128,1024]{2,1,0:T(8,128)(2,1)S(1)} %all-to-all-done) | copy-start | bytes 6291460
  76.4 2.5 %copy-start.24 = (s32[128]{0:T(128)S(1)}, s32[128]{0:T(128)}, u32[]{:S(2)}) copy-start(s32[128]{0:T(128)} %param.21) | copy-start | bytes 1540
  78.8 1.4 copy-start.25
  78.8 8.3 %collective-permute-start.9 = (bf16[2,256,1024]{2,1,0:T(8,128)(2,1)}, bf16[2,256,1024]{2,1,0:T(8,128)(2,1)}, u32[]{:S(2)}, u32[]{:S(2)}) collective-permute-start(bf16[2,256,1024]{2,1,0:T(8,128)(2,1)} %maximum_bitcast_fusion), channel_id=1, source_target_pairs={{0,1},{1,0},{2,3},{3,2},{4,5},{5,4},{6,7},{7,6},{8,9},{9,8},{10,11... | collective-permute-start | bytes 3145736 | tf_op jit(solution)/shard_map/ppermute | solution.py:20
  78.9 1.2 copy-start.13
  78.9 1.9 copy-start.21
  80.1 2.3 %copy-start.10 = (bf16[512,1024]{1,0:T(8,128)(2,1)S(1)}, bf16[512,1024]{1,0:T(8,128)(2,1)}, u32[]{:S(2)}) copy-start(bf16[512,1024]{1,0:T(8,128)(2,1)} %copy-done.9) | copy-start | bytes 3145732
  82.1 16.6 %collective-permute-start.10 = (bf16[256,1024]{1,0:T(8,128)(2,1)S(1)}, bf16[256,1024]{1,0:T(8,128)(2,1)S(1)}, u32[]{:S(2)}, u32[]{:S(2)}) collective-permute-start(bf16[256,1024]{1,0:T(8,128)(2,1)S(1)} %get-tuple-element.54), channel_id=1, source_target_pairs={{0,4},{4,8},{8,12},{12,0},{1,5},{5,9},{9,13},{13,1},{2,6},{6,10},{... | collective-permute-start | bytes 1572872 | tf_op jit(solution)/shard_map/ppermute | solution.py:25
  82.5 26.1 %collective-permute-start.11 = (bf16[256,1024]{1,0:T(8,128)(2,1)S(1)}, bf16[256,1024]{1,0:T(8,128)(2,1)S(1)}, u32[]{:S(2)}, u32[]{:S(2)}) collective-permute-start(bf16[256,1024]{1,0:T(8,128)(2,1)S(1)} %slice.117), channel_id=1, source_target_pairs={{0,12},{4,0},{8,4},{12,8},{1,13},{5,1},{9,5},{13,9},{2,14},{6,2},{... | collective-permute-start | bytes 1572872 | tf_op jit(solution)/shard_map/ppermute | solution.py:25
  88.5 1.0 copy-start.14
  88.7 19.8 %copy-start.2 = (bf16[2,2,256,1024]{3,2,1,0:T(8,128)(2,1)}, bf16[2,2,256,1024]{3,2,1,0:T(8,128)(2,1)S(1)}, u32[]{:S(2)}) copy-start(bf16[2,2,256,1024]{3,2,1,0:T(8,128)(2,1)S(1)} %pad_maximum_fusion) | copy-start | bytes 6291460
  90.3 22.7 %collective-permute-start.14 = (bf16[80,128]{1,0:T(8,128)(2,1)S(1)}, bf16[80,128]{1,0:T(8,128)(2,1)S(1)}, u32[]{:S(2)}, u32[]{:S(2)}) collective-permute-start(bf16[80,128]{1,0:T(8,128)(2,1)S(1)} %pad_maximum_fusion.6), channel_id=1, source_target_pairs={{0,4},{4,8},{8,12},{12,0},{1,5},{5,9},{9,13},{13,1},{2,6},{6,10},{... | collective-permute-start | bytes 61448 | tf_op jit(solution)/shard_map/ppermute | solution.py:25
  90.3 22.6 %collective-permute-start.15 = (bf16[80,128]{1,0:T(8,128)(2,1)S(1)}, bf16[80,128]{1,0:T(8,128)(2,1)S(1)}, u32[]{:S(2)}, u32[]{:S(2)}) collective-permute-start(bf16[80,128]{1,0:T(8,128)(2,1)S(1)} %pad_maximum_fusion.6), channel_id=1, source_target_pairs={{0,8},{4,12},{8,0},{12,4},{1,9},{5,13},{9,1},{13,5},{2,10},{6,14},... | collective-permute-start | bytes 61448 | tf_op jit(solution)/shard_map/ppermute | solution.py:25
  91.2 21.8 %collective-permute-start.16 = (bf16[80,128]{1,0:T(8,128)(2,1)S(1)}, bf16[80,128]{1,0:T(8,128)(2,1)S(1)}, u32[]{:S(2)}, u32[]{:S(2)}) collective-permute-start(bf16[80,128]{1,0:T(8,128)(2,1)S(1)} %pad_maximum_fusion.6), channel_id=1, source_target_pairs={{0,12},{4,0},{8,4},{12,8},{1,13},{5,1},{9,5},{13,9},{2,14},{6,2},{... | collective-permute-start | bytes 61448 | tf_op jit(solution)/shard_map/ppermute | solution.py:25
  108.6 4.2 %copy-start.22 = (bf16[1024,1024]{1,0:T(8,128)(2,1)}, bf16[1024,1024]{1,0:T(8,128)(2,1)S(1)}, u32[]{:S(2)}) copy-start(bf16[1024,1024]{1,0:T(8,128)(2,1)S(1)} %constant_dynamic-update-slice_fusion.3) | copy-start | bytes 6291460
  108.6 15.4 %collective-permute-start.20 = (bf16[1,128,1024]{2,1,0:T(8,128)(2,1)S(1)}, bf16[1,128,1024]{2,1,0:T(8,128)(2,1)S(1)}, u32[]{:S(2)}, u32[]{:S(2)}) collective-permute-start(bf16[1,128,1024]{2,1,0:T(8,128)(2,1)S(1)} %bitcast.259), channel_id=1, source_target_pairs={{0,16},{16,0},{1,17},{17,1},{2,18},{18,2},{3,19},{19,3},{4,20},{20... | collective-permute-start | bytes 786440 | tf_op jit(solution)/shard_map/ppermute | solution.py:20
  112.9 9.6 %copy-start.11 = (bf16[4,256,1024]{2,1,0:T(8,128)(2,1)}, bf16[4,256,1024]{2,1,0:T(8,128)(2,1)S(1)}, u32[]{:S(2)}) copy-start(bf16[4,256,1024]{2,1,0:T(8,128)(2,1)S(1)} %bitcast_dynamic-update-slice_fusion) | copy-start | bytes 6291460
  113.0 5.4 %collective-permute-start.17 = (bf16[1,4,80,128]{3,2,1,0:T(8,128)(2,1)S(1)}, bf16[1,4,80,128]{3,2,1,0:T(8,128)(2,1)S(1)}, u32[]{:S(2)}, u32[]{:S(2)}) collective-permute-start(bf16[1,4,80,128]{3,2,1,0:T(8,128)(2,1)S(1)} %maximum_bitcast_fusion.3), channel_id=1, source_target_pairs={{0,16},{16,0},{1,17},{17,1},{2,18},{18,2},{3,19},{19,3},{4,20},{20... | collective-permute-start | bytes 245768 | tf_op jit(solution)/shard_map/ppermute | solution.py:20
  114.6 63.3 %collective-permute-start.26 = (bf16[1024,256]{1,0:T(8,128)(2,1)}, bf16[1024,256]{1,0:T(8,128)(2,1)}, u32[]{:S(2)}, u32[]{:S(2)}) collective-permute-start(bf16[1024,256]{1,0:T(8,128)(2,1)} %get-tuple-element.48), channel_id=1, source_target_pairs={{0,4},{4,8},{8,12},{12,0},{1,5},{5,9},{9,13},{13,1},{2,6},{6,10},{... | collective-permute-start | bytes 1572872 | tf_op jit(solution)/shard_map/ppermute | solution.py:25
  116.6 55.4 %collective-permute-start.28 = (bf16[1024,256]{1,0:T(8,128)(2,1)}, bf16[1024,256]{1,0:T(8,128)(2,1)}, u32[]{:S(2)}, u32[]{:S(2)}) collective-permute-start(bf16[1024,256]{1,0:T(8,128)(2,1)} %get-tuple-element.47), channel_id=1, source_target_pairs={{0,12},{4,0},{8,4},{12,8},{1,13},{5,1},{9,5},{13,9},{2,14},{6,2},{... | collective-permute-start | bytes 1572872 | tf_op jit(solution)/shard_map/ppermute | solution.py:25
  118.5 5.4 %collective-permute-start.18 = (bf16[2,4,80,128]{3,2,1,0:T(8,128)(2,1)S(1)}, bf16[2,4,80,128]{3,2,1,0:T(8,128)(2,1)S(1)}, u32[]{:S(2)}, u32[]{:S(2)}) collective-permute-start(bf16[2,4,80,128]{3,2,1,0:T(8,128)(2,1)S(1)} %maximum_bitcast_fusion.2), channel_id=1, source_target_pairs={{0,2},{1,3},{2,0},{3,1},{4,6},{5,7},{6,4},{7,5},{8,10},{9,11},{10,... | collective-permute-start | bytes 491528 | tf_op jit(solution)/shard_map/ppermute | solution.py:20
  122.6 2.0 copy-start.7
  122.7 23.5 %collective-permute-start.12 = (bf16[2,2,128,1024]{3,2,1,0:T(8,128)(2,1)S(1)}, bf16[2,2,128,1024]{3,2,1,0:T(8,128)(2,1)}, u32[]{:S(2)}, u32[]{:S(2)}) collective-permute-start(bf16[2,2,128,1024]{3,2,1,0:T(8,128)(2,1)S(1)} %fusion.4), channel_id=1, source_target_pairs={{0,1},{1,0},{2,3},{3,2},{4,5},{5,4},{6,7},{7,6},{8,9},{9,8},{10,11... | collective-permute-start | bytes 3145736 | tf_op jit(solution)/shard_map/ppermute | solution.py:20
  124.0 2.6 %collective-permute-start.19 = (bf16[4,4,80,128]{3,2,1,0:T(8,128)(2,1)S(1)}, bf16[4,4,80,128]{3,2,1,0:T(8,128)(2,1)S(1)}, u32[]{:S(2)}, u32[]{:S(2)}) collective-permute-start(bf16[4,4,80,128]{3,2,1,0:T(8,128)(2,1)S(1)} %bitcast.256), channel_id=1, source_target_pairs={{0,1},{1,0},{2,3},{3,2},{4,5},{5,4},{6,7},{7,6},{8,9},{9,8},{10,11... | collective-permute-start | bytes 983048 | tf_op jit(solution)/shard_map/ppermute | solution.py:20
  125.4 15.1 %collective-permute-start.21 = (bf16[2,128,1024]{2,1,0:T(8,128)(2,1)}, bf16[2,128,1024]{2,1,0:T(8,128)(2,1)}, u32[]{:S(2)}, u32[]{:S(2)}) collective-permute-start(bf16[2,128,1024]{2,1,0:T(8,128)(2,1)} %maximum_bitcast_fusion.1), channel_id=1, source_target_pairs={{0,2},{1,3},{2,0},{3,1},{4,6},{5,7},{6,4},{7,5},{8,10},{9,11},{10,... | collective-permute-start | bytes 1572872 | tf_op jit(solution)/shard_map/ppermute | solution.py:20
  128.1 5.7 %collective-permute-start.23 = (f32[64,512]{1,0:T(8,128)S(1)}, f32[64,512]{1,0:T(8,128)S(1)}, u32[]{:S(2)}, u32[]{:S(2)}) collective-permute-start(f32[64,512]{1,0:T(8,128)S(1)} %bitcast.265), channel_id=1, source_target_pairs={{0,16},{16,0},{1,17},{17,1},{2,18},{18,2},{3,19},{19,3},{4,20},{20... | collective-permute-start | bytes 393224 | tf_op jit(solution)/shard_map/ppermute | solution.py:25
  133.8 8.5 %collective-permute-start.24 = (f32[64,512]{1,0:T(8,128)S(1)}, f32[64,512]{1,0:T(8,128)S(1)}, u32[]{:S(2)}, u32[]{:S(2)}) collective-permute-start(f32[64,512]{1,0:T(8,128)S(1)} %bitcast_add_fusion.3), channel_id=1, source_target_pairs={{0,2},{1,3},{2,0},{3,1},{4,6},{5,7},{6,4},{7,5},{8,10},{9,11},{10,... | collective-permute-start | bytes 393224 | tf_op jit(solution)/shard_map/ppermute | solution.py:20
  140.5 5.8 %copy-start.8 = (f32[2,2,2,128,1024]{4,3,2,1,0:T(8,128)S(1)}, f32[2,2,2,128,1024]{4,3,2,1,0:T(8,128)}, u32[]{:S(2)}) copy-start(f32[2,2,2,128,1024]{4,3,2,1,0:T(8,128)} %copy-done.7) | copy-start | bytes 12582916
  141.9 7.3 %collective-permute-start.22 = (bf16[4,128,1024]{2,1,0:T(8,128)(2,1)S(1)}, bf16[4,128,1024]{2,1,0:T(8,128)(2,1)S(1)}, u32[]{:S(2)}, u32[]{:S(2)}) collective-permute-start(bf16[4,128,1024]{2,1,0:T(8,128)(2,1)S(1)} %bitcast.234), channel_id=1, source_target_pairs={{0,1},{1,0},{2,3},{3,2},{4,5},{5,4},{6,7},{7,6},{8,9},{9,8},{10,11... | collective-permute-start | bytes 3145736 | tf_op jit(solution)/shard_map/ppermute | solution.py:20
  142.3 2.5 %collective-permute-start.25 = (f32[64,512]{1,0:T(8,128)S(1)}, f32[64,512]{1,0:T(8,128)S(1)}, u32[]{:S(2)}, u32[]{:S(2)}) collective-permute-start(f32[64,512]{1,0:T(8,128)S(1)} %add.252), channel_id=1, source_target_pairs={{0,1},{1,0},{2,3},{3,2},{4,5},{5,4},{6,7},{7,6},{8,9},{9,8},{10,11... | collective-permute-start | bytes 393224 | tf_op jit(solution)/shard_map/ppermute | solution.py:20
  144.8 36.9 %collective-permute-start.27 = (bf16[1024,256]{1,0:T(8,128)(2,1)S(1)}, bf16[1024,256]{1,0:T(8,128)(2,1)}, u32[]{:S(2)}, u32[]{:S(2)}) collective-permute-start(bf16[1024,256]{1,0:T(8,128)(2,1)S(1)} %get-tuple-element.46), channel_id=1, source_target_pairs={{0,8},{4,12},{8,0},{12,4},{1,9},{5,13},{9,1},{13,5},{2,10},{6,14},... | collective-permute-start | bytes 1572872 | tf_op jit(solution)/shard_map/ppermute | solution.py:25
  147.9 1.5 copy-start.5
  148.0 42.7 %collective-permute-start.13 = (bf16[2,1,128,1024]{3,2,1,0:T(8,128)(2,1)S(1)}, bf16[2,1,128,1024]{3,2,1,0:T(8,128)(2,1)}, u32[]{:S(2)}, u32[]{:S(2)}) collective-permute-start(bf16[2,1,128,1024]{3,2,1,0:T(8,128)(2,1)S(1)} %dynamic-slice_convert_fusion.1), channel_id=1, source_target_pairs={{0,2},{1,3},{2,0},{3,1},{4,6},{5,7},{6,4},{7,5},{8,10},{9,11},{10,... | collective-permute-start | bytes 1572872 | tf_op jit(solution)/shard_map/ppermute | solution.py:20
  149.9 1.9 copy-start.12
  150.3 1.0 copy-start.6
  151.8 2.4 %copy-start.23 = (bf16[1024,1024]{1,0:T(8,128)(2,1)S(1)}, bf16[1024,1024]{1,0:T(8,128)(2,1)}, u32[]{:S(2)}) copy-start(bf16[1024,1024]{1,0:T(8,128)(2,1)} %copy-done.22) | copy-start | bytes 6291460
  160.7 24.7 %collective-permute-start.29 = (bf16[64,1024]{1,0:T(8,128)(2,1)}, bf16[64,1024]{1,0:T(8,128)(2,1)}, u32[]{:S(2)}, u32[]{:S(2)}) collective-permute-start(bf16[64,1024]{1,0:T(8,128)(2,1)} %get-tuple-element.67), channel_id=1, source_target_pairs={{0,4},{4,8},{8,12},{12,0},{1,5},{5,9},{9,13},{13,1},{2,6},{6,10},{... | collective-permute-start | bytes 393224 | tf_op jit(solution)/shard_map/ppermute | solution.py:25
  161.4 29.2 %all-to-all-start.1 = ((bf16[8,128,1024]{2,1,0:T(8,128)(2,1)}), bf16[8,128,1024]{2,1,0:T(8,128)(2,1)S(1)}, u32[]{:S(2)}, u32[]{:S(2)}) async-start(bf16[8,128,1024]{2,1,0:T(8,128)(2,1)} %bitcast.253), calls=%async_computation.1 | async-start | bytes 4194304 | tf_op jit(solution)/shard_map/all_to_all | solution.py:74
  165.2 3.6 %copy-start.17 = (bf16[64,512]{1,0:T(8,128)(2,1)S(1)}, bf16[64,512]{1,0:T(8,128)(2,1)}, u32[]{:S(2)}) copy-start(bf16[64,512]{1,0:T(8,128)(2,1)} %get-tuple-element.87) | copy-start | bytes 196612
  168.7 1.6 copy-start.16
  168.9 1.6 copy-start.15
  170.4 1.6 copy-start.20
  172.0 13.4 %collective-permute-start.30 = (bf16[64,1024]{1,0:T(8,128)(2,1)S(1)}, bf16[64,1024]{1,0:T(8,128)(2,1)S(1)}, u32[]{:S(2)}, u32[]{:S(2)}) collective-permute-start(bf16[64,1024]{1,0:T(8,128)(2,1)S(1)} %copy-done.20), channel_id=1, source_target_pairs={{0,8},{4,12},{8,0},{12,4},{1,9},{5,13},{9,1},{13,5},{2,10},{6,14},... | collective-permute-start | bytes 393224 | tf_op jit(solution)/shard_map/ppermute | solution.py:25
  176.4 1.5 copy-start.19
  177.9 7.5 %collective-permute-start.31 = (bf16[64,1024]{1,0:T(8,128)(2,1)S(1)}, bf16[64,1024]{1,0:T(8,128)(2,1)}, u32[]{:S(2)}, u32[]{:S(2)}) collective-permute-start(bf16[64,1024]{1,0:T(8,128)(2,1)S(1)} %copy-done.19), channel_id=1, source_target_pairs={{0,12},{4,0},{8,4},{12,8},{1,13},{5,1},{9,5},{13,9},{2,14},{6,2},{... | collective-permute-start | bytes 393224 | tf_op jit(solution)/shard_map/ppermute | solution.py:25
  190.6 31.6 %all-to-all-start.2 = ((bf16[32,64,256]{2,1,0:T(8,128)(2,1)}), bf16[32,64,256]{2,1,0:T(8,128)(2,1)S(1)}, u32[]{:S(2)}, u32[]{:S(2)}) async-start(bf16[32,64,256]{2,1,0:T(8,128)(2,1)} %bitcast.237), calls=%async_computation.2 | async-start | bytes 2097152 | tf_op jit(solution)/shard_map/all_to_all | solution.py:74
  196.7 15.3 %collective-permute-start.32 = (bf16[128,1024]{1,0:T(8,128)(2,1)S(1)}, bf16[128,1024]{1,0:T(8,128)(2,1)S(1)}, u32[]{:S(2)}, u32[]{:S(2)}) collective-permute-start(bf16[128,1024]{1,0:T(8,128)(2,1)S(1)} %fusion.8), channel_id=1, source_target_pairs={{0,16},{16,0},{1,17},{17,1},{2,18},{18,2},{3,19},{19,3},{4,20},{20... | collective-permute-start | bytes 786440 | tf_op jit(solution)/shard_map/ppermute | solution.py:25
  200.5 11.5 %copy-start.3 = (bf16[2,2,256,1024]{3,2,1,0:T(8,128)(2,1)S(1)}, bf16[2,2,256,1024]{3,2,1,0:T(8,128)(2,1)}, u32[]{:S(2)}) copy-start(bf16[2,2,256,1024]{3,2,1,0:T(8,128)(2,1)} %copy-done.2) | copy-start | bytes 6291460

commit v5 on v4

--- a/solution.py
+++ b/solution.py
@@ -198,7 +198,6 @@
     label_rows = jnp.broadcast_to(row_job_labels.astype(BF16)[None], (16, rows))
     packet = jnp.concatenate([scaled, label_rows], axis=0)
     act_plane, packet, upstream = lax.optimization_barrier((act_plane, packet, upstream))
-    shares[outer // 2] = after(shares[outer // 2], packet)
     packets = jnp.stack(relative(packet, "z"))
 
     weight = placed([shares[by][0] for by in range(outer)], "z").reshape(flat, out_width)

time: 225 us -> 221 us (0.982)
    ppermute x18, waiting for transfers between devices: 41.4 us -> 44 us  [shifted(): lax.ppermute(array, axis, [(i, (i + by) % peers) for i in range(peers)])]
  transfers between devices with their start and end apart: 36 -> 36, of which waited for: 13 -> 13; matrix products, arithmetic and copies ran while one was open for 25% -> 26% of each run, Pallas kernels for 1% -> 1%
where the time goes in v5:
time: 221 us; the launch traced here: 220 us
  waiting for transfers between devices  97.3 us (44%)
  starting transfers between devices  53.2 us (24%)
  matrix products  24.4 us (11%)
  local copies, waits for them, and re-layouts  21.4 us (10%)
  other arithmetic  17.3 us (8%)
  Pallas kernels  4.72 us (2%)
    ppermute x18, waiting for transfers between devices, shifted(): lax.ppermute(array, axis, [(i, (i + by) % peers) for i in range(peers)])  44 us
    ppermute x15, waiting for transfers between devices, swapped(): return lax.ppermute(array, axis, [(i, i ^ bit) for i in range(peers)])  39.9 us
    ppermute x18, starting transfers between devices, shifted(): lax.ppermute(array, axis, [(i, (i + by) % peers) for i in range(peers)])  30.7 us
    dot_general x15, matrix products, dot(): lax.dot_general(left, right, (((left_dim,), (right_dim,)), ((), ())), pre...  24.4 us
    all_to_all x3, waiting for transfers between devices, exchanged(): return lax.all_to_all(array, axes, split_axis=0, concat_axis=0, tiled=True)  13.4 us
    unnamed x60, local copies, waits for them, and re-layouts  11.8 us
    all_to_all x3, starting transfers between devices, exchanged(): return lax.all_to_all(array, axes, split_axis=0, concat_axis=0, tiled=True)  11.7 us
    ppermute x15, starting transfers between devices, swapped(): return lax.ppermute(array, axis, [(i, i ^ bit) for i in range(peers)])  10.8 us
  transfers between devices with their start and end apart: 36, of which 13 were waited for; matrix products, arithmetic and copies ran while one was open for 26% of the time, Pallas kernels for 1%

profile of v5, /device:TPU:0, one launch (start us, length us, event | category | flops | bytes accessed | tf_op | source)
XLA Modules:
  0.0 219.9 jit_solution(2825856395906340331)
XLA Ops:
  0.6 3.1 %collective-permute-start.3 = (bf16[64,1024]{1,0:T(8,128)(2,1)}, bf16[64,1024]{1,0:T(8,128)(2,1)S(1)}, u32[]{:S(2)}, u32[]{:S(2)}) collective-permute-start(bf16[64,1024]{1,0:T(8,128)(2,1)} %bitcast.262), channel_id=1, source_target_pairs={{0,4},{4,8},{8,12},{12,0},{1,5},{5,9},{9,13},{13,1},{2,6},{6,10},{... | collective-permute-start | bytes 393224 | tf_op jit(solution)/shard_map/ppermute | solution.py:25
  3.7 2.6 %collective-permute-start.4 = (bf16[64,1024]{1,0:T(8,128)(2,1)}, bf16[64,1024]{1,0:T(8,128)(2,1)S(1)}, u32[]{:S(2)}, u32[]{:S(2)}) collective-permute-start(bf16[64,1024]{1,0:T(8,128)(2,1)} %bitcast.263), channel_id=1, source_target_pairs={{0,8},{4,12},{8,0},{12,4},{1,9},{5,13},{9,1},{13,5},{2,10},{6,14},... | collective-permute-start | bytes 393224 | tf_op jit(solution)/shard_map/ppermute | solution.py:25
  6.3 1.3 collective-permute-start.5
  7.7 1.2 copy-done.1
  9.6 1.5 collective-permute-start.1
  11.2 1.9 dynamic-slice_dynamic-update-slice_fusion
  13.8 1.6 shard_map.211
  17.2 3.7 %collective-permute-done.2 = bf16[64,1024]{1,0:T(8,128)(2,1)S(1)} collective-permute-done((bf16[64,1024]{1,0:T(8,128)(2,1)S(1)}, bf16[64,1024]{1,0:T(8,128)(2,1)S(1)}, u32[]{:S(2)}, u32[]{:S(2)}) %collective-permute-start.2) | collective-permute-done | bytes 131104 | tf_op jit(solution)/shard_map/ppermute | solution.py:20
  21.6 3.7 %all-to-all-start = ((bf16[8,128,1024]{2,1,0:T(8,128)(2,1)}), bf16[8,128,1024]{2,1,0:T(8,128)(2,1)S(1)}, u32[]{:S(2)}, u32[]{:S(2)}) async-start(bf16[8,128,1024]{2,1,0:T(8,128)(2,1)} %bitcast.9), calls=%async_computation | async-start | bytes 4194304 | tf_op jit(solution)/shard_map/all_to_all | solution.py:74
  27.7 3.2 %collective-permute-start.7 = (bf16[512,1024]{1,0:T(8,128)(2,1)}, bf16[512,1024]{1,0:T(8,128)(2,1)S(1)}, u32[]{:S(2)}, u32[]{:S(2)}) collective-permute-start(bf16[512,1024]{1,0:T(8,128)(2,1)} %get-tuple-element.24), channel_id=1, source_target_pairs={{0,12},{4,0},{8,4},{12,8},{1,13},{5,1},{9,5},{13,9},{2,14},{6,2},{... | collective-permute-start | bytes 3145736 | tf_op jit(solution)/shard_map/ppermute | solution.py:25
  32.8 1.8 collective-permute-start.8
  34.9 1.0 copy-done.13
  36.0 26.3 %collective-permute-done.8 = bf16[1,256,1024]{2,1,0:T(8,128)(2,1)} collective-permute-done((bf16[1,256,1024]{2,1,0:T(8,128)(2,1)}, bf16[1,256,1024]{2,1,0:T(8,128)(2,1)}, u32[]{:S(2)}, u32[]{:S(2)}) %collective-permute-start.8) | collective-permute-done | bytes 524320 | tf_op jit(solution)/shard_map/ppermute | solution.py:20
  62.3 13.1 %collective-permute-done.7 = bf16[512,1024]{1,0:T(8,128)(2,1)S(1)} collective-permute-done((bf16[512,1024]{1,0:T(8,128)(2,1)}, bf16[512,1024]{1,0:T(8,128)(2,1)S(1)}, u32[]{:S(2)}, u32[]{:S(2)}) %collective-permute-start.7) | collective-permute-done | bytes 1048608 | tf_op jit(solution)/shard_map/ppermute | solution.py:25
  75.5 2.1 collective-permute-start.22
  77.6 1.4 select_bitcast_fusion.7
  79.5 1.4 slice_dynamic-update-slice_fusion
  81.0 1.1 bitcast_dynamic-update-slice_fusion.2
  82.1 7.9 %collective-permute-done.22 = bf16[256,1024]{1,0:T(8,128)(2,1)S(1)} collective-permute-done((bf16[256,1024]{1,0:T(8,128)(2,1)S(1)}, bf16[256,1024]{1,0:T(8,128)(2,1)S(1)}, u32[]{:S(2)}, u32[]{:S(2)}) %collective-permute-start.22) | collective-permute-done | bytes 524320 | tf_op jit(solution)/shard_map/ppermute | solution.py:25
  90.1 11.5 %collective-permute-done.10 = bf16[256,1024]{1,0:T(8,128)(2,1)S(1)} collective-permute-done((bf16[256,1024]{1,0:T(8,128)(2,1)S(1)}, bf16[256,1024]{1,0:T(8,128)(2,1)S(1)}, u32[]{:S(2)}, u32[]{:S(2)}) %collective-permute-start.10) | collective-permute-done | bytes 524320 | tf_op jit(solution)/shard_map/ppermute | solution.py:25
  102.1 1.4 copy-done.2
  104.9 2.3 %collective-permute-start.14 = (bf16[80,128]{1,0:T(8,128)(2,1)S(1)}, bf16[80,128]{1,0:T(8,128)(2,1)S(1)}, u32[]{:S(2)}, u32[]{:S(2)}) collective-permute-start(bf16[80,128]{1,0:T(8,128)(2,1)S(1)} %pad_maximum_fusion.6), channel_id=1, source_target_pairs={{0,8},{4,12},{8,0},{12,4},{1,9},{5,13},{9,1},{13,5},{2,10},{6,14},... | collective-permute-start | bytes 61448 | tf_op jit(solution)/shard_map/ppermute | solution.py:25
  107.3 1.5 collective-permute-start.15
  108.7 1.5 collective-permute-start.19
  110.2 2.4 %fusion.36 = f32[1024,1024]{1,0:T(8,128)S(1)} fusion(bf16[1024,1024]{1,0:T(8,128)(2,1)S(1)} %constant_dynamic-update-slice_fusion.3, bf16[1024,1024]{1,0:T(8,128)(2,1)S(1)} %bitcast.225), kind=kOutput, calls=%fused_computation.162 | convolution fusion | flops 2147483648 | bytes 8388608 | tf_op jit(solution)/shard_map/dot_general | solution.py:82
  113.3 1.2 constant_dynamic-slice_fusion.2
  115.2 3.1 %collective-permute-start.28 = (bf16[1024,256]{1,0:T(8,128)(2,1)}, bf16[1024,256]{1,0:T(8,128)(2,1)}, u32[]{:S(2)}, u32[]{:S(2)}) collective-permute-start(bf16[1024,256]{1,0:T(8,128)(2,1)} %get-tuple-element.43), channel_id=1, source_target_pairs={{0,12},{4,0},{8,4},{12,8},{1,13},{5,1},{9,5},{13,9},{2,14},{6,2},{... | collective-permute-start | bytes 1572872 | tf_op jit(solution)/shard_map/ppermute | solution.py:25
  118.4 1.5 collective-permute-start.17
  119.9 2.4 %fusion.34 = f32[2,2,2,128,1024]{4,3,2,1,0:T(8,128)S(1)} fusion(bf16[2,2,2,128,1024]{4,3,2,1,0:T(8,128)(2,1)S(1)} %bitcast.227, bf16[1024,1024,1,1,1]{1,0,4,3,2:T(8,128)(2,1)S(1)} %bitcast.251), kind=kOutput, calls=%fused_computation.160 | convolution fusion | flops 2147483648 | bytes 8388608 | tf_op jit(solution)/shard_map/dot_general | solution.py:82
  122.5 1.2 collective-permute-done.17
  125.1 1.2 collective-permute-start.20
  127.9 1.6 collective-permute-start.23
  129.6 2.4 %fusion.35 = f32[1024,1024]{1,0:T(8,128)S(1)} fusion(bf16[1024,1024]{1,0:T(8,128)(2,1)S(1)} %bitcast.254, bf16[1024,1024]{1,0:T(8,128)(2,1)S(1)} %copy-done.23), kind=kOutput, calls=%fused_computation.161 | convolution fusion | flops 2147483648 | bytes 8388608 | tf_op jit(solution)/shard_map/dot_general | solution.py:82
  132.0 1.5 collective-permute-done.23
  134.2 6.0 %collective-permute-done.20 = bf16[2,128,1024]{2,1,0:T(8,128)(2,1)} collective-permute-done((bf16[2,128,1024]{2,1,0:T(8,128)(2,1)}, bf16[2,128,1024]{2,1,0:T(8,128)(2,1)}, u32[]{:S(2)}, u32[]{:S(2)}) %collective-permute-start.20) | collective-permute-done | bytes 524320 | tf_op jit(solution)/shard_map/ppermute | solution.py:20
  140.2 1.3 select_bitcast_fusion.5
  142.4 2.1 collective-permute-done.25
  144.9 1.7 bitcast_add_fusion
  146.7 1.2 collective-permute-start.12
  149.0 1.0 copy-done.6
  150.5 3.7 %add_convert_fusion = bf16[1024,1024]{1,0:T(8,128)(2,1)} fusion(f32[1024,1024]{1,0:T(8,128)S(1)} %fusion.35, bf16[1024,1024]{1,0:T(8,128)(2,1)S(1)} %bitcast.233, bf16[1024,1024]{1,0:T(8,128)(2,1)S(1)} %bitcast.252), kind=kOutput, calls=%fused_computation.1 | convolution fusion | flops 2149580800 | bytes 10485760 | tf_op jit(solution)/shard_map/dot_general | solution.py:82
  156.9 1.0 collective-permute-start.29
  157.9 3.8 %all-to-all-start.1 = ((bf16[8,128,1024]{2,1,0:T(8,128)(2,1)}), bf16[8,128,1024]{2,1,0:T(8,128)(2,1)S(1)}, u32[]{:S(2)}, u32[]{:S(2)}) async-start(bf16[8,128,1024]{2,1,0:T(8,128)(2,1)} %bitcast.253), calls=%async_computation.1 | async-start | bytes 4194304 | tf_op jit(solution)/shard_map/all_to_all | solution.py:74
  165.4 1.4 fusion.19
  167.1 1.4 fusion.13
  168.5 1.8 collective-permute-start.30
  170.3 1.4 fusion.15
  171.8 1.4 fusion.9
  173.2 2.9 %collective-permute-start.31 = (bf16[64,1024]{1,0:T(8,128)(2,1)S(1)}, bf16[64,1024]{1,0:T(8,128)(2,1)}, u32[]{:S(2)}, u32[]{:S(2)}) collective-permute-start(bf16[64,1024]{1,0:T(8,128)(2,1)S(1)} %copy-done.19), channel_id=1, source_target_pairs={{0,12},{4,0},{8,4},{12,8},{1,13},{5,1},{9,5},{13,9},{2,14},{6,2},{... | collective-permute-start | bytes 393224 | tf_op jit(solution)/shard_map/ppermute | solution.py:25
  176.1 1.4 convolution_add_fusion.3
  177.5 1.4 convolution_add_fusion.1
  178.9 1.4 fusion.2
  180.3 1.4 fusion.3
  181.7 1.0 pad_maximum_fusion.3
  182.8 4.3 %all-to-all-done.1 = bf16[8,128,1024]{2,1,0:T(8,128)(2,1)S(1)} async-done(((bf16[8,128,1024]{2,1,0:T(8,128)(2,1)}), bf16[8,128,1024]{2,1,0:T(8,128)(2,1)S(1)}, u32[]{:S(2)}, u32[]{:S(2)}) %all-to-all-start.1) | async-done | bytes 2097184 | tf_op jit(solution)/shard_map/all_to_all | solution.py:74
  187.1 4.1 %all-to-all-start.2 = ((bf16[32,64,256]{2,1,0:T(8,128)(2,1)}), bf16[32,64,256]{2,1,0:T(8,128)(2,1)S(1)}, u32[]{:S(2)}, u32[]{:S(2)}) async-start(bf16[32,64,256]{2,1,0:T(8,128)(2,1)} %bitcast.237), calls=%async_computation.2 | async-start | bytes 2097152 | tf_op jit(solution)/shard_map/all_to_all | solution.py:74
  191.2 1.6 convert_add_fusion
  192.9 1.8 collective-permute-start.32
  194.7 1.9 fusion.23
  196.6 1.6 shard_map.212
  198.2 9.9 %collective-permute-done.32 = bf16[128,1024]{1,0:T(8,128)(2,1)S(1)} collective-permute-done((bf16[128,1024]{1,0:T(8,128)(2,1)S(1)}, bf16[128,1024]{1,0:T(8,128)(2,1)S(1)}, u32[]{:S(2)}, u32[]{:S(2)}) %collective-permute-start.32) | collective-permute-done | bytes 262176 | tf_op jit(solution)/shard_map/ppermute | solution.py:25
  208.1 1.2 fusion.7
  209.3 9.1 %all-to-all-done.2 = bf16[32,64,256]{2,1,0:T(8,128)(2,1)S(1)} async-done(((bf16[32,64,256]{2,1,0:T(8,128)(2,1)}), bf16[32,64,256]{2,1,0:T(8,128)(2,1)S(1)}, u32[]{:S(2)}, u32[]{:S(2)}) %all-to-all-start.2) | async-done | bytes 1048608 | tf_op jit(solution)/shard_map/all_to_all | solution.py:74
  218.4 1.5 shard_map.213
  (174 shorter events, 26.0 us)
Async XLA Ops:
  0.6 13.1 %copy-start = (bf16[128,8192]{1,0:T(8,128)(2,1)S(1)}, bf16[128,8192]{1,0:T(8,128)(2,1)}, u32[]{:S(2)}) copy-start(bf16[128,8192]{1,0:T(8,128)(2,1)} %source.1) | copy-start | bytes 6291460
  0.6 20.9 %collective-permute-start.3 = (bf16[64,1024]{1,0:T(8,128)(2,1)}, bf16[64,1024]{1,0:T(8,128)(2,1)S(1)}, u32[]{:S(2)}, u32[]{:S(2)}) collective-permute-start(bf16[64,1024]{1,0:T(8,128)(2,1)} %bitcast.262), channel_id=1, source_target_pairs={{0,4},{4,8},{8,12},{12,0},{1,5},{5,9},{9,13},{13,1},{2,6},{6,10},{... | collective-permute-start | bytes 393224 | tf_op jit(solution)/shard_map/ppermute | solution.py:25
  3.7 17.9 %collective-permute-start.4 = (bf16[64,1024]{1,0:T(8,128)(2,1)}, bf16[64,1024]{1,0:T(8,128)(2,1)S(1)}, u32[]{:S(2)}, u32[]{:S(2)}) collective-permute-start(bf16[64,1024]{1,0:T(8,128)(2,1)} %bitcast.263), channel_id=1, source_target_pairs={{0,8},{4,12},{8,0},{12,4},{1,9},{5,13},{9,1},{13,5},{2,10},{6,14},... | collective-permute-start | bytes 393224 | tf_op jit(solution)/shard_map/ppermute | solution.py:25
  6.3 15.3 %collective-permute-start.5 = (bf16[64,1024]{1,0:T(8,128)(2,1)}, bf16[64,1024]{1,0:T(8,128)(2,1)S(1)}, u32[]{:S(2)}, u32[]{:S(2)}) collective-permute-start(bf16[64,1024]{1,0:T(8,128)(2,1)} %bitcast.264), channel_id=1, source_target_pairs={{0,12},{4,0},{8,4},{12,8},{1,13},{5,1},{9,5},{13,9},{2,14},{6,2},{... | collective-permute-start | bytes 393224 | tf_op jit(solution)/shard_map/ppermute | solution.py:25
  7.7 1.2 copy-start.1
  9.6 5.7 %collective-permute-start = (bf16[64,1024]{1,0:T(8,128)(2,1)}, bf16[64,1024]{1,0:T(8,128)(2,1)S(1)}, u32[]{:S(2)}, u32[]{:S(2)}) collective-permute-start(bf16[64,1024]{1,0:T(8,128)(2,1)} %get-tuple-element.70), channel_id=1, source_target_pairs={{0,1},{1,0},{2,3},{3,2},{4,5},{5,4},{6,7},{7,6},{8,9},{9,8},{10,11... | collective-permute-start | bytes 393224 | tf_op jit(solution)/shard_map/ppermute | solution.py:20
  9.6 6.8 %collective-permute-start.1 = (bf16[64,1024]{1,0:T(8,128)(2,1)S(1)}, bf16[64,1024]{1,0:T(8,128)(2,1)S(1)}, u32[]{:S(2)}, u32[]{:S(2)}) collective-permute-start(bf16[64,1024]{1,0:T(8,128)(2,1)S(1)} %get-tuple-element.69), channel_id=1, source_target_pairs={{0,2},{1,3},{2,0},{3,1},{4,6},{5,7},{6,4},{7,5},{8,10},{9,11},{10,... | collective-permute-start | bytes 393224 | tf_op jit(solution)/shard_map/ppermute | solution.py:20
  15.4 5.5 %collective-permute-start.2 = (bf16[64,1024]{1,0:T(8,128)(2,1)S(1)}, bf16[64,1024]{1,0:T(8,128)(2,1)S(1)}, u32[]{:S(2)}, u32[]{:S(2)}) collective-permute-start(bf16[64,1024]{1,0:T(8,128)(2,1)S(1)} %get-tuple-element.68), channel_id=1, source_target_pairs={{0,3},{1,2},{2,1},{3,0},{4,7},{5,6},{6,5},{7,4},{8,11},{9,10},{10,... | collective-permute-start | bytes 393224 | tf_op jit(solution)/shard_map/ppermute | solution.py:20
  21.6 4.7 %copy-start.18 = (bf16[1,64,1024]{2,1,0:T(8,128)(2,1)S(1)}, bf16[1,64,1024]{2,1,0:T(8,128)(2,1)}, u32[]{:S(2)}) copy-start(bf16[1,64,1024]{2,1,0:T(8,128)(2,1)} %param.24) | copy-start | bytes 393220
  21.6 13.0 %copy-start.24 = (s32[128]{0:T(128)S(1)}, s32[128]{0:T(128)}, u32[]{:S(2)}) copy-start(s32[128]{0:T(128)} %param.21) | copy-start | bytes 1540
  21.6 53.8 %all-to-all-start = ((bf16[8,128,1024]{2,1,0:T(8,128)(2,1)}), bf16[8,128,1024]{2,1,0:T(8,128)(2,1)S(1)}, u32[]{:S(2)}, u32[]{:S(2)}) async-start(bf16[8,128,1024]{2,1,0:T(8,128)(2,1)} %bitcast.9), calls=%async_computation | async-start | bytes 4194304 | tf_op jit(solution)/shard_map/all_to_all | solution.py:74
  27.0 8.9 %copy-start.25 = (s32[16]{0:T(128)S(1)}, s32[16]{0:T(128)}, u32[]{:S(2)}) copy-start(s32[16]{0:T(128)} %constant.229) | copy-start | bytes 196
  27.0 35.3 %collective-permute-start.6 = (bf16[512,1024]{1,0:T(8,128)(2,1)}, bf16[512,1024]{1,0:T(8,128)(2,1)}, u32[]{:S(2)}, u32[]{:S(2)}) collective-permute-start(bf16[512,1024]{1,0:T(8,128)(2,1)} %get-tuple-element.24), channel_id=1, source_target_pairs={{0,4},{4,8},{8,12},{12,0},{1,5},{5,9},{9,13},{13,1},{2,6},{6,10},{... | collective-permute-start | bytes 3145736 | tf_op jit(solution)/shard_map/ppermute | solution.py:25
  27.7 47.8 %collective-permute-start.7 = (bf16[512,1024]{1,0:T(8,128)(2,1)}, bf16[512,1024]{1,0:T(8,128)(2,1)S(1)}, u32[]{:S(2)}, u32[]{:S(2)}) collective-permute-start(bf16[512,1024]{1,0:T(8,128)(2,1)} %get-tuple-element.24), channel_id=1, source_target_pairs={{0,12},{4,0},{8,4},{12,8},{1,13},{5,1},{9,5},{13,9},{2,14},{6,2},{... | collective-permute-start | bytes 3145736 | tf_op jit(solution)/shard_map/ppermute | solution.py:25
  32.8 29.5 %collective-permute-start.8 = (bf16[1,256,1024]{2,1,0:T(8,128)(2,1)}, bf16[1,256,1024]{2,1,0:T(8,128)(2,1)}, u32[]{:S(2)}, u32[]{:S(2)}) collective-permute-start(bf16[1,256,1024]{2,1,0:T(8,128)(2,1)} %bitcast.14), channel_id=1, source_target_pairs={{0,2},{1,3},{2,0},{3,1},{4,6},{5,7},{6,4},{7,5},{8,10},{9,11},{10,... | collective-permute-start | bytes 1572872 | tf_op jit(solution)/shard_map/ppermute | solution.py:20
  34.7 1.2 copy-start.13
  35.9 26.4 %copy-start.9 = (bf16[4,256,1024]{2,1,0:T(8,128)(2,1)}, bf16[4,256,1024]{2,1,0:T(8,128)(2,1)S(1)}, u32[]{:S(2)}) copy-start(bf16[4,256,1024]{2,1,0:T(8,128)(2,1)S(1)} %bitcast_dynamic-update-slice_fusion.3) | copy-start | bytes 6291460
  75.4 44.5 %copy-start.4 = (bf16[8,128,1024]{2,1,0:T(8,128)(2,1)}, bf16[8,128,1024]{2,1,0:T(8,128)(2,1)S(1)}, u32[]{:S(2)}) copy-start(bf16[8,128,1024]{2,1,0:T(8,128)(2,1)S(1)} %all-to-all-done) | copy-start | bytes 6291460
  75.5 14.5 %collective-permute-start.22 = (bf16[256,1024]{1,0:T(8,128)(2,1)S(1)}, bf16[256,1024]{1,0:T(8,128)(2,1)S(1)}, u32[]{:S(2)}, u32[]{:S(2)}) collective-permute-start(bf16[256,1024]{1,0:T(8,128)(2,1)S(1)} %slice.121), channel_id=1, source_target_pairs={{0,12},{4,0},{8,4},{12,8},{1,13},{5,1},{9,5},{13,9},{2,14},{6,2},{... | collective-permute-start | bytes 1572872 | tf_op jit(solution)/shard_map/ppermute | solution.py:25
  77.6 1.9 copy-start.21
  79.0 2.0 copy-start.10
  79.2 22.5 %collective-permute-start.9 = (bf16[2,256,1024]{2,1,0:T(8,128)(2,1)S(1)}, bf16[2,256,1024]{2,1,0:T(8,128)(2,1)S(1)}, u32[]{:S(2)}, u32[]{:S(2)}) collective-permute-start(bf16[2,256,1024]{2,1,0:T(8,128)(2,1)S(1)} %maximum_bitcast_fusion), channel_id=1, source_target_pairs={{0,1},{1,0},{2,3},{3,2},{4,5},{5,4},{6,7},{7,6},{8,9},{9,8},{10,11... | collective-permute-start | bytes 3145736 | tf_op jit(solution)/shard_map/ppermute | solution.py:20
  81.0 20.6 %collective-permute-start.10 = (bf16[256,1024]{1,0:T(8,128)(2,1)S(1)}, bf16[256,1024]{1,0:T(8,128)(2,1)S(1)}, u32[]{:S(2)}, u32[]{:S(2)}) collective-permute-start(bf16[256,1024]{1,0:T(8,128)(2,1)S(1)} %get-tuple-element.52), channel_id=1, source_target_pairs={{0,4},{4,8},{8,12},{12,0},{1,5},{5,9},{9,13},{13,1},{2,6},{6,10},{... | collective-permute-start | bytes 1572872 | tf_op jit(solution)/shard_map/ppermute | solution.py:25
  90.1 20.1 %copy-start.22 = (bf16[1024,1024]{1,0:T(8,128)(2,1)}, bf16[1024,1024]{1,0:T(8,128)(2,1)S(1)}, u32[]{:S(2)}) copy-start(bf16[1024,1024]{1,0:T(8,128)(2,1)S(1)} %constant_dynamic-update-slice_fusion.3) | copy-start | bytes 6291460
  101.7 18.2 %copy-start.11 = (bf16[4,256,1024]{2,1,0:T(8,128)(2,1)}, bf16[4,256,1024]{2,1,0:T(8,128)(2,1)S(1)}, u32[]{:S(2)}) copy-start(bf16[4,256,1024]{2,1,0:T(8,128)(2,1)S(1)} %bitcast_dynamic-update-slice_fusion) | copy-start | bytes 6291460
  101.9 1.6 copy-start.14
  102.1 1.4 copy-start.2
  104.2 8.4 %collective-permute-start.13 = (bf16[80,128]{1,0:T(8,128)(2,1)S(1)}, bf16[80,128]{1,0:T(8,128)(2,1)S(1)}, u32[]{:S(2)}, u32[]{:S(2)}) collective-permute-start(bf16[80,128]{1,0:T(8,128)(2,1)S(1)} %pad_maximum_fusion.6), channel_id=1, source_target_pairs={{0,4},{4,8},{8,12},{12,0},{1,5},{5,9},{9,13},{13,1},{2,6},{6,10},{... | collective-permute-start | bytes 61448 | tf_op jit(solution)/shard_map/ppermute | solution.py:25
  104.9 7.7 %collective-permute-start.14 = (bf16[80,128]{1,0:T(8,128)(2,1)S(1)}, bf16[80,128]{1,0:T(8,128)(2,1)S(1)}, u32[]{:S(2)}, u32[]{:S(2)}) collective-permute-start(bf16[80,128]{1,0:T(8,128)(2,1)S(1)} %pad_maximum_fusion.6), channel_id=1, source_target_pairs={{0,8},{4,12},{8,0},{12,4},{1,9},{5,13},{9,1},{13,5},{2,10},{6,14},... | collective-permute-start | bytes 61448 | tf_op jit(solution)/shard_map/ppermute | solution.py:25
  107.3 5.4 %collective-permute-start.15 = (bf16[80,128]{1,0:T(8,128)(2,1)S(1)}, bf16[80,128]{1,0:T(8,128)(2,1)S(1)}, u32[]{:S(2)}, u32[]{:S(2)}) collective-permute-start(bf16[80,128]{1,0:T(8,128)(2,1)S(1)} %pad_maximum_fusion.6), channel_id=1, source_target_pairs={{0,12},{4,0},{8,4},{12,8},{1,13},{5,1},{9,5},{13,9},{2,14},{6,2},{... | collective-permute-start | bytes 61448 | tf_op jit(solution)/shard_map/ppermute | solution.py:25
  108.7 15.2 %collective-permute-start.19 = (bf16[1,128,1024]{2,1,0:T(8,128)(2,1)S(1)}, bf16[1,128,1024]{2,1,0:T(8,128)(2,1)S(1)}, u32[]{:S(2)}, u32[]{:S(2)}) collective-permute-start(bf16[1,128,1024]{2,1,0:T(8,128)(2,1)S(1)} %bitcast.259), channel_id=1, source_target_pairs={{0,16},{16,0},{1,17},{17,1},{2,18},{18,2},{3,19},{19,3},{4,20},{20... | collective-permute-start | bytes 786440 | tf_op jit(solution)/shard_map/ppermute | solution.py:20
  112.7 5.6 %collective-permute-start.16 = (bf16[1,4,80,128]{3,2,1,0:T(8,128)(2,1)S(1)}, bf16[1,4,80,128]{3,2,1,0:T(8,128)(2,1)S(1)}, u32[]{:S(2)}, u32[]{:S(2)}) collective-permute-start(bf16[1,4,80,128]{3,2,1,0:T(8,128)(2,1)S(1)} %maximum_bitcast_fusion.3), channel_id=1, source_target_pairs={{0,16},{16,0},{1,17},{17,1},{2,18},{18,2},{3,19},{19,3},{4,20},{20... | collective-permute-start | bytes 245768 | tf_op jit(solution)/shard_map/ppermute | solution.py:20
  114.5 58.7 %collective-permute-start.26 = (bf16[1024,256]{1,0:T(8,128)(2,1)}, bf16[1024,256]{1,0:T(8,128)(2,1)}, u32[]{:S(2)}, u32[]{:S(2)}) collective-permute-start(bf16[1024,256]{1,0:T(8,128)(2,1)} %get-tuple-element.44), channel_id=1, source_target_pairs={{0,4},{4,8},{8,12},{12,0},{1,5},{5,9},{9,13},{13,1},{2,6},{6,10},{... | collective-permute-start | bytes 1572872 | tf_op jit(solution)/shard_map/ppermute | solution.py:25
  115.2 53.3 %collective-permute-start.28 = (bf16[1024,256]{1,0:T(8,128)(2,1)}, bf16[1024,256]{1,0:T(8,128)(2,1)}, u32[]{:S(2)}, u32[]{:S(2)}) collective-permute-start(bf16[1024,256]{1,0:T(8,128)(2,1)} %get-tuple-element.43), channel_id=1, source_target_pairs={{0,12},{4,0},{8,4},{12,8},{1,13},{5,1},{9,5},{13,9},{2,14},{6,2},{... | collective-permute-start | bytes 1572872 | tf_op jit(solution)/shard_map/ppermute | solution.py:25
  118.4 5.4 %collective-permute-start.17 = (bf16[2,4,80,128]{3,2,1,0:T(8,128)(2,1)S(1)}, bf16[2,4,80,128]{3,2,1,0:T(8,128)(2,1)S(1)}, u32[]{:S(2)}, u32[]{:S(2)}) collective-permute-start(bf16[2,4,80,128]{3,2,1,0:T(8,128)(2,1)S(1)} %maximum_bitcast_fusion.2), channel_id=1, source_target_pairs={{0,2},{1,3},{2,0},{3,1},{4,6},{5,7},{6,4},{7,5},{8,10},{9,11},{10,... | collective-permute-start | bytes 491528 | tf_op jit(solution)/shard_map/ppermute | solution.py:20
  122.3 2.0 copy-start.7
  122.4 22.4 %collective-permute-start.11 = (bf16[2,2,128,1024]{3,2,1,0:T(8,128)(2,1)S(1)}, bf16[2,2,128,1024]{3,2,1,0:T(8,128)(2,1)}, u32[]{:S(2)}, u32[]{:S(2)}) collective-permute-start(bf16[2,2,128,1024]{3,2,1,0:T(8,128)(2,1)S(1)} %fusion.4), channel_id=1, source_target_pairs={{0,1},{1,0},{2,3},{3,2},{4,5},{5,4},{6,7},{7,6},{8,9},{9,8},{10,11... | collective-permute-start | bytes 3145736 | tf_op jit(solution)/shard_map/ppermute | solution.py:20
  123.9 2.5 %collective-permute-start.18 = (bf16[4,4,80,128]{3,2,1,0:T(8,128)(2,1)S(1)}, bf16[4,4,80,128]{3,2,1,0:T(8,128)(2,1)S(1)}, u32[]{:S(2)}, u32[]{:S(2)}) collective-permute-start(bf16[4,4,80,128]{3,2,1,0:T(8,128)(2,1)S(1)} %bitcast.256), channel_id=1, source_target_pairs={{0,1},{1,0},{2,3},{3,2},{4,5},{5,4},{6,7},{7,6},{8,9},{9,8},{10,11... | collective-permute-start | bytes 983048 | tf_op jit(solution)/shard_map/ppermute | solution.py:20
  125.1 15.1 %collective-permute-start.20 = (bf16[2,128,1024]{2,1,0:T(8,128)(2,1)}, bf16[2,128,1024]{2,1,0:T(8,128)(2,1)}, u32[]{:S(2)}, u32[]{:S(2)}) collective-permute-start(bf16[2,128,1024]{2,1,0:T(8,128)(2,1)} %maximum_bitcast_fusion.1), channel_id=1, source_target_pairs={{0,2},{1,3},{2,0},{3,1},{4,6},{5,7},{6,4},{7,5},{8,10},{9,11},{10,... | collective-permute-start | bytes 1572872 | tf_op jit(solution)/shard_map/ppermute | solution.py:20
  127.6 2.0 copy-start.23
  127.9 5.7 %collective-permute-start.23 = (f32[64,512]{1,0:T(8,128)S(1)}, f32[64,512]{1,0:T(8,128)S(1)}, u32[]{:S(2)}, u32[]{:S(2)}) collective-permute-start(f32[64,512]{1,0:T(8,128)S(1)} %bitcast.265), channel_id=1, source_target_pairs={{0,16},{16,0},{1,17},{17,1},{2,18},{18,2},{3,19},{19,3},{4,20},{20... | collective-permute-start | bytes 393224 | tf_op jit(solution)/shard_map/ppermute | solution.py:25
  133.6 8.7 %collective-permute-start.24 = (f32[64,512]{1,0:T(8,128)S(1)}, f32[64,512]{1,0:T(8,128)S(1)}, u32[]{:S(2)}, u32[]{:S(2)}) collective-permute-start(f32[64,512]{1,0:T(8,128)S(1)} %bitcast_add_fusion.3), channel_id=1, source_target_pairs={{0,2},{1,3},{2,0},{3,1},{4,6},{5,7},{6,4},{7,5},{8,10},{9,11},{10,... | collective-permute-start | bytes 393224 | tf_op jit(solution)/shard_map/ppermute | solution.py:20
  140.2 4.7 %copy-start.8 = (f32[2,2,2,128,1024]{4,3,2,1,0:T(8,128)S(1)}, f32[2,2,2,128,1024]{4,3,2,1,0:T(8,128)}, u32[]{:S(2)}) copy-start(f32[2,2,2,128,1024]{4,3,2,1,0:T(8,128)} %copy-done.7) | copy-start | bytes 12582916
  141.6 6.3 %collective-permute-start.21 = (bf16[4,128,1024]{2,1,0:T(8,128)(2,1)S(1)}, bf16[4,128,1024]{2,1,0:T(8,128)(2,1)S(1)}, u32[]{:S(2)}, u32[]{:S(2)}) collective-permute-start(bf16[4,128,1024]{2,1,0:T(8,128)(2,1)S(1)} %bitcast.234), channel_id=1, source_target_pairs={{0,1},{1,0},{2,3},{3,2},{4,5},{5,4},{6,7},{7,6},{8,9},{9,8},{10,11... | collective-permute-start | bytes 3145736 | tf_op jit(solution)/shard_map/ppermute | solution.py:20
  142.2 2.3 %collective-permute-start.25 = (f32[64,512]{1,0:T(8,128)S(1)}, f32[64,512]{1,0:T(8,128)S(1)}, u32[]{:S(2)}, u32[]{:S(2)}) collective-permute-start(f32[64,512]{1,0:T(8,128)S(1)} %add.252), channel_id=1, source_target_pairs={{0,1},{1,0},{2,3},{3,2},{4,5},{5,4},{6,7},{7,6},{8,9},{9,8},{10,11... | collective-permute-start | bytes 393224 | tf_op jit(solution)/shard_map/ppermute | solution.py:20
  144.5 34.4 %collective-permute-start.27 = (bf16[1024,256]{1,0:T(8,128)(2,1)S(1)}, bf16[1024,256]{1,0:T(8,128)(2,1)}, u32[]{:S(2)}, u32[]{:S(2)}) collective-permute-start(bf16[1024,256]{1,0:T(8,128)(2,1)S(1)} %get-tuple-element.42), channel_id=1, source_target_pairs={{0,8},{4,12},{8,0},{12,4},{1,9},{5,13},{9,1},{13,5},{2,10},{6,14},... | collective-permute-start | bytes 1572872 | tf_op jit(solution)/shard_map/ppermute | solution.py:25
  146.6 1.6 copy-start.5
  146.7 40.4 %collective-permute-start.12 = (bf16[2,1,128,1024]{3,2,1,0:T(8,128)(2,1)S(1)}, bf16[2,1,128,1024]{3,2,1,0:T(8,128)(2,1)}, u32[]{:S(2)}, u32[]{:S(2)}) collective-permute-start(bf16[2,1,128,1024]{3,2,1,0:T(8,128)(2,1)S(1)} %dynamic-slice_convert_fusion.1), channel_id=1, source_target_pairs={{0,2},{1,3},{2,0},{3,1},{4,6},{5,7},{6,4},{7,5},{8,10},{9,11},{10,... | collective-permute-start | bytes 1572872 | tf_op jit(solution)/shard_map/ppermute | solution.py:20
  148.5 1.9 copy-start.12
  149.0 1.0 copy-start.6
  156.9 25.9 %collective-permute-start.29 = (bf16[64,1024]{1,0:T(8,128)(2,1)}, bf16[64,1024]{1,0:T(8,128)(2,1)}, u32[]{:S(2)}, u32[]{:S(2)}) collective-permute-start(bf16[64,1024]{1,0:T(8,128)(2,1)} %get-tuple-element.63), channel_id=1, source_target_pairs={{0,4},{4,8},{8,12},{12,0},{1,5},{5,9},{9,13},{13,1},{2,6},{6,10},{... | collective-permute-start | bytes 393224 | tf_op jit(solution)/shard_map/ppermute | solution.py:25
  157.9 29.2 %all-to-all-start.1 = ((bf16[8,128,1024]{2,1,0:T(8,128)(2,1)}), bf16[8,128,1024]{2,1,0:T(8,128)(2,1)S(1)}, u32[]{:S(2)}, u32[]{:S(2)}) async-start(bf16[8,128,1024]{2,1,0:T(8,128)(2,1)} %bitcast.253), calls=%async_computation.1 | async-start | bytes 4194304 | tf_op jit(solution)/shard_map/all_to_all | solution.py:74
  161.7 3.6 %copy-start.17 = (bf16[64,512]{1,0:T(8,128)(2,1)S(1)}, bf16[64,512]{1,0:T(8,128)(2,1)}, u32[]{:S(2)}) copy-start(bf16[64,512]{1,0:T(8,128)(2,1)} %get-tuple-element.83) | copy-start | bytes 196612
  165.2 1.6 copy-start.16
  165.4 1.6 copy-start.15
  166.9 1.6 copy-start.20
  168.5 14.2 %collective-permute-start.30 = (bf16[64,1024]{1,0:T(8,128)(2,1)S(1)}, bf16[64,1024]{1,0:T(8,128)(2,1)S(1)}, u32[]{:S(2)}, u32[]{:S(2)}) collective-permute-start(bf16[64,1024]{1,0:T(8,128)(2,1)S(1)} %copy-done.20), channel_id=1, source_target_pairs={{0,8},{4,12},{8,0},{12,4},{1,9},{5,13},{9,1},{13,5},{2,10},{6,14},... | collective-permute-start | bytes 393224 | tf_op jit(solution)/shard_map/ppermute | solution.py:25
  171.7 1.5 copy-start.19
  173.2 9.5 %collective-permute-start.31 = (bf16[64,1024]{1,0:T(8,128)(2,1)S(1)}, bf16[64,1024]{1,0:T(8,128)(2,1)}, u32[]{:S(2)}, u32[]{:S(2)}) collective-permute-start(bf16[64,1024]{1,0:T(8,128)(2,1)S(1)} %copy-done.19), channel_id=1, source_target_pairs={{0,12},{4,0},{8,4},{12,8},{1,13},{5,1},{9,5},{13,9},{2,14},{6,2},{... | collective-permute-start | bytes 393224 | tf_op jit(solution)/shard_map/ppermute | solution.py:25
  187.1 31.3 %all-to-all-start.2 = ((bf16[32,64,256]{2,1,0:T(8,128)(2,1)}), bf16[32,64,256]{2,1,0:T(8,128)(2,1)S(1)}, u32[]{:S(2)}, u32[]{:S(2)}) async-start(bf16[32,64,256]{2,1,0:T(8,128)(2,1)} %bitcast.237), calls=%async_computation.2 | async-start | bytes 2097152 | tf_op jit(solution)/shard_map/all_to_all | solution.py:74
  192.9 15.3 %collective-permute-start.32 = (bf16[128,1024]{1,0:T(8,128)(2,1)S(1)}, bf16[128,1024]{1,0:T(8,128)(2,1)S(1)}, u32[]{:S(2)}, u32[]{:S(2)}) collective-permute-start(bf16[128,1024]{1,0:T(8,128)(2,1)S(1)} %fusion.8), channel_id=1, source_target_pairs={{0,16},{16,0},{1,17},{17,1},{2,18},{18,2},{3,19},{19,3},{4,20},{20... | collective-permute-start | bytes 786440 | tf_op jit(solution)/shard_map/ppermute | solution.py:25
  196.6 11.5 %copy-start.3 = (bf16[2,2,256,1024]{3,2,1,0:T(8,128)(2,1)S(1)}, bf16[2,2,256,1024]{3,2,1,0:T(8,128)(2,1)}, u32[]{:S(2)}) copy-start(bf16[2,2,256,1024]{3,2,1,0:T(8,128)(2,1)} %copy-done.2) | copy-start | bytes 6291460
